TPU v7x, 128 devices: a whole 4x4x4 slice. The times are simulated.
128 devices in a mesh: pool: 2 (over core), grp: 16 (over z, x), tp: 4 (over y).
Axes of the slice: x: 4, y: 4, z: 4, core: 2. Of those that a mesh axis runs over, the one named last changes fastest.
Arguments:
- queries: bfloat16 [1024, 6144], P(('pool', 'grp'), 'tp'), may hold values from -20 to 20
- key_cache: bfloat16 [1024, 128, 1024], P(('pool', 'grp'), None, 'tp'), may hold values from -20 to 20
- value_cache: bfloat16 [1024, 128, 1024], P(('pool', 'grp'), None, 'tp'), may hold values from -6 to 6
- key_new: bfloat16 [1024, 1024], P(('pool', 'grp'), 'tp'), may hold values from -6 to 6
- value_new: bfloat16 [1024, 1024], P(('pool', 'grp'), 'tp'), may hold values from -6 to 6
- lengths: int32 [1024], P(('pool', 'grp')), may hold values from 2 to 128
- residual: bfloat16 [1024, 6144], P(('pool', 'grp'), 'tp'), may hold values from -6 to 6
- norm_gain: bfloat16 [6144], P('tp'), may hold values from 0.099609375 to 1.8984375
- w_router: bfloat16 [6144, 8], P('tp'), may hold values from -0.078125 to 0.078125
- expert_ids: int32 [1024, 2], P(('pool', 'grp')), may hold values from 0 to 7, all different within a row; in each aligned block of 32 rows (0 to 31, 32 to 63, ...) at most 16 rows name the same one
- w_gate: bfloat16 [6144, 65536], P(None, ('pool', 'grp', 'tp')), may hold values from -0.078125 to 0.078125
- w_up: bfloat16 [6144, 65536], P(None, ('pool', 'grp', 'tp')), may hold values from -0.078125 to 0.078125
- w_down: bfloat16 [65536, 6144], P(('pool', 'grp', 'tp')), may hold values from -0.0625 to 0.0625
Outputs:
- layer_out: bfloat16 [1024, 6144], P(('pool', 'grp'), 'tp')
Inputs may be any that keep to these rules, and one draw needn't show every extreme that they name: `expert_ids`: each row names 2 different experts. In each aligned block of 32 rows (the rows of one device) no expert is named by more than 16 rows.
All inputs are finite; a program needn't handle non-finite values.
Results may differ from a plain program's by a relative error of at most 0.0065.
Values may be sent and summed in bfloat16 or wider, within the bound.
No kernel may reach another device: no remote copies, remote signals or barrier semaphores. Data moves between devices by JAX's collectives and lax.ppermute only.
A program may use at most 128 MiB of HBM per device.

v0:
```python
import jax
import jax.numpy as jnp
from jax import lax
from jax.sharding import PartitionSpec as P

HD = 128
TOP = 2
CAP = 16


def attend(queries, key_cache, value_cache, key_new, value_new, lengths):
    rows = queries.shape[0]
    heads_kv = key_new.shape[1] // HD
    repeat = queries.shape[1] // HD // heads_kv
    length = key_cache.shape[1]
    scale = 1.0 / HD**0.5
    qhead = queries.reshape(rows, heads_kv, repeat, HD)
    kcache = key_cache.reshape(rows, length, heads_kv, HD)
    vcache = value_cache.reshape(rows, length, heads_kv, HD)
    knew = key_new.reshape(rows, heads_kv, HD)
    vnew = value_new.reshape(rows, heads_kv, 1, HD).astype(jnp.float32)
    scores = (
        jnp.einsum("rgho,rcgo->rghc", qhead, kcache, preferred_element_type=jnp.float32) * scale
    )
    own = jnp.einsum("rgho,rgo->rgh", qhead, knew, preferred_element_type=jnp.float32) * scale
    valid = jnp.arange(length, dtype=jnp.int32)[None, :] < lengths[:, None]
    scores = jnp.where(valid[:, None, None, :], scores, -1e30)
    top = jnp.maximum(jnp.max(scores, -1), own)
    probs = jnp.exp(scores - top[..., None])
    pown = jnp.exp(own - top)
    total = jnp.sum(probs, -1) + pown
    weights = (probs / total[..., None]).astype(jnp.bfloat16)
    wown = (pown / total).astype(jnp.bfloat16).astype(jnp.float32)
    result = (
        jnp.einsum("rghc,rcgo->rgho", weights, vcache, preferred_element_type=jnp.float32)
        + wown[..., None] * vnew
    )
    return result.reshape(rows, repeat * heads_kv * HD)


def shards(
    queries,
    key_cache,
    value_cache,
    key_new,
    value_new,
    lengths,
    residual,
    norm_gain,
    w_router,
    expert_ids,
    w_gate,
    w_up,
    w_down,
):
    attn = attend(queries, key_cache, value_cache, key_new, value_new, lengths)
    hidden_state = (residual.astype(jnp.float32) + attn).astype(jnp.bfloat16)
    rows = hidden_state.shape[0]
    experts = w_router.shape[1]
    peers = lax.axis_size("pool") * lax.axis_size("grp")
    span = peers // experts
    assigned = rows * TOP
    flat_ids = expert_ids.reshape(-1)
    expert_hot = (flat_ids[:, None] == jnp.arange(experts, dtype=jnp.int32)[None, :]).astype(
        jnp.int32
    )
    earlier = jnp.cumsum(expert_hot, 0) - expert_hot
    slot = jnp.sum(earlier * expert_hot, 1)
    position = flat_ids * CAP + slot
    owner = jnp.arange(assigned, dtype=jnp.int32) // TOP
    place = jnp.arange(experts * CAP, dtype=jnp.int32)[:, None] == position[None, :]
    token_hot = owner[:, None] == jnp.arange(rows, dtype=jnp.int32)[None, :]
    dispatch = jnp.dot(
        place.astype(jnp.bfloat16),
        token_hot.astype(jnp.bfloat16),
        preferred_element_type=jnp.float32,
    ).astype(jnp.bfloat16)
    whole, gain_all, router_all = (
        lax.all_gather(hidden_state, "tp", axis=1, tiled=True),
        lax.all_gather(norm_gain, "tp", axis=0, tiled=True),
        lax.all_gather(w_router, "tp", axis=0, tiled=True),
    )
    hfloat = whole.astype(jnp.float32)
    meansq = jnp.mean(hfloat * hfloat, -1, keepdims=True)
    normed = (hfloat * lax.rsqrt(meansq + 1e-05) * gain_all.astype(jnp.float32)).astype(
        jnp.bfloat16
    )
    logits = jnp.dot(normed, router_all, preferred_element_type=jnp.float32)
    bucket = jnp.dot(dispatch, normed, preferred_element_type=jnp.float32).astype(jnp.bfloat16)
    outgoing = jnp.repeat(bucket.reshape(experts, CAP, -1), span, axis=0)
    incoming = lax.all_to_all(outgoing, ("pool", "grp"), split_axis=0, concat_axis=0, tiled=True)
    slot_rows = incoming.reshape(peers * CAP, -1)
    gate = jnp.dot(slot_rows, w_gate, preferred_element_type=jnp.float32)
    upper = jnp.dot(slot_rows, w_up, preferred_element_type=jnp.float32)
    act = (jax.nn.silu(gate) * upper).astype(jnp.bfloat16)
    partial_out = jnp.dot(act, w_down, preferred_element_type=jnp.float32)
    chosen = jnp.take_along_axis(logits, expert_ids, 1)
    gates = jax.nn.softmax(chosen, -1)
    spread = token_hot.T.astype(jnp.float32) * gates.reshape(-1)[None, :]
    combine = jnp.dot(spread, place.T.astype(jnp.float32), precision=lax.Precision.HIGHEST)
    returned = lax.all_to_all(
        partial_out.reshape(peers, CAP, -1),
        ("pool", "grp"),
        split_axis=0,
        concat_axis=0,
        tiled=True,
    )
    summed = jnp.sum(returned.reshape(experts, span, CAP, -1), 1).reshape(experts * CAP, -1)
    mixed = jnp.dot(combine, summed, precision=lax.Precision.HIGHEST)
    mine = lax.psum_scatter(mixed, "tp", scatter_dimension=1, tiled=True)
    return (hidden_state.astype(jnp.float32) + mine).astype(jnp.bfloat16)


def solution(mesh):
    placed = (
        P(("pool", "grp"), "tp"),
        P(("pool", "grp"), None, "tp"),
        P(("pool", "grp"), None, "tp"),
        P(("pool", "grp"), "tp"),
        P(("pool", "grp"), "tp"),
        P(("pool", "grp")),
        P(("pool", "grp"), "tp"),
        P("tp"),
        P("tp", None),
        P(("pool", "grp"), None),
        P(None, ("pool", "grp", "tp")),
        P(None, ("pool", "grp", "tp")),
        P(("pool", "grp", "tp"), None),
    )
    return jax.shard_map(
        shards, mesh=mesh, in_specs=placed, out_specs=P(("pool", "grp"), "tp"), check_vma=False
    )
```

profile of v0, /device:TPU:1, one launch (start us, length us, event | category | flops | bytes accessed | tf_op | source)
XLA Modules:
  0.0 349.2 jit_solution(14512973843035045105)
XLA Ops:
  6.5 0.9 iota_compare_fusion.9
  7.4 0.7 reshape.163
  8.1 0.8 copy.49
  9.0 10.4 %all-gather = bf16[4,1,1536]{2,1,0:T(2,128)(2,1)S(1)} all-gather(bf16[1,1,1536]{2,1,0:T(2,128)(2,1)S(1)} %reshape.163), channel_id=1, replica_groups=mesh['pool'=2,'grp'=16,'tp'=4] {'tp'}, dimensions={0}, use_global_device_ids=true | all-gather | bytes 15360 | tf_op jit(solution)/shard_map/all_gather | solution.py:80
  19.6 0.2 select_reduce_fusion
  19.8 0.7 reshape.169
  20.5 0.7 reshape.151
  21.2 1.0 reshape.138
  22.3 0.2 fusion.43
  22.5 1.3 fusion.42
  23.8 0.3 fusion.19
  24.2 2.3 fusion.13
  26.6 9.6 %all_gather.9 = bf16[32,6144]{1,0:T(8,128)(2,1)S(1)} all-gather(bf16[32,1536]{1,0:T(8,128)(2,1)S(1)} %add_convert_fusion.1), channel_id=1, replica_groups=mesh['pool'=2,'grp'=16,'tp'=4] {'tp'}, dimensions={1}, use_global_device_ids=true | all-gather | bytes 491520 | tf_op jit(solution)/shard_map/all_gather | solution.py:79
  36.2 0.2 fusion.16
  36.4 0.9 convolution_convert_fusion
  37.3 0.8 broadcast_in_dim.20
  38.1 87.2 %all_to_all.10 = bf16[32,16,6144]{2,1,0:T(8,128)(2,1)S(1)} all-to-all(bf16[32,16,6144]{2,1,0:T(8,128)(2,1)S(1)} %bitcast.49), channel_id=1, replica_groups=mesh['pool'=2,'grp'=16,'tp'=4] {'pool','grp'}, dimensions={0} | all-to-all | bytes 12582912 | tf_op jit(solution)/shard_map/all_to_all | solution.py:91
  125.3 3.4 fusion.44
  128.7 3.5 %fusion.6 = bf16[512,512]{1,0:T(8,128)(2,1)S(1)} fusion(bf16[512,6144]{1,0:T(8,128)(2,1)S(1)} %bitcast.54, bf16[6144,512]{1,0:T(8,128)(2,1)S(1)} %bitcast.63, f32[512,512]{1,0:T(8,128)S(1)} %fusion.44), kind=kOutput, calls=%fused_computation.10 | convolution fusion | flops 3222798336 | bytes 14155776 | tf_op jit(solution)/shard_map/dot_general | solution.py:94
  132.3 6.4 %fusion.45 = f32[512,6144]{1,0:T(8,128)} fusion(bf16[512,512]{1,0:T(8,128)(2,1)S(1)} %fusion.6, bf16[512,6144]{1,0:T(8,128)(2,1)S(1)} %bitcast.51), kind=kOutput, calls=%fused_computation.65 | convolution fusion | flops 3221225472 | bytes 19398656 | tf_op jit(solution)/shard_map/dot_general | solution.py:96
  138.6 6.3 %all-to-all-start.1 = ((f32[32,16,6144]{2,1,0:T(8,128)}), f32[32,16,6144]{2,1,0:T(8,128)}, u32[]{:S(2)}, u32[]{:S(2)}) async-start(f32[32,16,6144]{2,1,0:T(8,128)} %bitcast.48), calls=%async_computation.1 | async-start | bytes 25165824 | tf_op jit(solution)/shard_map/all_to_all | solution.py:101
  145.1 0.1 reshape.152
  145.2 10.4 %all_gather.11 = bf16[6144,8]{0,1:T(8,128)(2,1)S(1)} all-gather(bf16[1536,8]{0,1:T(8,128)(2,1)S(1)} %copy-done.3), channel_id=1, replica_groups=mesh['pool'=2,'grp'=16,'tp'=4] {'tp'}, dimensions={0}, use_global_device_ids=true | all-gather | bytes 122880 | tf_op jit(solution)/shard_map/all_gather | solution.py:81
  155.7 0.3 fusion.23
  156.0 0.7 gather_fusion
  157.0 0.1 div.52
  157.2 0.1 fusion.25
  157.3 153.7 %all-to-all-done.1 = f32[32,16,6144]{2,1,0:T(8,128)} async-done(((f32[32,16,6144]{2,1,0:T(8,128)}), f32[32,16,6144]{2,1,0:T(8,128)}, u32[]{:S(2)}, u32[]{:S(2)}) %all-to-all-start.1) | async-done | bytes 12582944 | tf_op jit(solution)/shard_map/all_to_all | solution.py:101
  311.0 5.9 %bitcast_reduce_fusion = f32[8,16,6144]{2,1,0:T(8,128)S(1)} fusion(f32[32,16,6144]{2,1,0:T(8,128)} %all-to-all-done.1), kind=kLoop, calls=%fused_computation.1 | loop fusion | flops 2359296 | bytes 15728640 | tf_op jit(solution)/shard_map/reduce_sum | solution.py:108
  316.9 2.6 fusion.46
  319.6 21.2 %reduce-scatter.2.cloned.1.call-done = f32[32,1536]{1,0:T(8,128)} async-done(((f32[32,6144]{1,0:T(8,128)}), f32[32,1536]{1,0:T(8,128)}) %reduce-scatter.2.cloned.1.call-update) | async-done | bytes 196624 | tf_op jit(solution)/shard_map/reduce_scatter | solution.py:110
  340.8 1.6 add_convert_fusion
  (45 shorter events, 1.0 us)
Async XLA Ops:
  6.5 15.9 %copy-start = (bf16[32,128,256]{2,1,0:T(8,128)(2,1)S(1)}, bf16[32,128,256]{2,1,0:T(8,128)(2,1)}, u32[]{:S(2)}) copy-start(bf16[32,128,256]{2,1,0:T(8,128)(2,1)} %param.14) | copy-start | bytes 6291460
  6.5 20.0 %copy-start.2 = (bf16[32,1536]{1,0:T(8,128)(2,1)S(1)}, bf16[32,1536]{1,0:T(8,128)(2,1)}, u32[]{:S(2)}) copy-start(bf16[32,1536]{1,0:T(8,128)(2,1)} %param.19) | copy-start | bytes 294916
  37.3 88.0 %slice-start.2 = ((s8[6291456]{0:T(1024)(128)(4,1)}), s8[4194304]{0:T(1024)(128)(4,1)S(1)}, s32[]{:S(2)}) async-start(s8[6291456]{0:T(1024)(128)(4,1)} %bitcast.60), calls=%async_computation.6 | async-start | bytes 8388608
  38.1 87.2 %slice-start.3 = ((s8[6291456]{0:T(1024)(128)(4,1)}), s8[2097152]{0:T(1024)(128)(4,1)S(1)}, s32[]{:S(2)}) async-start(s8[6291456]{0:T(1024)(128)(4,1)} %bitcast.60), calls=%async_computation.7 | async-start | bytes 4194304
  38.1 90.6 %slice-start.4 = ((s8[6291456]{0:T(1024)(128)(4,1)}), s8[4194304]{0:T(1024)(128)(4,1)S(1)}, s32[]{:S(2)}) async-start(s8[6291456]{0:T(1024)(128)(4,1)} %bitcast.62), calls=%async_computation.8 | async-start | bytes 8388608
  125.3 3.4 slice-start.5
  125.3 7.0 %slice-start = ((s8[6291456]{0:T(1024)(128)(4,1)}), s8[4194304]{0:T(1024)(128)(4,1)S(1)}, s32[]{:S(2)}) async-start(s8[6291456]{0:T(1024)(128)(4,1)} %bitcast.50), calls=%async_computation.4 | async-start | bytes 8388608
  128.7 3.5 %slice-start.1 = ((s8[6291456]{0:T(1024)(128)(4,1)}), s8[2097152]{0:T(1024)(128)(4,1)S(1)}, s32[]{:S(2)}) async-start(s8[6291456]{0:T(1024)(128)(4,1)} %bitcast.50), calls=%async_computation.5 | async-start | bytes 4194304
  138.6 6.4 %copy-start.4 = (s32[32,2]{0,1:T(2,128)S(1)}, s32[32,2]{0,1:T(2,128)}, u32[]{:S(2)}) copy-start(s32[32,2]{0,1:T(2,128)} %param.22) | copy-start | bytes 772
  138.6 6.6 %copy-start.3 = (bf16[1536,8]{0,1:T(8,128)(2,1)S(1)}, bf16[1536,8]{0,1:T(8,128)(2,1)}, u32[]{:S(2)}) copy-start(bf16[1536,8]{0,1:T(8,128)(2,1)} %param.21) | copy-start | bytes 73732
  138.6 172.4 %all-to-all-start.1 = ((f32[32,16,6144]{2,1,0:T(8,128)}), f32[32,16,6144]{2,1,0:T(8,128)}, u32[]{:S(2)}, u32[]{:S(2)}) async-start(f32[32,16,6144]{2,1,0:T(8,128)} %bitcast.48), calls=%async_computation.1 | async-start | bytes 25165824 | tf_op jit(solution)/shard_map/all_to_all | solution.py:101
  145.0 195.8 %reduce-scatter.2.cloned.1.call-start = ((), (), s32[]{:S(2)}) async-start(), calls=%async_computation.3 | async-start | bytes 983040 | tf_op jit(solution)/shard_map/reduce_scatter | solution.py:110
  311.0 31.3 %copy-start.1 = (bf16[32,128,256]{2,1,0:T(8,128)(2,1)S(1)}, bf16[32,128,256]{2,1,0:T(8,128)(2,1)}, u32[]{:S(2)}) copy-start(bf16[32,128,256]{2,1,0:T(8,128)(2,1)} %param.14) | copy-start | bytes 6291460
Sparse Core Ops, SparseCore 0:
  319.7 21.0 reduce-scatter.1
where the time goes:
time: 350 us; the launch traced here: 349 us
  waiting for transfers between devices  175 us (50%)
  blocking collectives  118 us (34%)
  matrix products  21 us (6%)
  between operations  13.7 us (4%)
  other arithmetic  9.42 us (3%)
  starting transfers between devices  6.36 us (2%)
  local copies, waits for them, and re-layouts  6.23 us (2%)
    all_to_all x1, waiting for transfers between devices, shards(): lax.all_to_all(partial_out.reshape(peers, CAP, -1), ('pool', 'grp'), spli...  154 us
    all_to_all x1, blocking collectives, shards(): lax.all_to_all(outgoing, ('pool', 'grp'), split_axis=0, concat_axis=0, ti...  87.2 us
    reduce_scatter x1, waiting for transfers between devices, shards(): mine = lax.psum_scatter(mixed, 'tp', scatter_dimension=1, tiled=True)  21.2 us
    all_gather x1, blocking collectives, shards(): lax.all_gather(w_router, 'tp', axis=0, tiled=True)  10.4 us
    all_gather x1, blocking collectives, shards(): lax.all_gather(norm_gain, 'tp', axis=0, tiled=True)  10.4 us
    all_gather x1, blocking collectives, shards(): lax.all_gather(hidden_state, 'tp', axis=1, tiled=True)  9.63 us
  transfers between devices with their start and end apart: 2, of which 2 were waited for; matrix products, arithmetic and copies ran while one was open for 1% of the time, Pallas kernels for 0%

commit v1 on v0

v1 whole, which is shorter than its diff:
```python
import functools

import jax
import jax.numpy as jnp
from jax import lax
from jax.experimental import pallas as pl
from jax.experimental.pallas import tpu as pltpu
from jax.sharding import Mesh
from jax.sharding import PartitionSpec as P

HD = 128
TOP = 2
CAP = 16
RING = 4
GROUPS = 1
bf16 = jnp.bfloat16
f32 = jnp.float32


def attend(queries, key_cache, value_cache, key_new, value_new, lengths):
    rows = queries.shape[0]
    heads_kv = key_new.shape[1] // HD
    repeat = queries.shape[1] // HD // heads_kv
    length = key_cache.shape[1]
    scale = 1.0 / HD**0.5
    qhead = queries.reshape(rows, heads_kv, repeat, HD)
    kcache = key_cache.reshape(rows, length, heads_kv, HD)
    vcache = value_cache.reshape(rows, length, heads_kv, HD)
    knew = key_new.reshape(rows, heads_kv, HD)
    vnew = value_new.reshape(rows, heads_kv, 1, HD).astype(f32)
    scores = jnp.einsum("rgho,rcgo->rghc", qhead, kcache, preferred_element_type=f32) * scale
    own = jnp.einsum("rgho,rgo->rgh", qhead, knew, preferred_element_type=f32) * scale
    valid = jnp.arange(length, dtype=jnp.int32)[None, :] < lengths[:, None]
    scores = jnp.where(valid[:, None, None, :], scores, -1e30)
    top = jnp.maximum(jnp.max(scores, -1), own)
    probs = jnp.exp(scores - top[..., None])
    pown = jnp.exp(own - top)
    total = jnp.sum(probs, -1) + pown
    weights = (probs / total[..., None]).astype(bf16)
    wown = (pown / total).astype(bf16).astype(f32)
    result = (
        jnp.einsum("rghc,rcgo->rgho", weights, vcache, preferred_element_type=f32)
        + wown[..., None] * vnew
    )
    return result.reshape(rows, repeat * heads_kv * HD)


def along(x, axis, by):
    return lax.ppermute(x, axis, [(i, (i + by) % RING) for i in range(RING)])


def swap_cores(x):
    return lax.ppermute(x, "pool", [(0, 1), (1, 0)])


def cross(x, leg, by):
    pairs = []
    for core in range(2):
        for i in range(RING):
            for j in range(RING):
                to = ((i + by) % RING, j) if core == leg else (i, (j + by) % RING)
                pairs.append((core * 16 + i * RING + j, core * 16 + to[0] * RING + to[1]))
    return lax.ppermute(x, ("pool", "x", "tp"), pairs)


def expert_kernel(
    place, own, above, below, far_a, far_b, inverse, w_gate, w_up, w_down,
    out_own, out_above, out_below, out_far_a, out_far_b,
    rows, gates, ups, downs, gate, upper, square, act, row_sem, gate_sem, up_sem, down_sem, out_sem,
):
    core, me = place[0], place[1]
    _, _, block, features = rows.shape
    units = gate.shape[1]
    count = RING * block

    def part(refs, outer, inner):
        first, second, far_1, far_2, third = refs
        if outer == 2:
            return far_1.at[inner] if inner < 2 else far_2.at[inner - 2]
        return {0: first, 1: second, 3: third}[outer].at[inner]

    def turned(quarter):
        return pl.ds(pl.multiple_of(lax.rem(me + quarter, RING) * features, features), features)

    arrived = (own, above, far_a, far_b, below)
    leaving = (out_own, out_above, out_far_a, out_far_b, out_below)

    def fetch(quarter, piece, flipped):
        source = part(arrived, piece, quarter) if flipped else part(arrived, quarter, piece)
        return pltpu.make_async_copy(source, rows.at[quarter, piece], row_sem.at[quarter, piece])

    def put(quarter, piece, flipped):
        target = part(leaving, piece, quarter) if flipped else part(leaving, quarter, piece)
        return pltpu.make_async_copy(rows.at[quarter, piece], target, out_sem.at[quarter, piece])

    def fetch_gate(quarter):
        return pltpu.make_async_copy(w_gate.at[turned(quarter), :], gates.at[quarter], gate_sem.at[quarter])

    def fetch_up(quarter):
        return pltpu.make_async_copy(w_up.at[turned(quarter), :], ups.at[quarter], up_sem.at[quarter])

    def fetch_down(quarter):
        return pltpu.make_async_copy(w_down.at[:, turned(quarter)], downs.at[quarter], down_sem.at[quarter])

    for quarter in range(RING):
        for flipped in range(2):
            @pl.when(core == flipped)
            def _():
                for piece in range(RING):
                    fetch(quarter, piece, flipped).start()
        fetch_gate(quarter).start()
        fetch_up(quarter).start()
    for quarter in range(RING):
        fetch_down(quarter).start()

    gate[...] = jnp.zeros_like(gate)
    upper[...] = jnp.zeros_like(upper)
    square[...] = jnp.zeros_like(square)

    @pl.loop(0, RING)
    def _(quarter):
        for piece in range(RING):
            pltpu.make_async_copy(
                own.at[0], rows.at[quarter, piece], row_sem.at[quarter, piece]
            ).wait()
        fetch_gate(quarter).wait()
        held = rows[quarter].reshape(count, features)
        gate[...] += jnp.dot(held, gates[quarter], preferred_element_type=f32)
        fetch_up(quarter).wait()
        upper[...] += jnp.dot(held, ups[quarter], preferred_element_type=f32)

        @pl.loop(0, features // 128)
        def _(lane):
            lanes = pl.ds(pl.multiple_of(lane * 128, 128), 128)
            plain = rows[quarter, :, :, lanes].reshape(count, 128).astype(f32) * inverse[quarter, :, lanes]
            square[...] += plain * plain

    mean = jnp.sum(square[...], -1, keepdims=True) / (RING * features)
    scale = lax.rsqrt(mean + 1e-05)
    scaled = gate[...] * scale
    act[...] = (scaled * jax.nn.sigmoid(scaled) * (upper[...] * scale)).astype(bf16)

    @pl.loop(0, RING)
    def _(quarter):
        fetch_down(quarter).wait()
        outcome = jnp.dot(act[...], downs[quarter], preferred_element_type=f32)
        rows[quarter] = outcome.astype(bf16).reshape(RING, block, features)
        for which in range(RING):
            for flipped in range(2):
                @pl.when((core == flipped) & (quarter == which))
                def _():
                    for piece in range(RING):
                        put(which, piece, flipped).start()

    for quarter in range(RING):
        for piece in range(RING):
            put(quarter, piece, 0).wait()


def expert(place, pieces, inverse, w_gate, w_up, w_down):
    own, above, below, far_a, far_b = pieces
    _, block, features = own.shape
    units = w_gate.shape[1]
    whole = jax.ShapeDtypeStruct(own.shape, bf16)
    half = jax.ShapeDtypeStruct(far_a.shape, bf16)
    anywhere = pl.BlockSpec(memory_space=pl.ANY)
    count = RING * block
    return pl.pallas_call(
        expert_kernel,
        out_shape=[whole, whole, whole, half, half],
        in_specs=[pl.BlockSpec(memory_space=pltpu.SMEM)]
        + [anywhere] * 5
        + [pl.BlockSpec(memory_space=pltpu.VMEM)]
        + [anywhere] * 3,
        out_specs=[anywhere] * 5,
        scratch_shapes=[
            pltpu.VMEM((RING, RING, block, features), bf16),
            pltpu.VMEM((RING, features, units), bf16),
            pltpu.VMEM((RING, features, units), bf16),
            pltpu.VMEM((RING, units, features), bf16),
            pltpu.VMEM((count, units), f32),
            pltpu.VMEM((count, units), f32),
            pltpu.VMEM((count, 128), f32),
            pltpu.VMEM((count, units), bf16),
            pltpu.SemaphoreType.DMA((RING, RING)),
            pltpu.SemaphoreType.DMA((RING,)),
            pltpu.SemaphoreType.DMA((RING,)),
            pltpu.SemaphoreType.DMA((RING,)),
            pltpu.SemaphoreType.DMA((RING, RING)),
        ],
        compiler_params=pltpu.CompilerParams(vmem_limit_bytes=52 * 1024 * 1024),
        cost_estimate=pl.CostEstimate(
            flops=6 * count * RING * features * units,
            bytes_accessed=6 * RING * features * (units + count // 3),
            transcendentals=count * units,
        ),
        name="expert",
    )(place, own, above, below, far_a, far_b, inverse, w_gate, w_up, w_down)


def shards(
    queries, key_cache, value_cache, key_new, value_new, lengths, residual,
    norm_gain, w_router, expert_ids, w_gate, w_up, w_down,
):
    rows, features = residual.shape
    experts = w_router.shape[1]
    me_pool, me_z, me_y = lax.axis_index("pool"), lax.axis_index("z"), lax.axis_index("tp")
    place = jnp.stack([me_pool, me_y]).astype(jnp.int32)
    gains = [norm_gain, along(norm_gain, "tp", -1), along(norm_gain, "tp", 2), along(norm_gain, "tp", 1)]
    inverse = 1.0 / jnp.stack(gains).astype(f32)[:, None, :]

    attn = attend(queries, key_cache, value_cache, key_new, value_new, lengths)
    hidden_state = (residual.astype(f32) + attn).astype(bf16)
    hfloat = hidden_state.astype(f32)
    raised = (hfloat * norm_gain.astype(f32)[None, :]).astype(bf16)

    near = ((expert_ids // RING + me_pool) % 2) * RING + (expert_ids % RING - me_z + RING) % RING
    flat = near.reshape(-1)
    expert_hot = (flat[:, None] == jnp.arange(experts, dtype=jnp.int32)[None, :]).astype(jnp.int32)
    earlier = jnp.cumsum(expert_hot, 0) - expert_hot
    slot = jnp.sum(earlier * expert_hot, 1)
    size = CAP // GROUPS
    position = (((slot // size) * experts + flat) * size + slot % size).reshape(rows, TOP)
    places = jnp.arange(experts * CAP, dtype=jnp.int32)
    hot = position[:, :, None] == places[None, None, :]
    dispatch = jnp.any(hot, 1).T.astype(bf16)
    bucket = jnp.dot(dispatch, raised, preferred_element_type=f32).astype(bf16)
    buckets = bucket.reshape(GROUPS, 2, RING, size, features)

    stats = jnp.concatenate(
        [
            jnp.dot(raised, w_router, preferred_element_type=f32),
            jnp.sum(hfloat * hfloat, -1, keepdims=True),
        ],
        1,
    )

    returned = []
    for group in range(GROUPS):
        partner = swap_cores(buckets[group, 1])
        pairs = jnp.stack([buckets[group, 0], partner], 1).reshape(RING, 2 * size, features)
        block = jnp.concatenate([pairs[0]] + [along(pairs[d], "z", d) for d in range(1, RING)])
        first = jnp.stack([block, cross(block, 0, -1), cross(block, 0, 2), cross(block, 0, 1)])
        if group == 0:
            stats, first = lax.optimization_barrier((stats, first))
            stats = lax.psum(stats, "tp")
        above = cross(first, 1, -1)
        below = cross(first, 1, 1)
        far_a = cross(above[:2], 1, -1)
        far_b = cross(below[2:], 1, 1)
        if group == 0:
            stats, inverse = lax.optimization_barrier((stats, inverse))
        own_out, above_out, below_out, far_a_out, far_b_out = expert(
            place, (first, above, below, far_a, far_b), inverse, w_gate, w_up, w_down
        )
        relay_a = cross(far_a_out, 1, 1)
        relay_b = cross(far_b_out, 1, -1)
        up = jnp.concatenate([(above_out[:2].astype(f32) + relay_a.astype(f32)).astype(bf16), above_out[2:]])
        down = jnp.concatenate([below_out[:2], (below_out[2:].astype(f32) + relay_b.astype(f32)).astype(bf16)])
        from_below = cross(up, 1, 1)
        from_above = cross(down, 1, -1)
        mine = own_out.astype(f32) + from_below.astype(f32) + from_above.astype(f32)
        sent = mine.astype(bf16)
        total = mine[0]
        for d in range(1, RING):
            total = total + cross(sent[d], 0, d).astype(f32)
        back = total.astype(bf16).reshape(RING, 2, size, features)
        home = jnp.stack([back[0]] + [along(back[d], "z", -d) for d in range(1, RING)])
        returned.append(jnp.stack([home[:, 0], swap_cores(home[:, 1])]))

    logits = stats[:, :experts] * lax.rsqrt(stats[:, experts:] / (features * RING) + 1e-05)
    chosen = jnp.take_along_axis(logits, expert_ids, 1)
    gates = jax.nn.softmax(chosen, -1)
    combine = jnp.sum(jnp.where(hot, gates[:, :, None], 0.0), 1)
    results = jnp.stack(returned).reshape(experts * CAP, features)
    mixed = jnp.dot(combine, results.astype(f32), precision=lax.Precision.HIGHEST)
    return (hfloat + mixed).astype(bf16)


def solution(mesh):
    split = Mesh(mesh.devices.reshape(2, RING, RING, RING), ("pool", "z", "x", "tp"))
    rows = ("pool", "z", "x")
    every = ("pool", "z", "x", "tp")
    placed = (
        P(rows, "tp"),
        P(rows, None, "tp"),
        P(rows, None, "tp"),
        P(rows, "tp"),
        P(rows, "tp"),
        P(rows),
        P(rows, "tp"),
        P("tp"),
        P("tp", None),
        P(rows, None),
        P(None, every),
        P(None, every),
        P(every, None),
    )
    return jax.shard_map(
        shards, mesh=split, in_specs=placed, out_specs=P(rows, "tp"), check_vma=False
    )
```

time: 350 us -> 186 us (0.53)
  blocking collectives: 118 us -> 9.07 us
  waiting for transfers between devices: 175 us -> 80.9 us
  starting transfers between devices: 6.36 us -> 51.7 us
  Pallas kernels: 0 us -> 19.8 us
  matrix products: 21 us -> 5.2 us
  between operations: 13.7 us -> 0.36 us
    all_to_all x1 -> x0, waiting for transfers between devices: 154 us -> none  [shards(): lax.all_to_all(partial_out.reshape(peers, CAP, -1), ('pool', 'grp'), spli...]
    all_to_all x1 -> x0, blocking collectives: 87.2 us -> none  [shards(): lax.all_to_all(outgoing, ('pool', 'grp'), split_axis=0, concat_axis=0, ti...]
    ppermute x0 -> x25, waiting for transfers between devices: none -> 80.9 us  [the longest x14 66.6 us: cross(): return lax.ppermute(x, ('pool', 'x', 'tp'), pairs)]
    ppermute x0 -> x25, starting transfers between devices: none -> 51.7 us  [the longest x2 23.7 us: swap_cores(): return lax.ppermute(x, 'pool', [(0, 1), (1, 0)])]
    all_gather x3 -> x0, blocking collectives: 30.4 us -> none  [the longest x1 10.4 us: shards(): lax.all_gather(w_router, 'tp', axis=0, tiled=True)]
    reduce_scatter x1 -> x0, waiting for transfers between devices: 21.2 us -> none  [shards(): mine = lax.psum_scatter(mixed, 'tp', scatter_dimension=1, tiled=True)]
    pallas_call x0 -> x1, Pallas kernels: none -> 19.8 us  [expert(): pl.pallas_call(expert_kernel, out_shape=[whole, whole, whole, half, half]...]
    dot_general x10 -> x6, matrix products: 21 us -> 5.2 us  [the longest x1 2.34 us: attend(): jnp.einsum('rghc,rcgo->rgho', weights, vcache, preferred_element_type=f32)]
  transfers between devices with their start and end apart: 2 -> 25, of which waited for: 2 -> 18; matrix products, arithmetic and copies ran while one was open for 1% -> 4% of each run, Pallas kernels for 0% -> 0%
where the time goes in v1:
time: 186 us
  waiting for transfers between devices  80.9 us (43%)
  starting transfers between devices  51.7 us (28%)
  Pallas kernels  19.8 us (11%)
  other arithmetic  11.5 us (6%)
  blocking collectives  9.07 us (5%)
  local copies, waits for them, and re-layouts  7.42 us (4%)
  matrix products  5.2 us (3%)
    ppermute x14, waiting for transfers between devices, cross(): return lax.ppermute(x, ('pool', 'x', 'tp'), pairs)  66.6 us
    ppermute x2, starting transfers between devices, swap_cores(): return lax.ppermute(x, 'pool', [(0, 1), (1, 0)])  23.7 us
    pallas_call x1, Pallas kernels, expert(): pl.pallas_call(expert_kernel, out_shape=[whole, whole, whole, half, half]...  19.8 us
    ppermute x14, starting transfers between devices, cross(): return lax.ppermute(x, ('pool', 'x', 'tp'), pairs)  17.9 us
    ppermute x9, waiting for transfers between devices, along(): return lax.ppermute(x, axis, [(i, (i + by) % RING) for i in range(RING)])  12.3 us
    ppermute x9, starting transfers between devices, along(): return lax.ppermute(x, axis, [(i, (i + by) % RING) for i in range(RING)])  10.2 us
    psum x1, blocking collectives, shards(): stats = lax.psum(stats, 'tp')  9.07 us
    convert_element_type x1, other arithmetic, shards(): sent = mine.astype(bf16)  4.69 us
  transfers between devices with their start and end apart: 25, of which 18 were waited for; matrix products, arithmetic and copies ran while one was open for 4% of the time, Pallas kernels for 0%

profile of v1, /device:TPU:1, one launch (start us, length us, event | category | flops | bytes accessed | tf_op | source)
XLA Modules:
  0.0 186.0 jit_solution(14817372274789273515)
XLA Ops:
  2.9 1.3 fusion.48
  4.6 2.3 %fusion.13 = f32[32,2,6,128]{3,2,1,0:T(8,128)S(1)} fusion(f32[32,2,6,128]{3,2,1,0:T(8,128)S(1)} %get-tuple-element.49, f32[32,2,128]{2,1,0:T(2,128)S(1)} %reshape.207, f32[32,2,6]{2,1,0:T(2,128)S(1)} %get-tuple-element.47, f32[32,2,6]{2,1,0:T(2,128)S(1)} %get-tuple-element.46, f32[32,2,6]{2,1,0:T(2,128)S(1)} %multiply_maximum_fusion, ...), kind=kOutput, calls=%fused_computation.18 | convolution fusion | flops 12828672 | bytes 2527744 | tf_op jit(solution)/shard_map/rghc,rcgo->rgho/dot_general | solution.py:42
  8.4 1.5 collective-permute-start
  11.1 1.8 collective-permute-start.1
  12.8 3.3 %collective-permute-start.2 = (bf16[32,1536]{1,0:T(8,128)(2,1)S(1)}, bf16[32,1536]{1,0:T(8,128)(2,1)S(1)}, u32[]{:S(2)}, u32[]{:S(2)}) collective-permute-start(bf16[32,1536]{1,0:T(8,128)(2,1)S(1)} %bitcast.104), channel_id=1, source_target_pairs={{0,32},{16,48},{32,0},{48,16},{1,33},{17,49},{33,1},{49,17},{2,34}... | collective-permute-start | bytes 294920 | tf_op jit(solution)/shard_map/ppermute | solution.py:49
  17.8 3.0 %collective-permute-done.2 = bf16[32,1536]{1,0:T(8,128)(2,1)S(1)} collective-permute-done((bf16[32,1536]{1,0:T(8,128)(2,1)S(1)}, bf16[32,1536]{1,0:T(8,128)(2,1)S(1)}, u32[]{:S(2)}, u32[]{:S(2)}) %collective-permute-start.2) | collective-permute-done | bytes 98336 | tf_op jit(solution)/shard_map/ppermute | solution.py:49
  20.9 2.8 %collective-permute-start.4 = (bf16[128,1536]{1,0:T(8,128)(2,1)S(1)}, bf16[128,1536]{1,0:T(8,128)(2,1)S(1)}, u32[]{:S(2)}, u32[]{:S(2)}) collective-permute-start(bf16[128,1536]{1,0:T(8,128)(2,1)S(1)} %get-tuple-element.39), channel_id=1, source_target_pairs={{0,12},{1,13},{2,14},{3,15},{4,0},{5,1},{6,2},{7,3},{8,4},{9,5},{1... | collective-permute-start | bytes 1179656 | tf_op jit(solution)/shard_map/ppermute | solution.py:63
  24.9 7.7 %collective-permute-done.4 = bf16[128,1536]{1,0:T(8,128)(2,1)S(1)} collective-permute-done((bf16[128,1536]{1,0:T(8,128)(2,1)S(1)}, bf16[128,1536]{1,0:T(8,128)(2,1)S(1)}, u32[]{:S(2)}, u32[]{:S(2)}) %collective-permute-start.4) | collective-permute-done | bytes 393248 | tf_op jit(solution)/shard_map/ppermute | solution.py:63
  32.6 3.7 %collective-permute-done.6 = bf16[128,1536]{1,0:T(8,128)(2,1)S(1)} collective-permute-done((bf16[128,1536]{1,0:T(8,128)(2,1)S(1)}, bf16[128,1536]{1,0:T(8,128)(2,1)S(1)}, u32[]{:S(2)}, u32[]{:S(2)}) %collective-permute-start.6) | collective-permute-done | bytes 393248 | tf_op jit(solution)/shard_map/ppermute | solution.py:63
  36.5 2.3 %collective-permute-start.10 = (bf16[4,128,1536]{2,1,0:T(8,128)(2,1)S(1)}, bf16[4,128,1536]{2,1,0:T(8,128)(2,1)S(1)}, u32[]{:S(2)}, u32[]{:S(2)}) collective-permute-start(bf16[4,128,1536]{2,1,0:T(8,128)(2,1)S(1)} %pad_maximum_fusion.own), channel_id=1, source_target_pairs={{0,3},{1,0},{2,1},{3,2},{4,7},{5,4},{6,5},{7,6},{8,11},{9,8},{10,9... | collective-permute-start | bytes 4718600 | tf_op jit(solution)/shard_map/ppermute | solution.py:63
  38.8 17.4 %collective-permute-done.10.above = bf16[4,128,1536]{2,1,0:T(8,128)(2,1)S(1)} collective-permute-done((bf16[4,128,1536]{2,1,0:T(8,128)(2,1)S(1)}, bf16[4,128,1536]{2,1,0:T(8,128)(2,1)S(1)}, u32[]{:S(2)}, u32[]{:S(2)}) %collective-permute-start.10) | collective-permute-done | bytes 1572896 | tf_op jit(solution)/shard_map/ppermute | solution.py:63
  56.2 3.5 %collective-permute-start.12 = (bf16[2,128,1536]{2,1,0:T(8,128)(2,1)S(1)}, bf16[2,128,1536]{2,1,0:T(8,128)(2,1)}, u32[]{:S(2)}, u32[]{:S(2)}) collective-permute-start(bf16[2,128,1536]{2,1,0:T(8,128)(2,1)S(1)} %slice.117), channel_id=1, source_target_pairs={{0,3},{1,0},{2,1},{3,2},{4,7},{5,4},{6,5},{7,6},{8,11},{9,8},{10,9... | collective-permute-start | bytes 2359304 | tf_op jit(solution)/shard_map/ppermute | solution.py:63
  62.7 1.3 collective-permute-done.7
  64.0 1.7 collective-permute-done.8
  66.0 9.1 %psum.7 = f32[32,9]{0,1:T(8,128)S(1)} all-reduce(f32[32,9]{0,1:T(8,128)S(1)} %pad_maximum_fusion.7), channel_id=1, replica_groups=mesh['pool'=2,'z'=4,'x'=4,'tp'=4] {'tp'}, use_global_device_ids=true, to_apply=%region_6.7 | all-reduce | flops 288 | bytes 2304 | tf_op jit(solution)/shard_map/psum | solution.py:246
  75.1 19.8 %expert.1 = (bf16[4,128,1536]{2,1,0:T(8,128)(2,1)}, bf16[4,128,1536]{2,1,0:T(8,128)(2,1)}, bf16[4,128,1536]{2,1,0:T(8,128)(2,1)}, bf16[2,128,1536]{2,1,0:T(8,128)(2,1)S(1)}, bf16[2,128,1536]{2,1,0:T(8,128)(2,1)S(1)}) custom-call(s32[2]{0:T(128)S(1)} %pad_add_fusion.place, bf16[4,128,1536]{2,1,0:T(8,128)(2,1)} %copy-done.1, bf16[4,128,1536]{2,1,0:T(8,128)(2,1)} %copy-done.4, ...), custom_call_target="tpu_custom_call" | custom-call | flops 9663676416 | bytes 25141248 | tf_op jit(solution)/shard_map/expert/pallas_call | solution.py:168
  95.1 1.3 slice.93
  96.4 2.7 %collective-permute-start.16 = (bf16[2,128,1536]{2,1,0:T(8,128)(2,1)S(1)}, bf16[2,128,1536]{2,1,0:T(8,128)(2,1)S(1)}, u32[]{:S(2)}, u32[]{:S(2)}) collective-permute-start(bf16[2,128,1536]{2,1,0:T(8,128)(2,1)S(1)} %get-tuple-element.22), channel_id=1, source_target_pairs={{0,3},{1,0},{2,1},{3,2},{4,7},{5,4},{6,5},{7,6},{8,11},{9,8},{10,9... | collective-permute-start | bytes 2359304 | tf_op jit(solution)/shard_map/ppermute | solution.py:63
  99.2 7.9 %collective-permute-done.14 = bf16[2,128,1536]{2,1,0:T(8,128)(2,1)S(1)} collective-permute-done((bf16[2,128,1536]{2,1,0:T(8,128)(2,1)S(1)}, bf16[2,128,1536]{2,1,0:T(8,128)(2,1)S(1)}, u32[]{:S(2)}, u32[]{:S(2)}) %collective-permute-start.14) | collective-permute-done | bytes 786464 | tf_op jit(solution)/shard_map/ppermute | solution.py:63
  107.3 1.3 pad_maximum_fusion.1
  108.8 1.3 pad_maximum_fusion.2
  110.1 2.8 %collective-permute-start.17 = (bf16[4,128,1536]{2,1,0:T(8,128)(2,1)}, bf16[4,128,1536]{2,1,0:T(8,128)(2,1)}, u32[]{:S(2)}, u32[]{:S(2)}) collective-permute-start(bf16[4,128,1536]{2,1,0:T(8,128)(2,1)} %pad_maximum_fusion.2), channel_id=1, source_target_pairs={{0,3},{1,0},{2,1},{3,2},{4,7},{5,4},{6,5},{7,6},{8,11},{9,8},{10,9... | collective-permute-start | bytes 4718600 | tf_op jit(solution)/shard_map/ppermute | solution.py:63
  113.2 16.5 %collective-permute-done.15 = bf16[4,128,1536]{2,1,0:T(8,128)(2,1)} collective-permute-done((bf16[4,128,1536]{2,1,0:T(8,128)(2,1)}, bf16[4,128,1536]{2,1,0:T(8,128)(2,1)}, u32[]{:S(2)}, u32[]{:S(2)}) %collective-permute-start.15) | collective-permute-done | bytes 1572896 | tf_op jit(solution)/shard_map/ppermute | solution.py:63
  130.6 4.7 %fusion.45 = (bf16[4,128,1536]{2,1,0:T(8,128)(2,1)S(1)}, f32[4,128,1536]{2,1,0:T(8,128)}) fusion(bf16[4,128,1536]{2,1,0:T(8,128)(2,1)} %collective-permute-done.17, bf16[4,128,1536]{2,1,0:T(8,128)(2,1)} %collective-permute-done.15, bf16[4,128,1536]{2,1,0:T(8,128)(2,1)} %get-tuple-element.18), kind=kLoop, calls=%fused_computation.102 | loop fusion | flops 4718592 | bytes 9437184 | tf_op jit(solution)/shard_map/convert_element_type | solution.py:263
  136.9 2.1 %collective-permute-start.20 = (bf16[128,1536]{1,0:T(8,128)(2,1)S(1)}, bf16[128,1536]{1,0:T(8,128)(2,1)}, u32[]{:S(2)}, u32[]{:S(2)}) collective-permute-start(bf16[128,1536]{1,0:T(8,128)(2,1)S(1)} %get-tuple-element.30), channel_id=1, source_target_pairs={{0,12},{1,13},{2,14},{3,15},{4,0},{5,1},{6,2},{7,3},{8,4},{9,5},{1... | collective-permute-start | bytes 1179656 | tf_op jit(solution)/shard_map/ppermute | solution.py:63
  139.9 11.1 %collective-permute-done.18 = bf16[128,1536]{1,0:T(8,128)(2,1)S(1)} collective-permute-done((bf16[128,1536]{1,0:T(8,128)(2,1)}, bf16[128,1536]{1,0:T(8,128)(2,1)S(1)}, u32[]{:S(2)}, u32[]{:S(2)}) %collective-permute-start.18) | collective-permute-done | bytes 393248 | tf_op jit(solution)/shard_map/ppermute | solution.py:63
  151.0 1.2 collective-permute-done.20
  152.3 1.4 fusion.19
  153.7 2.0 %collective-permute-start.21 = (bf16[2,16,1536]{2,1,0:T(8,128)(2,1)S(1)}, bf16[2,16,1536]{2,1,0:T(8,128)(2,1)S(1)}, u32[]{:S(2)}, u32[]{:S(2)}) collective-permute-start(bf16[2,16,1536]{2,1,0:T(8,128)(2,1)S(1)} %bitcast.105), channel_id=1, source_target_pairs={{0,48},{16,0},{32,16},{48,32},{1,49},{17,1},{33,17},{49,33},{2,50}... | collective-permute-start | bytes 294920 | tf_op jit(solution)/shard_map/ppermute | solution.py:49
  156.7 1.6 collective-permute-done.21
  158.3 2.4 %collective-permute-done.22 = bf16[2,16,1536]{2,1,0:T(8,128)(2,1)S(1)} collective-permute-done((bf16[2,16,1536]{2,1,0:T(8,128)(2,1)S(1)}, bf16[2,16,1536]{2,1,0:T(8,128)(2,1)S(1)}, u32[]{:S(2)}, u32[]{:S(2)}) %collective-permute-start.22) | collective-permute-done | bytes 98336 | tf_op jit(solution)/shard_map/ppermute | solution.py:49
  161.8 22.2 %collective-permute-start.24 = (bf16[4,16,1536]{2,1,0:T(8,128)(2,1)S(1)}, bf16[4,16,1536]{2,1,0:T(8,128)(2,1)S(1)}, u32[]{:S(2)}, u32[]{:S(2)}) collective-permute-start(bf16[4,16,1536]{2,1,0:T(8,128)(2,1)S(1)} %get-tuple-element.33), channel_id=1, source_target_pairs={{0,64},{64,0},{1,65},{65,1},{2,66},{66,2},{3,67},{67,3},{4,68},{68... | collective-permute-start | bytes 589832 | tf_op jit(solution)/shard_map/ppermute | solution.py:53
  (106 shorter events, 20.6 us)
Async XLA Ops:
  4.6 3.3 %copy-start.8 = (bf16[1536]{0:T(1024)(128)(2,1)S(1)}, bf16[1536]{0:T(1024)(128)(2,1)}, u32[]{:S(2)}) copy-start(bf16[1536]{0:T(1024)(128)(2,1)} %param.20) | copy-start | bytes 9220
  4.6 3.3 %copy-start.6 = (bf16[32,1536]{1,0:T(8,128)(2,1)S(1)}, bf16[32,1536]{1,0:T(8,128)(2,1)}, u32[]{:S(2)}) copy-start(bf16[32,1536]{1,0:T(8,128)(2,1)} %param.19) | copy-start | bytes 294916
  8.1 16.6 %copy-start.10 = (bf16[1536,8]{0,1:T(8,128)(2,1)S(1)}, bf16[1536,8]{0,1:T(8,128)(2,1)}, u32[]{:S(2)}) copy-start(bf16[1536,8]{0,1:T(8,128)(2,1)} %param.21) | copy-start | bytes 73732
  8.4 2.6 %collective-permute-start = (bf16[4,16,1536]{2,1,0:T(8,128)(2,1)S(1)}, bf16[4,16,1536]{2,1,0:T(8,128)(2,1)S(1)}, u32[]{:S(2)}, u32[]{:S(2)}) collective-permute-start(bf16[4,16,1536]{2,1,0:T(8,128)(2,1)S(1)} %get-tuple-element.45), channel_id=1, source_target_pairs={{0,64},{64,0},{1,65},{65,1},{2,66},{66,2},{3,67},{67,3},{4,68},{68... | collective-permute-start | bytes 589832 | tf_op jit(solution)/shard_map/ppermute | solution.py:53
  11.1 6.8 %collective-permute-start.1 = (bf16[32,1536]{1,0:T(8,128)(2,1)S(1)}, bf16[32,1536]{1,0:T(8,128)(2,1)S(1)}, u32[]{:S(2)}, u32[]{:S(2)}) collective-permute-start(bf16[32,1536]{1,0:T(8,128)(2,1)S(1)} %bitcast.107), channel_id=1, source_target_pairs={{0,16},{16,32},{32,48},{48,0},{1,17},{17,33},{33,49},{49,1},{2,18}... | collective-permute-start | bytes 294920 | tf_op jit(solution)/shard_map/ppermute | solution.py:49
  12.8 8.0 %collective-permute-start.2 = (bf16[32,1536]{1,0:T(8,128)(2,1)S(1)}, bf16[32,1536]{1,0:T(8,128)(2,1)S(1)}, u32[]{:S(2)}, u32[]{:S(2)}) collective-permute-start(bf16[32,1536]{1,0:T(8,128)(2,1)S(1)} %bitcast.104), channel_id=1, source_target_pairs={{0,32},{16,48},{32,0},{48,16},{1,33},{17,49},{33,1},{49,17},{2,34}... | collective-permute-start | bytes 294920 | tf_op jit(solution)/shard_map/ppermute | solution.py:49
  16.2 4.7 %collective-permute-start.3 = (bf16[32,1536]{1,0:T(8,128)(2,1)S(1)}, bf16[32,1536]{1,0:T(8,128)(2,1)S(1)}, u32[]{:S(2)}, u32[]{:S(2)}) collective-permute-start(bf16[32,1536]{1,0:T(8,128)(2,1)S(1)} %bitcast.101), channel_id=1, source_target_pairs={{0,48},{16,0},{32,16},{48,32},{1,49},{17,1},{33,17},{49,33},{2,50}... | collective-permute-start | bytes 294920 | tf_op jit(solution)/shard_map/ppermute | solution.py:49
  20.9 11.7 %collective-permute-start.4 = (bf16[128,1536]{1,0:T(8,128)(2,1)S(1)}, bf16[128,1536]{1,0:T(8,128)(2,1)S(1)}, u32[]{:S(2)}, u32[]{:S(2)}) collective-permute-start(bf16[128,1536]{1,0:T(8,128)(2,1)S(1)} %get-tuple-element.39), channel_id=1, source_target_pairs={{0,12},{1,13},{2,14},{3,15},{4,0},{5,1},{6,2},{7,3},{8,4},{9,5},{1... | collective-permute-start | bytes 1179656 | tf_op jit(solution)/shard_map/ppermute | solution.py:63
  23.7 8.9 %collective-permute-start.5 = (bf16[128,1536]{1,0:T(8,128)(2,1)S(1)}, bf16[128,1536]{1,0:T(8,128)(2,1)S(1)}, u32[]{:S(2)}, u32[]{:S(2)}) collective-permute-start(bf16[128,1536]{1,0:T(8,128)(2,1)S(1)} %get-tuple-element.39), channel_id=1, source_target_pairs={{0,8},{1,9},{2,10},{3,11},{4,12},{5,13},{6,14},{7,15},{8,0},{9,1},... | collective-permute-start | bytes 1179656 | tf_op jit(solution)/shard_map/ppermute | solution.py:63
  24.0 12.3 %collective-permute-start.6 = (bf16[128,1536]{1,0:T(8,128)(2,1)S(1)}, bf16[128,1536]{1,0:T(8,128)(2,1)S(1)}, u32[]{:S(2)}, u32[]{:S(2)}) collective-permute-start(bf16[128,1536]{1,0:T(8,128)(2,1)S(1)} %get-tuple-element.39), channel_id=1, source_target_pairs={{0,4},{1,5},{2,6},{3,7},{4,8},{5,9},{6,10},{7,11},{8,12},{9,13},{1... | collective-permute-start | bytes 1179656 | tf_op jit(solution)/shard_map/ppermute | solution.py:63
  36.5 24.2 %copy-start.1 = (bf16[4,128,1536]{2,1,0:T(8,128)(2,1)}, bf16[4,128,1536]{2,1,0:T(8,128)(2,1)S(1)}, u32[]{:S(2)}) copy-start(bf16[4,128,1536]{2,1,0:T(8,128)(2,1)S(1)} %pad_maximum_fusion.own) | copy-start | bytes 4718596
  36.5 19.6 %collective-permute-start.10 = (bf16[4,128,1536]{2,1,0:T(8,128)(2,1)S(1)}, bf16[4,128,1536]{2,1,0:T(8,128)(2,1)S(1)}, u32[]{:S(2)}, u32[]{:S(2)}) collective-permute-start(bf16[4,128,1536]{2,1,0:T(8,128)(2,1)S(1)} %pad_maximum_fusion.own), channel_id=1, source_target_pairs={{0,3},{1,0},{2,1},{3,2},{4,7},{5,4},{6,5},{7,6},{8,11},{9,8},{10,9... | collective-permute-start | bytes 4718600 | tf_op jit(solution)/shard_map/ppermute | solution.py:63
  38.8 20.9 %collective-permute-start.11 = (bf16[4,128,1536]{2,1,0:T(8,128)(2,1)S(1)}, bf16[4,128,1536]{2,1,0:T(8,128)(2,1)S(1)}, u32[]{:S(2)}, u32[]{:S(2)}) collective-permute-start(bf16[4,128,1536]{2,1,0:T(8,128)(2,1)S(1)} %pad_maximum_fusion.own), channel_id=1, source_target_pairs={{0,1},{1,2},{2,3},{3,0},{4,5},{5,6},{6,7},{7,4},{8,9},{9,10},{10,1... | collective-permute-start | bytes 4718600 | tf_op jit(solution)/shard_map/ppermute | solution.py:63
  56.1 4.5 %copy-start.4 = (bf16[4,128,1536]{2,1,0:T(8,128)(2,1)}, bf16[4,128,1536]{2,1,0:T(8,128)(2,1)S(1)}, u32[]{:S(2)}) copy-start(bf16[4,128,1536]{2,1,0:T(8,128)(2,1)S(1)} %collective-permute-done.10.above) | copy-start | bytes 4718596
  56.2 18.9 %collective-permute-start.12 = (bf16[2,128,1536]{2,1,0:T(8,128)(2,1)S(1)}, bf16[2,128,1536]{2,1,0:T(8,128)(2,1)}, u32[]{:S(2)}, u32[]{:S(2)}) collective-permute-start(bf16[2,128,1536]{2,1,0:T(8,128)(2,1)S(1)} %slice.117), channel_id=1, source_target_pairs={{0,3},{1,0},{2,1},{3,2},{4,7},{5,4},{6,5},{7,6},{8,11},{9,8},{10,9... | collective-permute-start | bytes 2359304 | tf_op jit(solution)/shard_map/ppermute | solution.py:63
  60.7 14.4 %collective-permute-start.13 = (bf16[2,128,1536]{2,1,0:T(8,128)(2,1)}, bf16[2,128,1536]{2,1,0:T(8,128)(2,1)}, u32[]{:S(2)}, u32[]{:S(2)}) collective-permute-start(bf16[2,128,1536]{2,1,0:T(8,128)(2,1)} %slice.118), channel_id=1, source_target_pairs={{0,1},{1,2},{2,3},{3,0},{4,5},{5,6},{6,7},{7,4},{8,9},{9,10},{10,1... | collective-permute-start | bytes 2359304 | tf_op jit(solution)/shard_map/ppermute | solution.py:63
  61.1 2.9 %collective-permute-start.7 = (bf16[1536]{0:T(1024)(128)(2,1)S(1)}, bf16[1536]{0:T(1024)(128)(2,1)S(1)}, u32[]{:S(2)}, u32[]{:S(2)}) collective-permute-start(bf16[1536]{0:T(1024)(128)(2,1)S(1)} %copy-done.8), channel_id=1, source_target_pairs={{0,3},{1,0},{2,1},{3,2},{4,7},{5,4},{6,5},{7,6},{8,11},{9,8},{10,9... | collective-permute-start | bytes 9224 | tf_op jit(solution)/shard_map/ppermute | solution.py:49
  61.7 4.0 %collective-permute-start.8 = (bf16[1536]{0:T(1024)(128)(2,1)S(1)}, bf16[1536]{0:T(1024)(128)(2,1)S(1)}, u32[]{:S(2)}, u32[]{:S(2)}) collective-permute-start(bf16[1536]{0:T(1024)(128)(2,1)S(1)} %copy-done.8), channel_id=1, source_target_pairs={{0,2},{1,3},{2,0},{3,1},{4,6},{5,7},{6,4},{7,5},{8,10},{9,11},{10,... | collective-permute-start | bytes 9224 | tf_op jit(solution)/shard_map/ppermute | solution.py:49
  61.8 4.2 %collective-permute-start.9 = (bf16[1536]{0:T(1024)(128)(2,1)S(1)}, bf16[1536]{0:T(1024)(128)(2,1)S(1)}, u32[]{:S(2)}, u32[]{:S(2)}) collective-permute-start(bf16[1536]{0:T(1024)(128)(2,1)S(1)} %copy-done.8), channel_id=1, source_target_pairs={{0,1},{1,2},{2,3},{3,0},{4,5},{5,6},{6,7},{7,4},{8,9},{9,10},{10,1... | collective-permute-start | bytes 9224 | tf_op jit(solution)/shard_map/ppermute | solution.py:49
  95.0 4.1 %copy-start.2 = (bf16[4,128,1536]{2,1,0:T(8,128)(2,1)S(1)}, bf16[4,128,1536]{2,1,0:T(8,128)(2,1)}, u32[]{:S(2)}) copy-start(bf16[4,128,1536]{2,1,0:T(8,128)(2,1)} %get-tuple-element.21) | copy-start | bytes 4718596
  95.0 12.1 %collective-permute-start.14 = (bf16[2,128,1536]{2,1,0:T(8,128)(2,1)S(1)}, bf16[2,128,1536]{2,1,0:T(8,128)(2,1)S(1)}, u32[]{:S(2)}, u32[]{:S(2)}) collective-permute-start(bf16[2,128,1536]{2,1,0:T(8,128)(2,1)S(1)} %get-tuple-element.20), channel_id=1, source_target_pairs={{0,1},{1,2},{2,3},{3,0},{4,5},{5,6},{6,7},{7,4},{8,9},{9,10},{10,1... | collective-permute-start | bytes 2359304 | tf_op jit(solution)/shard_map/ppermute | solution.py:63
  95.1 12.0 %copy-start.3 = (bf16[4,128,1536]{2,1,0:T(8,128)(2,1)S(1)}, bf16[4,128,1536]{2,1,0:T(8,128)(2,1)}, u32[]{:S(2)}) copy-start(bf16[4,128,1536]{2,1,0:T(8,128)(2,1)} %get-tuple-element.19) | copy-start | bytes 4718596
  96.4 12.2 %collective-permute-start.16 = (bf16[2,128,1536]{2,1,0:T(8,128)(2,1)S(1)}, bf16[2,128,1536]{2,1,0:T(8,128)(2,1)S(1)}, u32[]{:S(2)}, u32[]{:S(2)}) collective-permute-start(bf16[2,128,1536]{2,1,0:T(8,128)(2,1)S(1)} %get-tuple-element.22), channel_id=1, source_target_pairs={{0,3},{1,0},{2,1},{3,2},{4,7},{5,4},{6,5},{7,6},{8,11},{9,8},{10,9... | collective-permute-start | bytes 2359304 | tf_op jit(solution)/shard_map/ppermute | solution.py:63
  108.6 21.1 %collective-permute-start.15 = (bf16[4,128,1536]{2,1,0:T(8,128)(2,1)}, bf16[4,128,1536]{2,1,0:T(8,128)(2,1)}, u32[]{:S(2)}, u32[]{:S(2)}) collective-permute-start(bf16[4,128,1536]{2,1,0:T(8,128)(2,1)} %pad_maximum_fusion.1), channel_id=1, source_target_pairs={{0,1},{1,2},{2,3},{3,0},{4,5},{5,6},{6,7},{7,4},{8,9},{9,10},{10,1... | collective-permute-start | bytes 4718600 | tf_op jit(solution)/shard_map/ppermute | solution.py:63
  110.1 20.5 %collective-permute-start.17 = (bf16[4,128,1536]{2,1,0:T(8,128)(2,1)}, bf16[4,128,1536]{2,1,0:T(8,128)(2,1)}, u32[]{:S(2)}, u32[]{:S(2)}) collective-permute-start(bf16[4,128,1536]{2,1,0:T(8,128)(2,1)} %pad_maximum_fusion.2), channel_id=1, source_target_pairs={{0,3},{1,0},{2,1},{3,2},{4,7},{5,4},{6,5},{7,6},{8,11},{9,8},{10,9... | collective-permute-start | bytes 4718600 | tf_op jit(solution)/shard_map/ppermute | solution.py:63
  136.3 14.8 %collective-permute-start.18 = (bf16[128,1536]{1,0:T(8,128)(2,1)}, bf16[128,1536]{1,0:T(8,128)(2,1)S(1)}, u32[]{:S(2)}, u32[]{:S(2)}) collective-permute-start(bf16[128,1536]{1,0:T(8,128)(2,1)} %get-tuple-element.29), channel_id=1, source_target_pairs={{0,4},{1,5},{2,6},{3,7},{4,8},{5,9},{6,10},{7,11},{8,12},{9,13},{1... | collective-permute-start | bytes 1179656 | tf_op jit(solution)/shard_map/ppermute | solution.py:63
  136.3 14.8 %collective-permute-start.19 = (bf16[128,1536]{1,0:T(8,128)(2,1)}, bf16[128,1536]{1,0:T(8,128)(2,1)S(1)}, u32[]{:S(2)}, u32[]{:S(2)}) collective-permute-start(bf16[128,1536]{1,0:T(8,128)(2,1)} %get-tuple-element.31), channel_id=1, source_target_pairs={{0,8},{1,9},{2,10},{3,11},{4,12},{5,13},{6,14},{7,15},{8,0},{9,1},... | collective-permute-start | bytes 1179656 | tf_op jit(solution)/shard_map/ppermute | solution.py:63
  136.9 15.4 %collective-permute-start.20 = (bf16[128,1536]{1,0:T(8,128)(2,1)S(1)}, bf16[128,1536]{1,0:T(8,128)(2,1)}, u32[]{:S(2)}, u32[]{:S(2)}) collective-permute-start(bf16[128,1536]{1,0:T(8,128)(2,1)S(1)} %get-tuple-element.30), channel_id=1, source_target_pairs={{0,12},{1,13},{2,14},{3,15},{4,0},{5,1},{6,2},{7,3},{8,4},{9,5},{1... | collective-permute-start | bytes 1179656 | tf_op jit(solution)/shard_map/ppermute | solution.py:63
  153.7 4.6 %collective-permute-start.21 = (bf16[2,16,1536]{2,1,0:T(8,128)(2,1)S(1)}, bf16[2,16,1536]{2,1,0:T(8,128)(2,1)S(1)}, u32[]{:S(2)}, u32[]{:S(2)}) collective-permute-start(bf16[2,16,1536]{2,1,0:T(8,128)(2,1)S(1)} %bitcast.105), channel_id=1, source_target_pairs={{0,48},{16,0},{32,16},{48,32},{1,49},{17,1},{33,17},{49,33},{2,50}... | collective-permute-start | bytes 294920 | tf_op jit(solution)/shard_map/ppermute | solution.py:49
  155.7 5.0 %collective-permute-start.22 = (bf16[2,16,1536]{2,1,0:T(8,128)(2,1)S(1)}, bf16[2,16,1536]{2,1,0:T(8,128)(2,1)S(1)}, u32[]{:S(2)}, u32[]{:S(2)}) collective-permute-start(bf16[2,16,1536]{2,1,0:T(8,128)(2,1)S(1)} %bitcast.102), channel_id=1, source_target_pairs={{0,32},{16,48},{32,0},{48,16},{1,33},{17,49},{33,1},{49,17},{2,34}... | collective-permute-start | bytes 294920 | tf_op jit(solution)/shard_map/ppermute | solution.py:49
  156.7 5.1 %collective-permute-start.23 = (bf16[2,16,1536]{2,1,0:T(8,128)(2,1)S(1)}, bf16[2,16,1536]{2,1,0:T(8,128)(2,1)S(1)}, u32[]{:S(2)}, u32[]{:S(2)}) collective-permute-start(bf16[2,16,1536]{2,1,0:T(8,128)(2,1)S(1)} %bitcast.99), channel_id=1, source_target_pairs={{0,16},{16,32},{32,48},{48,0},{1,17},{17,33},{33,49},{49,1},{2,18}... | collective-permute-start | bytes 294920 | tf_op jit(solution)/shard_map/ppermute | solution.py:49
  161.8 23.2 %collective-permute-start.24 = (bf16[4,16,1536]{2,1,0:T(8,128)(2,1)S(1)}, bf16[4,16,1536]{2,1,0:T(8,128)(2,1)S(1)}, u32[]{:S(2)}, u32[]{:S(2)}) collective-permute-start(bf16[4,16,1536]{2,1,0:T(8,128)(2,1)S(1)} %get-tuple-element.33), channel_id=1, source_target_pairs={{0,64},{64,0},{1,65},{65,1},{2,66},{66,2},{3,67},{67,3},{4,68},{68... | collective-permute-start | bytes 589832 | tf_op jit(solution)/shard_map/ppermute | solution.py:53
  (4 other events, 8.4 us)

commit v2 on v1

v2 whole, which is shorter than its diff:
```python
import functools

import jax
import jax.numpy as jnp
from jax import lax
from jax.experimental import pallas as pl
from jax.experimental.pallas import tpu as pltpu
from jax.sharding import Mesh
from jax.sharding import PartitionSpec as P

HD = 128
TOP = 2
CAP = 16
RING = 4
GROUPS = 1
bf16 = jnp.bfloat16
f32 = jnp.float32


def attend(queries, key_cache, value_cache, key_new, value_new, lengths):
    rows = queries.shape[0]
    heads_kv = key_new.shape[1] // HD
    repeat = queries.shape[1] // HD // heads_kv
    length = key_cache.shape[1]
    scale = 1.0 / HD**0.5
    qhead = queries.reshape(rows, heads_kv, repeat, HD)
    kcache = key_cache.reshape(rows, length, heads_kv, HD)
    vcache = value_cache.reshape(rows, length, heads_kv, HD)
    knew = key_new.reshape(rows, heads_kv, HD)
    vnew = value_new.reshape(rows, heads_kv, 1, HD).astype(f32)
    scores = jnp.einsum("rgho,rcgo->rghc", qhead, kcache, preferred_element_type=f32) * scale
    own = jnp.einsum("rgho,rgo->rgh", qhead, knew, preferred_element_type=f32) * scale
    valid = jnp.arange(length, dtype=jnp.int32)[None, :] < lengths[:, None]
    scores = jnp.where(valid[:, None, None, :], scores, -1e30)
    top = jnp.maximum(jnp.max(scores, -1), own)
    probs = jnp.exp(scores - top[..., None])
    pown = jnp.exp(own - top)
    total = jnp.sum(probs, -1) + pown
    weights = (probs / total[..., None]).astype(bf16)
    wown = (pown / total).astype(bf16).astype(f32)
    result = (
        jnp.einsum("rghc,rcgo->rgho", weights, vcache, preferred_element_type=f32)
        + wown[..., None] * vnew
    )
    return result.reshape(rows, repeat * heads_kv * HD)


def along(x, axis, by):
    return lax.ppermute(x, axis, [(i, (i + by) % RING) for i in range(RING)])


def swap_cores(x):
    return lax.ppermute(x, "pool", [(0, 1), (1, 0)])


def cross(x, leg, by):
    pairs = []
    for core in range(2):
        for i in range(RING):
            for j in range(RING):
                to = ((i + by) % RING, j) if core == leg else (i, (j + by) % RING)
                pairs.append((core * 16 + i * RING + j, core * 16 + to[0] * RING + to[1]))
    return lax.ppermute(x, ("pool", "x", "tp"), pairs)


ORDER = (0, 1, 3, 2)


def turned(me, quarter, features):
    return pl.ds(pl.multiple_of(lax.rem(me + quarter, RING) * features, features), features)


def pieces_of(flipped, arrived):
    if flipped:
        rows = [p for p in range(RING) if ORDER[p] in arrived]
        return [(q, [(p, arrived[ORDER[p]][q // 2].at[q % 2]) for p in rows]) for q in range(RING)]
    quarters = [q for q in ORDER if q in arrived]
    return [(q, [(p, arrived[q][ORDER[p] // 2].at[ORDER[p] % 2]) for p in range(RING)]) for q in quarters]


def bring_kernel(place, w_gate, w_up, w_down, gate_in, up_in, down_in, sem):
    pairs = ((w_gate, gate_in), (w_up, up_in), (w_down, down_in))
    copies = [pltpu.make_async_copy(source, target, sem.at[i]) for i, (source, target) in enumerate(pairs)]
    for copy in copies:
        copy.start()
    for copy in copies:
        copy.wait()


def early_kernel(
    place, own_0, own_1, above_0, above_1, below_0, below_1, w_gate, w_up, gate, upper, rows, sem
):
    core, me = place[0], place[1]
    _, _, block, features = rows.shape
    arrived = {0: (own_0, own_1), 1: (above_0, above_1), 3: (below_0, below_1)}
    gate[...] = jnp.zeros_like(gate)
    upper[...] = jnp.zeros_like(upper)

    for flipped in range(2):
        @pl.when(core == flipped)
        def _():
            work = pieces_of(flipped, arrived)
            for quarter, blocks in work:
                for p, source in blocks:
                    pltpu.make_async_copy(source, rows.at[quarter, p], sem.at[quarter, p]).start()
            for quarter, blocks in work:
                number = len(blocks)
                for p, source in blocks:
                    pltpu.make_async_copy(source, rows.at[quarter, p], sem.at[quarter, p]).wait()
                some = pl.ds(0, number * block)
                held = rows[quarter, :number].reshape(number * block, features)
                cut = turned(me, quarter, features)
                gate[some, :] += jnp.dot(held, w_gate[cut, :], preferred_element_type=f32)
                upper[some, :] += jnp.dot(held, w_up[cut, :], preferred_element_type=f32)


def late_kernel(place, far_0, far_1, gate_in, up_in, w_gate, w_up, w_down, act, out_0, out_1, rows, gate, upper, sem):
    core, me = place[0], place[1]
    _, block, features = rows.shape
    count = RING * block
    halves, outs = (far_0, far_1), (out_0, out_1)
    last = pl.ds((RING - 1) * block, block)

    for flipped in range(2):
        @pl.when(core == flipped)
        def _():
            for p in range(RING):
                inner = p if flipped else ORDER[p]
                pltpu.make_async_copy(halves[inner // 2].at[inner % 2], rows.at[p], sem.at[p]).start()

    gate[...] = gate_in[...]
    upper[...] = up_in[...]
    for p in range(RING):
        pltpu.make_async_copy(far_0.at[0], rows.at[p], sem.at[p]).wait()

    @pl.when(core == 0)
    def _():
        held = rows[...].reshape(count, features)
        gate[...] += jnp.dot(held, w_gate[turned(me, 2, features), :], preferred_element_type=f32)
        upper[...] += jnp.dot(held, w_up[turned(me, 2, features), :], preferred_element_type=f32)

    @pl.when(core == 1)
    def _():
        @pl.loop(0, RING)
        def _(quarter):
            gate[last, :] += jnp.dot(rows[quarter], w_gate[turned(me, quarter, features), :], preferred_element_type=f32)
            upper[last, :] += jnp.dot(rows[quarter], w_up[turned(me, quarter, features), :], preferred_element_type=f32)

    held = gate[...]
    act[...] = (held * jax.nn.sigmoid(held) * upper[...]).astype(bf16)

    @pl.when(core == 0)
    def _():
        outcome = jnp.dot(act[...], w_down[:, turned(me, 2, features)], preferred_element_type=f32).astype(bf16)
        for p in range(RING):
            outs[ORDER[p] // 2][ORDER[p] % 2] = outcome[p * block : (p + 1) * block]

    @pl.when(core == 1)
    def _():
        for quarter in range(RING):
            outs[quarter // 2][quarter % 2] = jnp.dot(
                act[last, :], w_down[:, turned(me, quarter, features)], preferred_element_type=f32
            ).astype(bf16)


def rest_kernel(place, act, w_down, own_0, own_1, above_0, above_1, below_0, below_1, rows, sem):
    core, me = place[0], place[1]
    _, _, block, features = rows.shape
    halves = {0: (own_0, own_1), 1: (above_0, above_1), 3: (below_0, below_1)}

    def step(quarter, blocks):
        outcome = jnp.dot(
            act[: blocks * block, :], w_down[:, turned(me, quarter, features)], preferred_element_type=f32
        )
        rows[quarter, :blocks] = outcome.astype(bf16).reshape(blocks, block, features)
        for p in range(blocks):
            if blocks < RING:
                target = halves[ORDER[p]][quarter // 2].at[quarter % 2]
            else:
                target = halves[quarter][ORDER[p] // 2].at[ORDER[p] % 2]
            pltpu.make_async_copy(rows.at[quarter, p], target, sem.at[quarter, p]).start()

    for flipped in range(2):
        @pl.when(core == flipped)
        def _():
            quarters, blocks = (range(RING), RING - 1) if flipped else ((1, 3, 0), RING)
            for quarter in quarters:
                step(quarter, blocks)
            for quarter in quarters:
                for p in range(blocks):
                    pltpu.make_async_copy(rows.at[quarter, p], own_0.at[0], sem.at[quarter, p]).wait()


ANYWHERE = pl.BlockSpec(memory_space=pl.ANY)
SCALARS = pl.BlockSpec(memory_space=pltpu.SMEM)
INSIDE = pl.BlockSpec(memory_space=pltpu.VMEM)
MIB = 1024 * 1024


def cost(macs, moved, raised=0):
    return pl.CostEstimate(flops=2 * macs, bytes_accessed=moved, transcendentals=raised)


def bring(place, w_gate, w_up, w_down):
    weights = [pltpu.with_memory_space_constraint(w, pltpu.HBM) for w in (w_gate, w_up, w_down)]
    return pl.pallas_call(
        bring_kernel,
        out_shape=[pltpu.VMEM(w.shape, bf16) for w in weights],
        in_specs=[SCALARS] + [pl.BlockSpec(memory_space=pltpu.HBM)] * 3,
        out_specs=[INSIDE] * 3,
        scratch_shapes=[pltpu.SemaphoreType.DMA((3,))],
        compiler_params=pltpu.CompilerParams(vmem_limit_bytes=MIB),
        cost_estimate=cost(0, 3 * w_gate.size * 2),
        name="bring",
    )(place, *weights)


def early(place, pieces, w_gate, w_up):
    _, block, features = pieces[0].shape
    units = w_gate.shape[1]
    count = RING * block
    return pl.pallas_call(
        early_kernel,
        out_shape=[jax.ShapeDtypeStruct((count, units), f32)] * 2,
        in_specs=[SCALARS] + [ANYWHERE] * 6 + [INSIDE] * 2,
        out_specs=[INSIDE] * 2,
        scratch_shapes=[
            pltpu.VMEM((RING, RING, block, features), bf16),
            pltpu.SemaphoreType.DMA((RING, RING)),
        ],
        compiler_params=pltpu.CompilerParams(vmem_limit_bytes=16 * MIB),
        cost_estimate=cost(3 * count * features * units * 2, 3 * count * features * 2),
        name="early",
    )(place, *pieces, w_gate, w_up)


def late(place, far, gate, upper, w_gate, w_up, w_down):
    _, block, features = far[0].shape
    units = w_gate.shape[1]
    count = RING * block
    half = jax.ShapeDtypeStruct(far[0].shape, bf16)
    return pl.pallas_call(
        late_kernel,
        out_shape=[jax.ShapeDtypeStruct((count, units), bf16), half, half],
        in_specs=[SCALARS] + [ANYWHERE] * 2 + [INSIDE] * 5,
        out_specs=[INSIDE] * 3,
        scratch_shapes=[
            pltpu.VMEM((RING, block, features), bf16),
            pltpu.VMEM((count, units), f32),
            pltpu.VMEM((count, units), f32),
            pltpu.SemaphoreType.DMA((RING,)),
        ],
        compiler_params=pltpu.CompilerParams(vmem_limit_bytes=16 * MIB),
        cost_estimate=cost(count * features * units * 3, 2 * count * features * 2, count * units),
        name="late",
    )(place, *far, gate, upper, w_gate, w_up, w_down)


def rest(place, act, w_down, shape):
    _, block, features = shape
    return pl.pallas_call(
        rest_kernel,
        out_shape=[jax.ShapeDtypeStruct(shape, bf16)] * 6,
        in_specs=[SCALARS] + [INSIDE] * 2,
        out_specs=[ANYWHERE] * 6,
        scratch_shapes=[
            pltpu.VMEM((RING, RING, block, features), bf16),
            pltpu.SemaphoreType.DMA((RING, RING)),
        ],
        compiler_params=pltpu.CompilerParams(vmem_limit_bytes=16 * MIB),
        cost_estimate=cost(3 * act.size * features, 3 * RING * block * features * 2),
        name="rest",
    )(place, act, w_down)


def shards(
    queries, key_cache, value_cache, key_new, value_new, lengths, residual,
    norm_gain, w_router, expert_ids, w_gate, w_up, w_down,
):
    rows, features = residual.shape
    experts = w_router.shape[1]
    me_pool, me_z, me_y = lax.axis_index("pool"), lax.axis_index("z"), lax.axis_index("tp")
    place = jnp.stack([me_pool, me_y]).astype(jnp.int32)

    attn = attend(queries, key_cache, value_cache, key_new, value_new, lengths)
    hidden_state = (residual.astype(f32) + attn).astype(bf16)
    hfloat = hidden_state.astype(f32)
    raised = hfloat * norm_gain.astype(f32)[None, :]
    stats = jnp.concatenate(
        [
            jnp.dot(raised.astype(bf16), w_router, preferred_element_type=f32),
            jnp.sum(hfloat * hfloat, -1, keepdims=True),
        ],
        1,
    )
    stats = stats + along(stats, "tp", 1) + along(stats, "tp", 2) + along(stats, "tp", 3)
    scale = lax.rsqrt(stats[:, experts:] / (features * RING) + 1e-05)
    normed = (raised * scale).astype(bf16)

    near = ((expert_ids // RING + me_pool) % 2) * RING + (expert_ids % RING - me_z + RING) % RING
    flat = near.reshape(-1)
    expert_hot = (flat[:, None] == jnp.arange(experts, dtype=jnp.int32)[None, :]).astype(jnp.int32)
    earlier = jnp.cumsum(expert_hot, 0) - expert_hot
    slot = jnp.sum(earlier * expert_hot, 1)
    size = CAP // GROUPS
    position = (((slot // size) * experts + flat) * size + slot % size).reshape(rows, TOP)
    places = jnp.arange(experts * CAP, dtype=jnp.int32)
    hot = position[:, :, None] == places[None, None, :]
    dispatch = jnp.any(hot, 1).T.astype(bf16)
    bucket = jnp.dot(dispatch, normed, preferred_element_type=f32).astype(bf16)
    buckets = bucket.reshape(GROUPS, 2, RING, size, features)

    returned = []
    for group in range(GROUPS):
        partner = swap_cores(buckets[group, 1])
        pairs = jnp.stack([buckets[group, 0], partner], 1).reshape(RING, 2 * size, features)
        block = jnp.concatenate([pairs[0]] + [along(pairs[d], "z", d) for d in range(1, RING)])
        near_block, last_block = cross(block, 0, -1), cross(block, 0, 1)
        if group == 0:
            place, block = lax.optimization_barrier((place, block))
            weights = bring(place, w_gate, w_up, w_down)
            near_block, weights = lax.optimization_barrier((near_block, weights))
            gate_in, up_in, down_in = weights
        near_block, kept = lax.optimization_barrier((near_block, block))
        far_block = cross(kept, 0, 2)
        own = [jnp.stack([block, near_block]), jnp.stack([far_block, last_block])]
        above, below = [None, None], [None, None]
        for half in range(2):
            above[half] = cross(own[half], 1, -1)
            below[half] = cross(own[half], 1, 1)
        below = lax.optimization_barrier(below)
        far = [cross(above[0], 1, -1), cross(below[1], 1, 1)]
        gate, upper = early(place, own + above + below, gate_in, up_in)
        act, far_0, far_1 = late(place, far, gate, upper, gate_in, up_in, down_in)
        relay_0, relay_1 = cross(far_0, 1, 1), cross(far_1, 1, -1)
        own_0, own_1, above_0, above_1, below_0, below_1 = rest(place, act, down_in, far_0.shape)
        up_1 = cross(above_1, 1, 1)
        down_0 = cross(below_0, 1, -1)
        up_0 = cross((above_0.astype(f32) + relay_0.astype(f32)).astype(bf16), 1, 1)
        down_1 = cross((below_1.astype(f32) + relay_1.astype(f32)).astype(bf16), 1, -1)
        terms = ((own_0, up_0, down_0), (own_1, up_1, down_1))
        def mine(d):
            return sum(t[d % 2].astype(f32) for t in terms[d // 2])

        parts = [cross(mine(d).astype(bf16), 0, d) for d in (1, 2, 3)]
        terms, parts = lax.optimization_barrier((terms, parts))
        total = mine(0) + sum(p.astype(f32) for p in parts)
        back = total.astype(bf16).reshape(RING, 2, size, features)
        home = jnp.stack([back[0]] + [along(back[d], "z", -d) for d in range(1, RING)])
        returned.append(jnp.stack([home[:, 0], swap_cores(home[:, 1])]))

    logits = stats[:, :experts] * scale
    chosen = jnp.take_along_axis(logits, expert_ids, 1)
    gates = jax.nn.softmax(chosen, -1)
    combine = jnp.sum(jnp.where(hot, gates[:, :, None], 0.0), 1)
    results = jnp.stack(returned).reshape(experts * CAP, features)
    mixed = jnp.dot(combine, results.astype(f32), precision=lax.Precision.HIGHEST)
    return (hfloat + mixed).astype(bf16)


def solution(mesh):
    split = Mesh(mesh.devices.reshape(2, RING, RING, RING), ("pool", "z", "x", "tp"))
    rows = ("pool", "z", "x")
    every = ("pool", "z", "x", "tp")
    placed = (
        P(rows, "tp"),
        P(rows, None, "tp"),
        P(rows, None, "tp"),
        P(rows, "tp"),
        P(rows, "tp"),
        P(rows),
        P(rows, "tp"),
        P("tp"),
        P("tp", None),
        P(rows, None),
        P(None, every),
        P(None, every),
        P(every, None),
    )
    return jax.shard_map(
        shards, mesh=split, in_specs=placed, out_specs=P(rows, "tp"), check_vma=False
    )
```

time: 186 us -> 143 us (0.77)
  waiting for transfers between devices: 80.9 us -> 53.1 us
  blocking collectives: 9.07 us -> 0 us
  starting transfers between devices: 51.7 us -> 44.4 us
  Pallas kernels: 19.8 us -> 26.7 us
  local copies, waits for them, and re-layouts: 7.42 us -> 3.57 us
  other arithmetic: 11.5 us -> 9.25 us
    ppermute x14 -> x18, waiting for transfers between devices: 66.6 us -> 41.5 us  [cross(): return lax.ppermute(x, ('pool', 'x', 'tp'), pairs)]
    ppermute x2, starting transfers between devices: 23.7 us -> 8.61 us  [swap_cores(): return lax.ppermute(x, 'pool', [(0, 1), (1, 0)])]
    psum x1 -> x0, blocking collectives: 9.07 us -> none  [shards(): stats = lax.psum(stats, 'tp')]
    pallas_call x1 -> x4, Pallas kernels: 19.8 us -> 26.7 us  [the longest x1 8.44 us: early(): pl.pallas_call(early_kernel, out_shape=[jax.ShapeDtypeStruct((count, unit...]
    ppermute x9, starting transfers between devices: 10.2 us -> 14.7 us  [along(): return lax.ppermute(x, axis, [(i, (i + by) % RING) for i in range(RING)])]
    ppermute x14 -> x18, starting transfers between devices: 17.9 us -> 21.1 us  [cross(): return lax.ppermute(x, ('pool', 'x', 'tp'), pairs)]
    ppermute x9, waiting for transfers between devices: 12.3 us -> 9.49 us  [along(): return lax.ppermute(x, axis, [(i, (i + by) % RING) for i in range(RING)])]
    concatenate x3 -> x2, other arithmetic: 2.59 us -> 0.04 us  [the longest x1 0.03 us: shards(): jnp.concatenate([pairs[0]] + [along(pairs[d], 'z', d) for d in range(1, R...]
  transfers between devices with their start and end apart: 25 -> 29, of which waited for: 18 -> 18; matrix products, arithmetic and copies ran while one was open for 4% -> 5% of each run, Pallas kernels for 0% -> 15%
where the time goes in v2:
time: 143 us
  waiting for transfers between devices  53.1 us (37%)
  starting transfers between devices  44.4 us (31%)
  Pallas kernels  26.7 us (19%)
  other arithmetic  9.25 us (6%)
  matrix products  5.24 us (4%)
  local copies, waits for them, and re-layouts  3.57 us (2%)
    ppermute x18, waiting for transfers between devices, cross(): return lax.ppermute(x, ('pool', 'x', 'tp'), pairs)  41.5 us
    ppermute x18, starting transfers between devices, cross(): return lax.ppermute(x, ('pool', 'x', 'tp'), pairs)  21.1 us
    ppermute x9, starting transfers between devices, along(): return lax.ppermute(x, axis, [(i, (i + by) % RING) for i in range(RING)])  14.7 us
    ppermute x9, waiting for transfers between devices, along(): return lax.ppermute(x, axis, [(i, (i + by) % RING) for i in range(RING)])  9.49 us
    ppermute x2, starting transfers between devices, swap_cores(): return lax.ppermute(x, 'pool', [(0, 1), (1, 0)])  8.61 us
    pallas_call x1, Pallas kernels, early(): pl.pallas_call(early_kernel, out_shape=[jax.ShapeDtypeStruct((count, unit...  8.44 us
    pallas_call x1, Pallas kernels, bring(): pl.pallas_call(bring_kernel, out_shape=[pltpu.VMEM(w.shape, bf16) for w i...  6.96 us
    pallas_call x1, Pallas kernels, rest(): pl.pallas_call(rest_kernel, out_shape=[jax.ShapeDtypeStruct(shape, bf16)]...  6.25 us
  transfers between devices with their start and end apart: 29, of which 18 were waited for; matrix products, arithmetic and copies ran while one was open for 5% of the time, Pallas kernels for 15%

profile of v2, /device:TPU:1, one launch (start us, length us, event | category | flops | bytes accessed | tf_op | source)
XLA Modules:
  0.0 142.5 jit_solution(6483583732798076806)
XLA Ops:
  4.6 2.4 %fusion.13 = f32[32,2,6,128]{3,2,1,0:T(8,128)S(1)} fusion(f32[32,2,6,128]{3,2,1,0:T(8,128)S(1)} %get-tuple-element.86, f32[32,2,128]{2,1,0:T(2,128)S(1)} %reshape.167, f32[32,2,6]{2,1,0:T(2,128)S(1)} %get-tuple-element.84, f32[32,2,6]{2,1,0:T(2,128)S(1)} %get-tuple-element.83, f32[32,2,6]{2,1,0:T(2,128)S(1)} %multiply_maximum_fusion, ...), kind=kOutput, calls=%fused_computation.14 | convolution fusion | flops 12828672 | bytes 2527744 | tf_op jit(solution)/shard_map/rghc,rcgo->rgho/dot_general | solution.py:42
  7.4 2.1 %collective-permute-start = (f32[32,9]{0,1:T(8,128)S(1)}, f32[32,9]{0,1:T(8,128)S(1)}, u32[]{:S(2)}, u32[]{:S(2)}) collective-permute-start(f32[32,9]{0,1:T(8,128)S(1)} %pad_maximum_fusion.6), channel_id=1, source_target_pairs={{0,1},{1,2},{2,3},{3,0},{4,5},{5,6},{6,7},{7,4},{8,9},{9,10},{10,1... | collective-permute-start | bytes 3464 | tf_op jit(solution)/shard_map/ppermute | solution.py:49
  9.5 2.6 %collective-permute-start.1 = (f32[32,9]{0,1:T(8,128)S(1)}, f32[32,9]{0,1:T(8,128)S(1)}, u32[]{:S(2)}, u32[]{:S(2)}) collective-permute-start(f32[32,9]{0,1:T(8,128)S(1)} %pad_maximum_fusion.6), channel_id=1, source_target_pairs={{0,2},{1,3},{2,0},{3,1},{4,6},{5,7},{6,4},{7,5},{8,10},{9,11},{10,... | collective-permute-start | bytes 3464 | tf_op jit(solution)/shard_map/ppermute | solution.py:49
  15.3 2.2 %collective-permute-start.3 = (bf16[4,16,1536]{2,1,0:T(8,128)(2,1)S(1)}, bf16[4,16,1536]{2,1,0:T(8,128)(2,1)S(1)}, u32[]{:S(2)}, u32[]{:S(2)}) collective-permute-start(bf16[4,16,1536]{2,1,0:T(8,128)(2,1)S(1)} %get-tuple-element.82), channel_id=1, source_target_pairs={{0,64},{64,0},{1,65},{65,1},{2,66},{66,2},{3,67},{67,3},{4,68},{68... | collective-permute-start | bytes 589832 | tf_op jit(solution)/shard_map/ppermute | solution.py:53
  18.6 1.7 %collective-permute-start.4 = (bf16[32,1536]{1,0:T(8,128)(2,1)S(1)}, bf16[32,1536]{1,0:T(8,128)(2,1)S(1)}, u32[]{:S(2)}, u32[]{:S(2)}) collective-permute-start(bf16[32,1536]{1,0:T(8,128)(2,1)S(1)} %bitcast.101), channel_id=1, source_target_pairs={{0,16},{16,32},{32,48},{48,0},{1,17},{17,33},{33,49},{49,1},{2,18}... | collective-permute-start | bytes 294920 | tf_op jit(solution)/shard_map/ppermute | solution.py:49
  20.3 3.3 %collective-permute-start.5 = (bf16[32,1536]{1,0:T(8,128)(2,1)S(1)}, bf16[32,1536]{1,0:T(8,128)(2,1)S(1)}, u32[]{:S(2)}, u32[]{:S(2)}) collective-permute-start(bf16[32,1536]{1,0:T(8,128)(2,1)S(1)} %bitcast.98), channel_id=1, source_target_pairs={{0,32},{16,48},{32,0},{48,16},{1,33},{17,49},{33,1},{49,17},{2,34}... | collective-permute-start | bytes 294920 | tf_op jit(solution)/shard_map/ppermute | solution.py:49
  25.3 3.0 %collective-permute-done.5 = bf16[32,1536]{1,0:T(8,128)(2,1)S(1)} collective-permute-done((bf16[32,1536]{1,0:T(8,128)(2,1)S(1)}, bf16[32,1536]{1,0:T(8,128)(2,1)S(1)}, u32[]{:S(2)}, u32[]{:S(2)}) %collective-permute-start.5) | collective-permute-done | bytes 98336 | tf_op jit(solution)/shard_map/ppermute | solution.py:49
  28.3 2.3 %collective-permute-start.7 = (bf16[128,1536]{1,0:T(8,128)(2,1)S(1)}, bf16[128,1536]{1,0:T(8,128)(2,1)S(1)}, u32[]{:S(2)}, u32[]{:S(2)}) collective-permute-start(bf16[128,1536]{1,0:T(8,128)(2,1)S(1)} %pad_maximum_fusion.2), channel_id=1, source_target_pairs={{0,12},{1,13},{2,14},{3,15},{4,0},{5,1},{6,2},{7,3},{8,4},{9,5},{1... | collective-permute-start | bytes 1179656 | tf_op jit(solution)/shard_map/ppermute | solution.py:63
  30.7 7.0 %bring.1 = (bf16[6144,512]{1,0:T(8,128)(2,1)S(1)}, bf16[6144,512]{1,0:T(8,128)(2,1)S(1)}, bf16[512,6144]{1,0:T(8,128)(2,1)S(1)}) custom-call(s32[2]{0:T(128)S(1)} %pad_add_fusion.place, bf16[6144,512]{1,0:T(8,128)(2,1)} %w_gate.1, bf16[6144,512]{1,0:T(8,128)(2,1)} %w_up.1, bf16[512,6144]{1,0:T(8,128)(2,1)} %w_down.1), custom_call_target="tpu_custom_call" | custom-call | bytes 18874368 | tf_op jit(solution)/shard_map/bring/pallas_call | solution.py:206
  40.3 1.5 %collective-permute-start.8 = (bf16[2,128,1536]{2,1,0:T(8,128)(2,1)S(1)}, bf16[2,128,1536]{2,1,0:T(8,128)(2,1)S(1)}, u32[]{:S(2)}, u32[]{:S(2)}) collective-permute-start(bf16[2,128,1536]{2,1,0:T(8,128)(2,1)S(1)} %pad_maximum_fusion.own_0), channel_id=1, source_target_pairs={{0,3},{1,0},{2,1},{3,2},{4,7},{5,4},{6,5},{7,6},{8,11},{9,8},{10,9... | collective-permute-start | bytes 2359304 | tf_op jit(solution)/shard_map/ppermute | solution.py:63
  41.8 4.4 %collective-permute-done.11 = bf16[128,1536]{1,0:T(8,128)(2,1)S(1)} collective-permute-done((bf16[128,1536]{1,0:T(8,128)(2,1)S(1)}, bf16[128,1536]{1,0:T(8,128)(2,1)S(1)}, u32[]{:S(2)}, u32[]{:S(2)}) %collective-permute-start.11) | collective-permute-done | bytes 393248 | tf_op jit(solution)/shard_map/ppermute | solution.py:63
  47.3 2.4 %collective-permute-start.15 = (bf16[2,128,1536]{2,1,0:T(8,128)(2,1)S(1)}, bf16[2,128,1536]{2,1,0:T(8,128)(2,1)S(1)}, u32[]{:S(2)}, u32[]{:S(2)}) collective-permute-start(bf16[2,128,1536]{2,1,0:T(8,128)(2,1)S(1)} %pad_maximum_fusion.1.own_1), channel_id=1, source_target_pairs={{0,3},{1,0},{2,1},{3,2},{4,7},{5,4},{6,5},{7,6},{8,11},{9,8},{10,9... | collective-permute-start | bytes 2359304 | tf_op jit(solution)/shard_map/ppermute | solution.py:63
  49.6 5.8 %collective-permute-done.8.above_0 = bf16[2,128,1536]{2,1,0:T(8,128)(2,1)S(1)} collective-permute-done((bf16[2,128,1536]{2,1,0:T(8,128)(2,1)S(1)}, bf16[2,128,1536]{2,1,0:T(8,128)(2,1)S(1)}, u32[]{:S(2)}, u32[]{:S(2)}) %collective-permute-start.8) | collective-permute-done | bytes 786464 | tf_op jit(solution)/shard_map/ppermute | solution.py:63
  55.4 2.7 %collective-permute-start.9 = (bf16[2,128,1536]{2,1,0:T(8,128)(2,1)S(1)}, bf16[2,128,1536]{2,1,0:T(8,128)(2,1)S(1)}, u32[]{:S(2)}, u32[]{:S(2)}) collective-permute-start(bf16[2,128,1536]{2,1,0:T(8,128)(2,1)S(1)} %collective-permute-done.8.above_0), channel_id=1, source_target_pairs={{0,3},{1,0},{2,1},{3,2},{4,7},{5,4},{6,5},{7,6},{8,11},{9,8},{10,9... | collective-permute-start | bytes 2359304 | tf_op jit(solution)/shard_map/ppermute | solution.py:63
  58.1 6.0 %collective-permute-done.13.below_1 = bf16[2,128,1536]{2,1,0:T(8,128)(2,1)S(1)} collective-permute-done((bf16[2,128,1536]{2,1,0:T(8,128)(2,1)S(1)}, bf16[2,128,1536]{2,1,0:T(8,128)(2,1)S(1)}, u32[]{:S(2)}, u32[]{:S(2)}) %collective-permute-start.13) | collective-permute-done | bytes 786464 | tf_op jit(solution)/shard_map/ppermute | solution.py:63
  64.1 8.4 %early.1 = (f32[512,512]{1,0:T(8,128)S(1)}, f32[512,512]{1,0:T(8,128)S(1)}) custom-call(s32[2]{0:T(128)S(1)} %pad_add_fusion.place, bf16[2,128,1536]{2,1,0:T(8,128)(2,1)S(1)} %pad_maximum_fusion.own_0, bf16[2,128,1536]{2,1,0:T(8,128)(2,1)S(1)} %pad_maximum_fusion.1.own_1, bf16[2,128,1536]{2,1,0:T(8,128)(2,1)S(1)} %collective-permute-done.8.above_0, ...), custom_call_target="tpu_custom_call" | custom-call | flops 4831838208 | bytes 4718592 | tf_op jit(solution)/shard_map/early/pallas_call | solution.py:222
  72.6 3.9 %collective-permute-done.14.far_1 = bf16[2,128,1536]{2,1,0:T(8,128)(2,1)S(1)} collective-permute-done((bf16[2,128,1536]{2,1,0:T(8,128)(2,1)S(1)}, bf16[2,128,1536]{2,1,0:T(8,128)(2,1)S(1)}, u32[]{:S(2)}, u32[]{:S(2)}) %collective-permute-start.14) | collective-permute-done | bytes 786464 | tf_op jit(solution)/shard_map/ppermute | solution.py:63
  76.4 5.0 %late.1 = (bf16[512,512]{1,0:T(8,128)(2,1)S(1)}, bf16[2,128,1536]{2,1,0:T(8,128)(2,1)S(1)}, bf16[2,128,1536]{2,1,0:T(8,128)(2,1)S(1)}) custom-call(s32[2]{0:T(128)S(1)} %pad_add_fusion.place, bf16[2,128,1536]{2,1,0:T(8,128)(2,1)S(1)} %collective-permute-done.9.far_0, bf16[2,128,1536]{2,1,0:T(8,128)(2,1)S(1)} %collective-permute-done.14.far_1, ...), custom_call_target="tpu_custom_call" | custom-call | flops 2415919104 | bytes 3145728 | tf_op jit(solution)/shard_map/late/pallas_call | solution.py:242
  81.6 1.4 collective-permute-start.16
  83.0 6.2 %rest.1 = (bf16[2,128,1536]{2,1,0:T(8,128)(2,1)S(1)}, bf16[2,128,1536]{2,1,0:T(8,128)(2,1)S(1)}, bf16[2,128,1536]{2,1,0:T(8,128)(2,1)S(1)}, bf16[2,128,1536]{2,1...) custom-call(s32[2]{0:T(128)S(1)} %pad_add_fusion.place, ...), custom_call_target="tpu_custom_call" | custom-call | flops 2415919104 | bytes 4718592 | tf_op jit(solution)/shard_map/rest/pallas_call | solution.py:261
  89.3 2.7 %collective-permute-start.18 = (bf16[2,128,1536]{2,1,0:T(8,128)(2,1)S(1)}, bf16[2,128,1536]{2,1,0:T(8,128)(2,1)}, u32[]{:S(2)}, u32[]{:S(2)}) collective-permute-start(bf16[2,128,1536]{2,1,0:T(8,128)(2,1)S(1)} %get-tuple-element.54), channel_id=1, source_target_pairs={{0,3},{1,0},{2,1},{3,2},{4,7},{5,4},{6,5},{7,6},{8,11},{9,8},{10,9... | collective-permute-start | bytes 2359304 | tf_op jit(solution)/shard_map/ppermute | solution.py:63
  96.5 6.0 %collective-permute-done.19 = bf16[2,128,1536]{2,1,0:T(8,128)(2,1)} collective-permute-done((bf16[2,128,1536]{2,1,0:T(8,128)(2,1)}, bf16[2,128,1536]{2,1,0:T(8,128)(2,1)}, u32[]{:S(2)}, u32[]{:S(2)}) %collective-permute-start.19) | collective-permute-done | bytes 786464 | tf_op jit(solution)/shard_map/ppermute | solution.py:63
  102.5 7.1 %collective-permute-done.21 = bf16[2,128,1536]{2,1,0:T(8,128)(2,1)} collective-permute-done((bf16[2,128,1536]{2,1,0:T(8,128)(2,1)}, bf16[2,128,1536]{2,1,0:T(8,128)(2,1)}, u32[]{:S(2)}, u32[]{:S(2)}) %collective-permute-start.21) | collective-permute-done | bytes 786464 | tf_op jit(solution)/shard_map/ppermute | solution.py:63
  109.6 1.6 %fusion.19 = (bf16[128,1536]{1,0:T(8,128)(2,1)S(1)}, bf16[128,1536]{1,0:T(8,128)(2,1)S(1)}) fusion(bf16[2,128,1536]{2,1,0:T(8,128)(2,1)} %collective-permute-done.21, bf16[2,128,1536]{2,1,0:T(8,128)(2,1)} %collective-permute-done.19, bf16[2,128,1536]{2,1,0:T(8,128)(2,1)S(1)} %get-tuple-element.55), kind=kLoop, calls=%fused_computation.30 | loop fusion | flops 2359296 | bytes 3145728 | tf_op jit(solution)/shard_map/convert_element_type | solution.py:345
  112.5 1.6 %collective-permute-start.24 = (bf16[128,1536]{1,0:T(8,128)(2,1)S(1)}, bf16[128,1536]{1,0:T(8,128)(2,1)}, u32[]{:S(2)}, u32[]{:S(2)}) collective-permute-start(bf16[128,1536]{1,0:T(8,128)(2,1)S(1)} %get-tuple-element.69), channel_id=1, source_target_pairs={{0,12},{1,13},{2,14},{3,15},{4,0},{5,1},{6,2},{7,3},{8,4},{9,5},{1... | collective-permute-start | bytes 1179656 | tf_op jit(solution)/shard_map/ppermute | solution.py:63
  116.4 3.4 %collective-permute-done.23 = bf16[128,1536]{1,0:T(8,128)(2,1)} collective-permute-done((bf16[128,1536]{1,0:T(8,128)(2,1)S(1)}, bf16[128,1536]{1,0:T(8,128)(2,1)}, u32[]{:S(2)}, u32[]{:S(2)}) %collective-permute-start.23) | collective-permute-done | bytes 393248 | tf_op jit(solution)/shard_map/ppermute | solution.py:63
  119.9 3.1 %collective-permute-done.24 = bf16[128,1536]{1,0:T(8,128)(2,1)} collective-permute-done((bf16[128,1536]{1,0:T(8,128)(2,1)S(1)}, bf16[128,1536]{1,0:T(8,128)(2,1)}, u32[]{:S(2)}, u32[]{:S(2)}) %collective-permute-start.24) | collective-permute-done | bytes 393248 | tf_op jit(solution)/shard_map/ppermute | solution.py:63
  124.1 1.9 %fusion.16 = bf16[128,1536]{1,0:T(8,128)(2,1)S(1)} fusion(bf16[128,1536]{1,0:T(8,128)(2,1)} %collective-permute-done.24, bf16[128,1536]{1,0:T(8,128)(2,1)} %collective-permute-done.23, bf16[128,1536]{1,0:T(8,128)(2,1)} %collective-permute-done.22, bf16[2,128,1536]{2,1,0:T(8,128)(2,1)} %collective-permute-done.18, ...), kind=kLoop, calls=%fused_computation.18 | loop fusion | flops 2359296 | bytes 2752512 | tf_op jit(solution)/shard_map/convert_element_type | solution.py:348
  126.1 1.9 %collective-permute-start.25 = (bf16[2,16,1536]{2,1,0:T(8,128)(2,1)S(1)}, bf16[2,16,1536]{2,1,0:T(8,128)(2,1)S(1)}, u32[]{:S(2)}, u32[]{:S(2)}) collective-permute-start(bf16[2,16,1536]{2,1,0:T(8,128)(2,1)S(1)} %bitcast.99), channel_id=1, source_target_pairs={{0,48},{16,0},{32,16},{48,32},{1,49},{17,1},{33,17},{49,33},{2,50}... | collective-permute-start | bytes 294920 | tf_op jit(solution)/shard_map/ppermute | solution.py:49
  129.2 1.3 collective-permute-done.25
  130.5 2.4 %collective-permute-done.26 = bf16[2,16,1536]{2,1,0:T(8,128)(2,1)S(1)} collective-permute-done((bf16[2,16,1536]{2,1,0:T(8,128)(2,1)S(1)}, bf16[2,16,1536]{2,1,0:T(8,128)(2,1)S(1)}, u32[]{:S(2)}, u32[]{:S(2)}) %collective-permute-start.26) | collective-permute-done | bytes 98336 | tf_op jit(solution)/shard_map/ppermute | solution.py:49
  134.1 6.4 %collective-permute-start.28 = (bf16[4,16,1536]{2,1,0:T(8,128)(2,1)S(1)}, bf16[4,16,1536]{2,1,0:T(8,128)(2,1)S(1)}, u32[]{:S(2)}, u32[]{:S(2)}) collective-permute-start(bf16[4,16,1536]{2,1,0:T(8,128)(2,1)S(1)} %get-tuple-element.72), channel_id=1, source_target_pairs={{0,64},{64,0},{1,65},{65,1},{2,66},{66,2},{3,67},{67,3},{4,68},{68... | collective-permute-start | bytes 589832 | tf_op jit(solution)/shard_map/ppermute | solution.py:53
  (99 shorter events, 28.5 us)
Async XLA Ops:
  0.0 4.5 %copy-start.3 = (bf16[32,256]{1,0:T(8,128)(2,1)S(1)}, bf16[32,256]{1,0:T(8,128)(2,1)}, u32[]{:S(2)}) copy-start(bf16[32,256]{1,0:T(8,128)(2,1)} %param.17) | copy-start | bytes 49156
  4.6 8.6 %copy-start.4 = (s32[32,2]{0,1:T(2,128)S(1)}, s32[32,2]{0,1:T(2,128)}, u32[]{:S(2)}) copy-start(s32[32,2]{0,1:T(2,128)} %param.22) | copy-start | bytes 772
  7.4 6.7 %collective-permute-start = (f32[32,9]{0,1:T(8,128)S(1)}, f32[32,9]{0,1:T(8,128)S(1)}, u32[]{:S(2)}, u32[]{:S(2)}) collective-permute-start(f32[32,9]{0,1:T(8,128)S(1)} %pad_maximum_fusion.6), channel_id=1, source_target_pairs={{0,1},{1,2},{2,3},{3,0},{4,5},{5,6},{6,7},{7,4},{8,9},{9,10},{10,1... | collective-permute-start | bytes 3464 | tf_op jit(solution)/shard_map/ppermute | solution.py:49
  9.5 4.6 %collective-permute-start.1 = (f32[32,9]{0,1:T(8,128)S(1)}, f32[32,9]{0,1:T(8,128)S(1)}, u32[]{:S(2)}, u32[]{:S(2)}) collective-permute-start(f32[32,9]{0,1:T(8,128)S(1)} %pad_maximum_fusion.6), channel_id=1, source_target_pairs={{0,2},{1,3},{2,0},{3,1},{4,6},{5,7},{6,4},{7,5},{8,10},{9,11},{10,... | collective-permute-start | bytes 3464 | tf_op jit(solution)/shard_map/ppermute | solution.py:49
  12.1 2.8 %collective-permute-start.2 = (f32[32,9]{0,1:T(8,128)S(1)}, f32[32,9]{0,1:T(8,128)S(1)}, u32[]{:S(2)}, u32[]{:S(2)}) collective-permute-start(f32[32,9]{0,1:T(8,128)S(1)} %pad_maximum_fusion.6), channel_id=1, source_target_pairs={{0,3},{1,0},{2,1},{3,2},{4,7},{5,4},{6,5},{7,6},{8,11},{9,8},{10,9... | collective-permute-start | bytes 3464 | tf_op jit(solution)/shard_map/ppermute | solution.py:49
  15.3 3.2 %collective-permute-start.3 = (bf16[4,16,1536]{2,1,0:T(8,128)(2,1)S(1)}, bf16[4,16,1536]{2,1,0:T(8,128)(2,1)S(1)}, u32[]{:S(2)}, u32[]{:S(2)}) collective-permute-start(bf16[4,16,1536]{2,1,0:T(8,128)(2,1)S(1)} %get-tuple-element.82), channel_id=1, source_target_pairs={{0,64},{64,0},{1,65},{65,1},{2,66},{66,2},{3,67},{67,3},{4,68},{68... | collective-permute-start | bytes 589832 | tf_op jit(solution)/shard_map/ppermute | solution.py:53
  18.6 6.7 %collective-permute-start.4 = (bf16[32,1536]{1,0:T(8,128)(2,1)S(1)}, bf16[32,1536]{1,0:T(8,128)(2,1)S(1)}, u32[]{:S(2)}, u32[]{:S(2)}) collective-permute-start(bf16[32,1536]{1,0:T(8,128)(2,1)S(1)} %bitcast.101), channel_id=1, source_target_pairs={{0,16},{16,32},{32,48},{48,0},{1,17},{17,33},{33,49},{49,1},{2,18}... | collective-permute-start | bytes 294920 | tf_op jit(solution)/shard_map/ppermute | solution.py:49
  20.3 8.0 %collective-permute-start.5 = (bf16[32,1536]{1,0:T(8,128)(2,1)S(1)}, bf16[32,1536]{1,0:T(8,128)(2,1)S(1)}, u32[]{:S(2)}, u32[]{:S(2)}) collective-permute-start(bf16[32,1536]{1,0:T(8,128)(2,1)S(1)} %bitcast.98), channel_id=1, source_target_pairs={{0,32},{16,48},{32,0},{48,16},{1,33},{17,49},{33,1},{49,17},{2,34}... | collective-permute-start | bytes 294920 | tf_op jit(solution)/shard_map/ppermute | solution.py:49
  23.6 4.7 %collective-permute-start.6 = (bf16[32,1536]{1,0:T(8,128)(2,1)S(1)}, bf16[32,1536]{1,0:T(8,128)(2,1)S(1)}, u32[]{:S(2)}, u32[]{:S(2)}) collective-permute-start(bf16[32,1536]{1,0:T(8,128)(2,1)S(1)} %bitcast.95), channel_id=1, source_target_pairs={{0,48},{16,0},{32,16},{48,32},{1,49},{17,1},{33,17},{49,33},{2,50}... | collective-permute-start | bytes 294920 | tf_op jit(solution)/shard_map/ppermute | solution.py:49
  28.3 9.4 %collective-permute-start.7 = (bf16[128,1536]{1,0:T(8,128)(2,1)S(1)}, bf16[128,1536]{1,0:T(8,128)(2,1)S(1)}, u32[]{:S(2)}, u32[]{:S(2)}) collective-permute-start(bf16[128,1536]{1,0:T(8,128)(2,1)S(1)} %pad_maximum_fusion.2), channel_id=1, source_target_pairs={{0,12},{1,13},{2,14},{3,15},{4,0},{5,1},{6,2},{7,3},{8,4},{9,5},{1... | collective-permute-start | bytes 1179656 | tf_op jit(solution)/shard_map/ppermute | solution.py:63
  30.7 11.1 %collective-permute-start.12 = (bf16[128,1536]{1,0:T(8,128)(2,1)S(1)}, bf16[128,1536]{1,0:T(8,128)(2,1)S(1)}, u32[]{:S(2)}, u32[]{:S(2)}) collective-permute-start(bf16[128,1536]{1,0:T(8,128)(2,1)S(1)} %pad_maximum_fusion.2), channel_id=1, source_target_pairs={{0,4},{1,5},{2,6},{3,7},{4,8},{5,9},{6,10},{7,11},{8,12},{9,13},{1... | collective-permute-start | bytes 1179656 | tf_op jit(solution)/shard_map/ppermute | solution.py:63
  37.7 8.5 %collective-permute-start.11 = (bf16[128,1536]{1,0:T(8,128)(2,1)S(1)}, bf16[128,1536]{1,0:T(8,128)(2,1)S(1)}, u32[]{:S(2)}, u32[]{:S(2)}) collective-permute-start(bf16[128,1536]{1,0:T(8,128)(2,1)S(1)} %pad_maximum_fusion.2), channel_id=1, source_target_pairs={{0,8},{1,9},{2,10},{3,11},{4,12},{5,13},{6,14},{7,15},{8,0},{9,1},... | collective-permute-start | bytes 1179656 | tf_op jit(solution)/shard_map/ppermute | solution.py:63
  39.0 19.0 %collective-permute-start.10 = (bf16[2,128,1536]{2,1,0:T(8,128)(2,1)S(1)}, bf16[2,128,1536]{2,1,0:T(8,128)(2,1)S(1)}, u32[]{:S(2)}, u32[]{:S(2)}) collective-permute-start(bf16[2,128,1536]{2,1,0:T(8,128)(2,1)S(1)} %pad_maximum_fusion.own_0), channel_id=1, source_target_pairs={{0,1},{1,2},{2,3},{3,0},{4,5},{5,6},{6,7},{7,4},{8,9},{9,10},{10,1... | collective-permute-start | bytes 2359304 | tf_op jit(solution)/shard_map/ppermute | solution.py:63
  40.3 15.1 %collective-permute-start.8 = (bf16[2,128,1536]{2,1,0:T(8,128)(2,1)S(1)}, bf16[2,128,1536]{2,1,0:T(8,128)(2,1)S(1)}, u32[]{:S(2)}, u32[]{:S(2)}) collective-permute-start(bf16[2,128,1536]{2,1,0:T(8,128)(2,1)S(1)} %pad_maximum_fusion.own_0), channel_id=1, source_target_pairs={{0,3},{1,0},{2,1},{3,2},{4,7},{5,4},{6,5},{7,6},{8,11},{9,8},{10,9... | collective-permute-start | bytes 2359304 | tf_op jit(solution)/shard_map/ppermute | solution.py:63
  46.3 17.8 %collective-permute-start.13 = (bf16[2,128,1536]{2,1,0:T(8,128)(2,1)S(1)}, bf16[2,128,1536]{2,1,0:T(8,128)(2,1)S(1)}, u32[]{:S(2)}, u32[]{:S(2)}) collective-permute-start(bf16[2,128,1536]{2,1,0:T(8,128)(2,1)S(1)} %pad_maximum_fusion.1.own_1), channel_id=1, source_target_pairs={{0,1},{1,2},{2,3},{3,0},{4,5},{5,6},{6,7},{7,4},{8,9},{9,10},{10,1... | collective-permute-start | bytes 2359304 | tf_op jit(solution)/shard_map/ppermute | solution.py:63
  47.3 16.8 %collective-permute-start.15 = (bf16[2,128,1536]{2,1,0:T(8,128)(2,1)S(1)}, bf16[2,128,1536]{2,1,0:T(8,128)(2,1)S(1)}, u32[]{:S(2)}, u32[]{:S(2)}) collective-permute-start(bf16[2,128,1536]{2,1,0:T(8,128)(2,1)S(1)} %pad_maximum_fusion.1.own_1), channel_id=1, source_target_pairs={{0,3},{1,0},{2,1},{3,2},{4,7},{5,4},{6,5},{7,6},{8,11},{9,8},{10,9... | collective-permute-start | bytes 2359304 | tf_op jit(solution)/shard_map/ppermute | solution.py:63
  55.4 17.2 %collective-permute-start.9 = (bf16[2,128,1536]{2,1,0:T(8,128)(2,1)S(1)}, bf16[2,128,1536]{2,1,0:T(8,128)(2,1)S(1)}, u32[]{:S(2)}, u32[]{:S(2)}) collective-permute-start(bf16[2,128,1536]{2,1,0:T(8,128)(2,1)S(1)} %collective-permute-done.8.above_0), channel_id=1, source_target_pairs={{0,3},{1,0},{2,1},{3,2},{4,7},{5,4},{6,5},{7,6},{8,11},{9,8},{10,9... | collective-permute-start | bytes 2359304 | tf_op jit(solution)/shard_map/ppermute | solution.py:63
  64.1 12.3 %collective-permute-start.14 = (bf16[2,128,1536]{2,1,0:T(8,128)(2,1)S(1)}, bf16[2,128,1536]{2,1,0:T(8,128)(2,1)S(1)}, u32[]{:S(2)}, u32[]{:S(2)}) collective-permute-start(bf16[2,128,1536]{2,1,0:T(8,128)(2,1)S(1)} %collective-permute-done.13.below_1), channel_id=1, source_target_pairs={{0,1},{1,2},{2,3},{3,0},{4,5},{5,6},{6,7},{7,4},{8,9},{9,10},{10,1... | collective-permute-start | bytes 2359304 | tf_op jit(solution)/shard_map/ppermute | solution.py:63
  81.5 11.2 %collective-permute-start.20 = (bf16[2,128,1536]{2,1,0:T(8,128)(2,1)S(1)}, bf16[2,128,1536]{2,1,0:T(8,128)(2,1)S(1)}, u32[]{:S(2)}, u32[]{:S(2)}) collective-permute-start(bf16[2,128,1536]{2,1,0:T(8,128)(2,1)S(1)} %get-tuple-element.58), channel_id=1, source_target_pairs={{0,3},{1,0},{2,1},{3,2},{4,7},{5,4},{6,5},{7,6},{8,11},{9,8},{10,9... | collective-permute-start | bytes 2359304 | tf_op jit(solution)/shard_map/ppermute | solution.py:63
  81.6 13.4 %collective-permute-start.16 = (bf16[2,128,1536]{2,1,0:T(8,128)(2,1)S(1)}, bf16[2,128,1536]{2,1,0:T(8,128)(2,1)S(1)}, u32[]{:S(2)}, u32[]{:S(2)}) collective-permute-start(bf16[2,128,1536]{2,1,0:T(8,128)(2,1)S(1)} %get-tuple-element.53), channel_id=1, source_target_pairs={{0,1},{1,2},{2,3},{3,0},{4,5},{5,6},{6,7},{7,4},{8,9},{9,10},{10,1... | collective-permute-start | bytes 2359304 | tf_op jit(solution)/shard_map/ppermute | solution.py:63
  89.2 13.2 %collective-permute-start.19 = (bf16[2,128,1536]{2,1,0:T(8,128)(2,1)}, bf16[2,128,1536]{2,1,0:T(8,128)(2,1)}, u32[]{:S(2)}, u32[]{:S(2)}) collective-permute-start(bf16[2,128,1536]{2,1,0:T(8,128)(2,1)} %get-tuple-element.56), channel_id=1, source_target_pairs={{0,1},{1,2},{2,3},{3,0},{4,5},{5,6},{6,7},{7,4},{8,9},{9,10},{10,1... | collective-permute-start | bytes 2359304 | tf_op jit(solution)/shard_map/ppermute | solution.py:63
  89.3 24.8 %collective-permute-start.18 = (bf16[2,128,1536]{2,1,0:T(8,128)(2,1)S(1)}, bf16[2,128,1536]{2,1,0:T(8,128)(2,1)}, u32[]{:S(2)}, u32[]{:S(2)}) collective-permute-start(bf16[2,128,1536]{2,1,0:T(8,128)(2,1)S(1)} %get-tuple-element.54), channel_id=1, source_target_pairs={{0,3},{1,0},{2,1},{3,2},{4,7},{5,4},{6,5},{7,6},{8,11},{9,8},{10,9... | collective-permute-start | bytes 2359304 | tf_op jit(solution)/shard_map/ppermute | solution.py:63
  93.7 15.9 %collective-permute-start.21 = (bf16[2,128,1536]{2,1,0:T(8,128)(2,1)}, bf16[2,128,1536]{2,1,0:T(8,128)(2,1)}, u32[]{:S(2)}, u32[]{:S(2)}) collective-permute-start(bf16[2,128,1536]{2,1,0:T(8,128)(2,1)} %add_convert_fusion), channel_id=1, source_target_pairs={{0,3},{1,0},{2,1},{3,2},{4,7},{5,4},{6,5},{7,6},{8,11},{9,8},{10,9... | collective-permute-start | bytes 2359304 | tf_op jit(solution)/shard_map/ppermute | solution.py:63
  96.1 18.1 %collective-permute-start.17 = (bf16[2,128,1536]{2,1,0:T(8,128)(2,1)}, bf16[2,128,1536]{2,1,0:T(8,128)(2,1)}, u32[]{:S(2)}, u32[]{:S(2)}) collective-permute-start(bf16[2,128,1536]{2,1,0:T(8,128)(2,1)} %add_convert_fusion.1), channel_id=1, source_target_pairs={{0,1},{1,2},{2,3},{3,0},{4,5},{5,6},{6,7},{7,4},{8,9},{9,10},{10,1... | collective-permute-start | bytes 2359304 | tf_op jit(solution)/shard_map/ppermute | solution.py:63
  111.3 8.6 %collective-permute-start.23 = (bf16[128,1536]{1,0:T(8,128)(2,1)S(1)}, bf16[128,1536]{1,0:T(8,128)(2,1)}, u32[]{:S(2)}, u32[]{:S(2)}) collective-permute-start(bf16[128,1536]{1,0:T(8,128)(2,1)S(1)} %get-tuple-element.70), channel_id=1, source_target_pairs={{0,8},{1,9},{2,10},{3,11},{4,12},{5,13},{6,14},{7,15},{8,0},{9,1},... | collective-permute-start | bytes 1179656 | tf_op jit(solution)/shard_map/ppermute | solution.py:63
  112.5 10.4 %collective-permute-start.24 = (bf16[128,1536]{1,0:T(8,128)(2,1)S(1)}, bf16[128,1536]{1,0:T(8,128)(2,1)}, u32[]{:S(2)}, u32[]{:S(2)}) collective-permute-start(bf16[128,1536]{1,0:T(8,128)(2,1)S(1)} %get-tuple-element.69), channel_id=1, source_target_pairs={{0,12},{1,13},{2,14},{3,15},{4,0},{5,1},{6,2},{7,3},{8,4},{9,5},{1... | collective-permute-start | bytes 1179656 | tf_op jit(solution)/shard_map/ppermute | solution.py:63
  115.4 8.7 %collective-permute-start.22 = (bf16[128,1536]{1,0:T(8,128)(2,1)S(1)}, bf16[128,1536]{1,0:T(8,128)(2,1)}, u32[]{:S(2)}, u32[]{:S(2)}) collective-permute-start(bf16[128,1536]{1,0:T(8,128)(2,1)S(1)} %fusion.17), channel_id=1, source_target_pairs={{0,4},{1,5},{2,6},{3,7},{4,8},{5,9},{6,10},{7,11},{8,12},{9,13},{1... | collective-permute-start | bytes 1179656 | tf_op jit(solution)/shard_map/ppermute | solution.py:63
  124.1 18.4 %copy-start.1 = (bf16[32,128,256]{2,1,0:T(8,128)(2,1)S(1)}, bf16[32,128,256]{2,1,0:T(8,128)(2,1)}, u32[]{:S(2)}) copy-start(bf16[32,128,256]{2,1,0:T(8,128)(2,1)} %param.14) | copy-start | bytes 6291460
  126.1 4.5 %collective-permute-start.25 = (bf16[2,16,1536]{2,1,0:T(8,128)(2,1)S(1)}, bf16[2,16,1536]{2,1,0:T(8,128)(2,1)S(1)}, u32[]{:S(2)}, u32[]{:S(2)}) collective-permute-start(bf16[2,16,1536]{2,1,0:T(8,128)(2,1)S(1)} %bitcast.99), channel_id=1, source_target_pairs={{0,48},{16,0},{32,16},{48,32},{1,49},{17,1},{33,17},{49,33},{2,50}... | collective-permute-start | bytes 294920 | tf_op jit(solution)/shard_map/ppermute | solution.py:49
  127.9 5.0 %collective-permute-start.26 = (bf16[2,16,1536]{2,1,0:T(8,128)(2,1)S(1)}, bf16[2,16,1536]{2,1,0:T(8,128)(2,1)S(1)}, u32[]{:S(2)}, u32[]{:S(2)}) collective-permute-start(bf16[2,16,1536]{2,1,0:T(8,128)(2,1)S(1)} %bitcast.96), channel_id=1, source_target_pairs={{0,32},{16,48},{32,0},{48,16},{1,33},{17,49},{33,1},{49,17},{2,34}... | collective-permute-start | bytes 294920 | tf_op jit(solution)/shard_map/ppermute | solution.py:49
  129.2 4.8 %collective-permute-start.27 = (bf16[2,16,1536]{2,1,0:T(8,128)(2,1)S(1)}, bf16[2,16,1536]{2,1,0:T(8,128)(2,1)S(1)}, u32[]{:S(2)}, u32[]{:S(2)}) collective-permute-start(bf16[2,16,1536]{2,1,0:T(8,128)(2,1)S(1)} %bitcast.93), channel_id=1, source_target_pairs={{0,16},{16,32},{32,48},{48,0},{1,17},{17,33},{33,49},{49,1},{2,18}... | collective-permute-start | bytes 294920 | tf_op jit(solution)/shard_map/ppermute | solution.py:49
  134.1 7.5 %collective-permute-start.28 = (bf16[4,16,1536]{2,1,0:T(8,128)(2,1)S(1)}, bf16[4,16,1536]{2,1,0:T(8,128)(2,1)S(1)}, u32[]{:S(2)}, u32[]{:S(2)}) collective-permute-start(bf16[4,16,1536]{2,1,0:T(8,128)(2,1)S(1)} %get-tuple-element.72), channel_id=1, source_target_pairs={{0,64},{64,0},{1,65},{65,1},{2,66},{66,2},{3,67},{67,3},{4,68},{68... | collective-permute-start | bytes 589832 | tf_op jit(solution)/shard_map/ppermute | solution.py:53
  (4 other events, 10.4 us)

commit v3 on v2

--- a/solution.py
+++ b/solution.py
@@ -78,48 +78,80 @@
     return [(q, [(p, arrived[q][ORDER[p] // 2].at[ORDER[p] % 2]) for p in range(RING)]) for q in quarters]
 
 
-def bring_kernel(place, w_gate, w_up, w_down, gate_in, up_in, down_in, sem):
-    pairs = ((w_gate, gate_in), (w_up, up_in), (w_down, down_in))
-    copies = [pltpu.make_async_copy(source, target, sem.at[i]) for i, (source, target) in enumerate(pairs)]
-    for copy in copies:
-        copy.start()
-    for copy in copies:
-        copy.wait()
+def add_squares(square, rows, position, inverse):
+    block, features = rows.shape
+    total = jnp.zeros((block, 128), f32)
+    for lane in range(0, features, 128):
+        plain = rows[:, lane : lane + 128].astype(f32) * inverse[:, lane : lane + 128]
+        total = total + plain * plain
+    square[position * block : (position + 1) * block, :] += total
 
 
 def early_kernel(
-    place, own_0, own_1, above_0, above_1, below_0, below_1, w_gate, w_up, gate, upper, rows, sem
+    place, own_0, own_1, above_0, above_1, below_0, below_1, inverse, w_gate, w_up,
+    gate, upper, square, gate_in, up_in, rows, sem, gate_sem, up_sem,
 ):
     core, me = place[0], place[1]
     _, _, block, features = rows.shape
     arrived = {0: (own_0, own_1), 1: (above_0, above_1), 3: (below_0, below_1)}
     gate[...] = jnp.zeros_like(gate)
     upper[...] = jnp.zeros_like(upper)
+    square[...] = jnp.zeros_like(square)
+
+    def weights(quarter):
+        cut = turned(me, quarter, features)
+        return (
+            pltpu.make_async_copy(w_gate.at[cut, :], gate_in.at[cut, :], gate_sem.at[quarter]),
+            pltpu.make_async_copy(w_up.at[cut, :], up_in.at[cut, :], up_sem.at[quarter]),
+        )
 
     for flipped in range(2):
         @pl.when(core == flipped)
         def _():
-            work = pieces_of(flipped, arrived)
-            for quarter, blocks in work:
-                for p, source in blocks:
-                    pltpu.make_async_copy(source, rows.at[quarter, p], sem.at[quarter, p]).start()
-            for quarter, blocks in work:
-                number = len(blocks)
+            work = dict(pieces_of(flipped, arrived))
+            order = list(work) + [q for q in range(RING) if q not in work]
+
+            def begin(step):
+                if step < RING:
+                    quarter = order[step]
+                    for p, source in work.get(quarter, ()):
+                        pltpu.make_async_copy(source, rows.at[quarter, p], sem.at[quarter, p]).start()
+                    for copy in weights(quarter):
+                        copy.start()
+
+            begin(0)
+            begin(1)
+            for step, quarter in enumerate(order):
+                blocks = work.get(quarter, ())
                 for p, source in blocks:
                     pltpu.make_async_copy(source, rows.at[quarter, p], sem.at[quarter, p]).wait()
+                for copy in weights(quarter):
+                    copy.wait()
+                begin(step + 2)
+                if not blocks:
+                    continue
+                number = len(blocks)
                 some = pl.ds(0, number * block)
                 held = rows[quarter, :number].reshape(number * block, features)
                 cut = turned(me, quarter, features)
-                gate[some, :] += jnp.dot(held, w_gate[cut, :], preferred_element_type=f32)
-                upper[some, :] += jnp.dot(held, w_up[cut, :], preferred_element_type=f32)
-
-
-def late_kernel(place, far_0, far_1, gate_in, up_in, w_gate, w_up, w_down, act, out_0, out_1, rows, gate, upper, sem):
+                gate[some, :] += jnp.dot(held, gate_in[cut, :], preferred_element_type=f32)
+                upper[some, :] += jnp.dot(held, up_in[cut, :], preferred_element_type=f32)
+                for p, _ in blocks:
+                    add_squares(square, rows.at[quarter, p], p, inverse.at[quarter])
+
+
+def late_kernel(
+    place, far_0, far_1, inverse, gate_in, up_in, square_in, w_gate, w_up, w_down,
+    act, out_0, out_1, rows, gate, upper, square, downs, sem, down_sem,
+):
     core, me = place[0], place[1]
     _, block, features = rows.shape
     count = RING * block
     halves, outs = (far_0, far_1), (out_0, out_1)
     last = pl.ds((RING - 1) * block, block)
+
+    def fetch(quarter):
+        return pltpu.make_async_copy(w_down.at[:, turned(me, quarter, features)], downs.at[quarter], down_sem.at[quarter])
 
     for flipped in range(2):
         @pl.when(core == flipped)
@@ -127,9 +159,12 @@
             for p in range(RING):
                 inner = p if flipped else ORDER[p]
                 pltpu.make_async_copy(halves[inner // 2].at[inner % 2], rows.at[p], sem.at[p]).start()
+            for quarter in range(RING) if flipped else (2,):
+                fetch(quarter).start()
 
     gate[...] = gate_in[...]
     upper[...] = up_in[...]
+    square[...] = square_in[...]
     for p in range(RING):
         pltpu.make_async_copy(far_0.at[0], rows.at[p], sem.at[p]).wait()
 
@@ -138,6 +173,8 @@
         held = rows[...].reshape(count, features)
         gate[...] += jnp.dot(held, w_gate[turned(me, 2, features), :], preferred_element_type=f32)
         upper[...] += jnp.dot(held, w_up[turned(me, 2, features), :], preferred_element_type=f32)
+        for p in range(RING):
+            add_squares(square, rows.at[p], p, inverse.at[2])
 
     @pl.when(core == 1)
     def _():
@@ -145,33 +182,40 @@
         def _(quarter):
             gate[last, :] += jnp.dot(rows[quarter], w_gate[turned(me, quarter, features), :], preferred_element_type=f32)
             upper[last, :] += jnp.dot(rows[quarter], w_up[turned(me, quarter, features), :], preferred_element_type=f32)
-
-    held = gate[...]
-    act[...] = (held * jax.nn.sigmoid(held) * upper[...]).astype(bf16)
+            add_squares(square, rows.at[quarter], RING - 1, inverse.at[quarter])
+
+    mean = jnp.sum(square[...], -1, keepdims=True) / (RING * features)
+    scale = lax.rsqrt(mean + 1e-05)
+    held = gate[...] * scale
+    act[...] = (held * jax.nn.sigmoid(held) * (upper[...] * scale)).astype(bf16)
 
     @pl.when(core == 0)
     def _():
-        outcome = jnp.dot(act[...], w_down[:, turned(me, 2, features)], preferred_element_type=f32).astype(bf16)
+        fetch(2).wait()
+        outcome = jnp.dot(act[...], downs[2], preferred_element_type=f32).astype(bf16)
         for p in range(RING):
             outs[ORDER[p] // 2][ORDER[p] % 2] = outcome[p * block : (p + 1) * block]
 
     @pl.when(core == 1)
     def _():
         for quarter in range(RING):
+            fetch(quarter).wait()
             outs[quarter // 2][quarter % 2] = jnp.dot(
-                act[last, :], w_down[:, turned(me, quarter, features)], preferred_element_type=f32
+                act[last, :], downs[quarter], preferred_element_type=f32
             ).astype(bf16)
 
 
-def rest_kernel(place, act, w_down, own_0, own_1, above_0, above_1, below_0, below_1, rows, sem):
+def rest_kernel(place, act, w_down, own_0, own_1, above_0, above_1, below_0, below_1, rows, downs, sem, down_sem):
     core, me = place[0], place[1]
     _, _, block, features = rows.shape
     halves = {0: (own_0, own_1), 1: (above_0, above_1), 3: (below_0, below_1)}
 
+    def fetch(quarter):
+        return pltpu.make_async_copy(w_down.at[:, turned(me, quarter, features)], downs.at[quarter], down_sem.at[quarter])
+
     def step(quarter, blocks):
-        outcome = jnp.dot(
-            act[: blocks * block, :], w_down[:, turned(me, quarter, features)], preferred_element_type=f32
-        )
+        fetch(quarter).wait()
+        outcome = jnp.dot(act[: blocks * block, :], downs[quarter], preferred_element_type=f32)
         rows[quarter, :blocks] = outcome.astype(bf16).reshape(blocks, block, features)
         for p in range(blocks):
             if blocks < RING:
@@ -185,6 +229,8 @@
         def _():
             quarters, blocks = (range(RING), RING - 1) if flipped else ((1, 3, 0), RING)
             for quarter in quarters:
+                fetch(quarter).start()
+            for quarter in quarters:
                 step(quarter, blocks)
             for quarter in quarters:
                 for p in range(blocks):
@@ -201,40 +247,30 @@
     return pl.CostEstimate(flops=2 * macs, bytes_accessed=moved, transcendentals=raised)
 
 
-def bring(place, w_gate, w_up, w_down):
-    weights = [pltpu.with_memory_space_constraint(w, pltpu.HBM) for w in (w_gate, w_up, w_down)]
-    return pl.pallas_call(
-        bring_kernel,
-        out_shape=[pltpu.VMEM(w.shape, bf16) for w in weights],
-        in_specs=[SCALARS] + [pl.BlockSpec(memory_space=pltpu.HBM)] * 3,
-        out_specs=[INSIDE] * 3,
-        scratch_shapes=[pltpu.SemaphoreType.DMA((3,))],
-        compiler_params=pltpu.CompilerParams(vmem_limit_bytes=MIB),
-        cost_estimate=cost(0, 3 * w_gate.size * 2),
-        name="bring",
-    )(place, *weights)
-
-
-def early(place, pieces, w_gate, w_up):
+def early(place, pieces, inverse, w_gate, w_up):
     _, block, features = pieces[0].shape
     units = w_gate.shape[1]
     count = RING * block
+    weights = [pltpu.with_memory_space_constraint(w, pltpu.HBM) for w in (w_gate, w_up)]
     return pl.pallas_call(
         early_kernel,
-        out_shape=[jax.ShapeDtypeStruct((count, units), f32)] * 2,
-        in_specs=[SCALARS] + [ANYWHERE] * 6 + [INSIDE] * 2,
-        out_specs=[INSIDE] * 2,
+        out_shape=[jax.ShapeDtypeStruct((count, n), f32) for n in (units, units, 128)]
+        + [pltpu.VMEM(w.shape, bf16) for w in weights],
+        in_specs=[SCALARS] + [ANYWHERE] * 6 + [INSIDE] + [pl.BlockSpec(memory_space=pltpu.HBM)] * 2,
+        out_specs=[INSIDE] * 5,
         scratch_shapes=[
             pltpu.VMEM((RING, RING, block, features), bf16),
             pltpu.SemaphoreType.DMA((RING, RING)),
+            pltpu.SemaphoreType.DMA((RING,)),
+            pltpu.SemaphoreType.DMA((RING,)),
         ],
         compiler_params=pltpu.CompilerParams(vmem_limit_bytes=16 * MIB),
-        cost_estimate=cost(3 * count * features * units * 2, 3 * count * features * 2),
+        cost_estimate=cost(3 * count * features * units * 2, 3 * count * features * 2 + 4 * w_gate.size),
         name="early",
-    )(place, *pieces, w_gate, w_up)
-
-
-def late(place, far, gate, upper, w_gate, w_up, w_down):
+    )(place, *pieces, inverse, *weights)
+
+
+def late(place, far, inverse, gate, upper, square, w_gate, w_up, w_down):
     _, block, features = far[0].shape
     units = w_gate.shape[1]
     count = RING * block
@@ -242,35 +278,44 @@
     return pl.pallas_call(
         late_kernel,
         out_shape=[jax.ShapeDtypeStruct((count, units), bf16), half, half],
-        in_specs=[SCALARS] + [ANYWHERE] * 2 + [INSIDE] * 5,
+        in_specs=[SCALARS] + [ANYWHERE] * 2 + [INSIDE] * 6 + [pl.BlockSpec(memory_space=pltpu.HBM)],
         out_specs=[INSIDE] * 3,
         scratch_shapes=[
             pltpu.VMEM((RING, block, features), bf16),
             pltpu.VMEM((count, units), f32),
             pltpu.VMEM((count, units), f32),
+            pltpu.VMEM((count, 128), f32),
+            pltpu.VMEM((RING, units, features), bf16),
+            pltpu.SemaphoreType.DMA((RING,)),
             pltpu.SemaphoreType.DMA((RING,)),
         ],
-        compiler_params=pltpu.CompilerParams(vmem_limit_bytes=16 * MIB),
+        compiler_params=pltpu.CompilerParams(vmem_limit_bytes=20 * MIB),
         cost_estimate=cost(count * features * units * 3, 2 * count * features * 2, count * units),
         name="late",
-    )(place, *far, gate, upper, w_gate, w_up, w_down)
+    )(
+        place, *far, inverse, gate, upper, square, w_gate, w_up,
+        pltpu.with_memory_space_constraint(w_down, pltpu.HBM),
+    )
 
 
 def rest(place, act, w_down, shape):
     _, block, features = shape
+    units = act.shape[1]
     return pl.pallas_call(
         rest_kernel,
         out_shape=[jax.ShapeDtypeStruct(shape, bf16)] * 6,
-        in_specs=[SCALARS] + [INSIDE] * 2,
+        in_specs=[SCALARS, INSIDE, pl.BlockSpec(memory_space=pltpu.HBM)],
         out_specs=[ANYWHERE] * 6,
         scratch_shapes=[
             pltpu.VMEM((RING, RING, block, features), bf16),
+            pltpu.VMEM((RING, units, features), bf16),
             pltpu.SemaphoreType.DMA((RING, RING)),
+            pltpu.SemaphoreType.DMA((RING,)),
         ],
-        compiler_params=pltpu.CompilerParams(vmem_limit_bytes=16 * MIB),
-        cost_estimate=cost(3 * act.size * features, 3 * RING * block * features * 2),
+        compiler_params=pltpu.CompilerParams(vmem_limit_bytes=20 * MIB),
+        cost_estimate=cost(3 * act.size * features, 3 * RING * block * features * 2 + 2 * w_down.size),
         name="rest",
-    )(place, act, w_down)
+    )(place, act, pltpu.with_memory_space_constraint(w_down, pltpu.HBM))
 
 
 def shards(
@@ -285,17 +330,15 @@
     attn = attend(queries, key_cache, value_cache, key_new, value_new, lengths)
     hidden_state = (residual.astype(f32) + attn).astype(bf16)
     hfloat = hidden_state.astype(f32)
-    raised = hfloat * norm_gain.astype(f32)[None, :]
+    raised = (hfloat * norm_gain.astype(f32)[None, :]).astype(bf16)
     stats = jnp.concatenate(
         [
-            jnp.dot(raised.astype(bf16), w_router, preferred_element_type=f32),
+            jnp.dot(raised, w_router, preferred_element_type=f32),
             jnp.sum(hfloat * hfloat, -1, keepdims=True),
         ],
         1,
     )
-    stats = stats + along(stats, "tp", 1) + along(stats, "tp", 2) + along(stats, "tp", 3)
-    scale = lax.rsqrt(stats[:, experts:] / (features * RING) + 1e-05)
-    normed = (raised * scale).astype(bf16)
+    shared = jnp.concatenate([stats.reshape(-1), norm_gain.astype(f32)])
 
     near = ((expert_ids // RING + me_pool) % 2) * RING + (expert_ids % RING - me_z + RING) % RING
     flat = near.reshape(-1)
@@ -307,7 +350,7 @@
     places = jnp.arange(experts * CAP, dtype=jnp.int32)
     hot = position[:, :, None] == places[None, None, :]
     dispatch = jnp.any(hot, 1).T.astype(bf16)
-    bucket = jnp.dot(dispatch, normed, preferred_element_type=f32).astype(bf16)
+    bucket = jnp.dot(dispatch, raised, preferred_element_type=f32).astype(bf16)
     buckets = bucket.reshape(GROUPS, 2, RING, size, features)
 
     returned = []
@@ -315,25 +358,33 @@
         partner = swap_cores(buckets[group, 1])
         pairs = jnp.stack([buckets[group, 0], partner], 1).reshape(RING, 2 * size, features)
         block = jnp.concatenate([pairs[0]] + [along(pairs[d], "z", d) for d in range(1, RING)])
+        if group == 0:
+            twin = lax.ppermute(shared, "tp", [(i, i ^ 1) for i in range(RING)])
+            block, twin = lax.optimization_barrier((block, twin))
+            couple = jnp.stack([shared, twin])
+            block, couple = lax.optimization_barrier((block, couple))
+            others = lax.ppermute(couple, "tp", [(i, i ^ 2) for i in range(RING)])
         near_block, last_block = cross(block, 0, -1), cross(block, 0, 1)
+        far_block = cross(block, 0, 2)
         if group == 0:
-            place, block = lax.optimization_barrier((place, block))
-            weights = bring(place, w_gate, w_up, w_down)
-            near_block, weights = lax.optimization_barrier((near_block, weights))
-            gate_in, up_in, down_in = weights
-        near_block, kept = lax.optimization_barrier((near_block, block))
-        far_block = cross(kept, 0, 2)
+            far_block, others = lax.optimization_barrier((far_block, others))
+            everyone = jnp.concatenate([couple, others])
+            stats = jnp.sum(everyone[:, : stats.size], 0).reshape(stats.shape)
+            scale = lax.rsqrt(stats[:, experts:] / (features * RING) + 1e-05)
+            turns = jnp.arange(RING, dtype=jnp.int32)
+            pick = (me_y ^ turns)[None, :] == ((me_y + turns) % RING)[:, None]
+            gains = jnp.sum(jnp.where(pick[:, :, None], everyone[None, :, stats.size :], 0.0), 1)
+            inverse = 1.0 / gains[:, None, :]
         own = [jnp.stack([block, near_block]), jnp.stack([far_block, last_block])]
         above, below = [None, None], [None, None]
         for half in range(2):
             above[half] = cross(own[half], 1, -1)
             below[half] = cross(own[half], 1, 1)
-        below = lax.optimization_barrier(below)
         far = [cross(above[0], 1, -1), cross(below[1], 1, 1)]
-        gate, upper = early(place, own + above + below, gate_in, up_in)
-        act, far_0, far_1 = late(place, far, gate, upper, gate_in, up_in, down_in)
+        gate, upper, square, gate_in, up_in = early(place, own + above + below, inverse, w_gate, w_up)
+        act, far_0, far_1 = late(place, far, inverse, gate, upper, square, gate_in, up_in, w_down)
         relay_0, relay_1 = cross(far_0, 1, 1), cross(far_1, 1, -1)
-        own_0, own_1, above_0, above_1, below_0, below_1 = rest(place, act, down_in, far_0.shape)
+        own_0, own_1, above_0, above_1, below_0, below_1 = rest(place, act, w_down, far_0.shape)
         up_1 = cross(above_1, 1, 1)
         down_0 = cross(below_0, 1, -1)
         up_0 = cross((above_0.astype(f32) + relay_0.astype(f32)).astype(bf16), 1, 1)

time: 143 us -> 135 us (0.944)
  waiting for transfers between devices: 53.1 us -> 48.9 us
  starting transfers between devices: 44.4 us -> 41.9 us
  Pallas kernels: 26.7 us -> 24.3 us
    ppermute x18, waiting for transfers between devices: 41.5 us -> 32.8 us  [cross(): return lax.ppermute(x, ('pool', 'x', 'tp'), pairs)]
    ppermute x0 -> x2, waiting for transfers between devices: none -> 7.09 us  [the longest x1 7.09 us: shards(): others = lax.ppermute(couple, 'tp', [(i, i ^ 2) for i in range(RING)])]
    ppermute x9 -> x6, starting transfers between devices: 14.7 us -> 8.98 us  [along(): return lax.ppermute(x, axis, [(i, (i + by) % RING) for i in range(RING)])]
    pallas_call x2 -> x1, Pallas kernels: 15.4 us -> 10.6 us  [early(): pl.pallas_call(early_kernel, out_shape=[jax.ShapeDtypeStruct((count, n),...]
    ppermute x18, starting transfers between devices: 21.1 us -> 24.7 us  [cross(): return lax.ppermute(x, ('pool', 'x', 'tp'), pairs)]
    ppermute x9 -> x6, waiting for transfers between devices: 9.49 us -> 7.26 us  [along(): return lax.ppermute(x, axis, [(i, (i + by) % RING) for i in range(RING)])]
    ppermute x2, starting transfers between devices: 8.61 us -> 6.89 us  [swap_cores(): return lax.ppermute(x, 'pool', [(0, 1), (1, 0)])]
    pallas_call x1, Pallas kernels: 6.25 us -> 7.68 us  [rest(): pl.pallas_call(rest_kernel, out_shape=[jax.ShapeDtypeStruct(shape, bf16)]...]
  transfers between devices with their start and end apart: 29 -> 28, of which waited for: 18 -> 15; matrix products, arithmetic and copies ran while one was open for 5% -> 6% of each run, Pallas kernels for 15% -> 14%
where the time goes in v3:
time: 135 us
  waiting for transfers between devices  48.9 us (36%)
  starting transfers between devices  41.9 us (31%)
  Pallas kernels  24.3 us (18%)
  other arithmetic  9.89 us (7%)
  matrix products  5.21 us (4%)
  local copies, waits for them, and re-layouts  3.97 us (3%)
    ppermute x18, waiting for transfers between devices, cross(): return lax.ppermute(x, ('pool', 'x', 'tp'), pairs)  32.8 us
    ppermute x18, starting transfers between devices, cross(): return lax.ppermute(x, ('pool', 'x', 'tp'), pairs)  24.7 us
    pallas_call x1, Pallas kernels, early(): pl.pallas_call(early_kernel, out_shape=[jax.ShapeDtypeStruct((count, n),...  10.6 us
    ppermute x6, starting transfers between devices, along(): return lax.ppermute(x, axis, [(i, (i + by) % RING) for i in range(RING)])  8.98 us
    pallas_call x1, Pallas kernels, rest(): pl.pallas_call(rest_kernel, out_shape=[jax.ShapeDtypeStruct(shape, bf16)]...  7.68 us
    ppermute x6, waiting for transfers between devices, along(): return lax.ppermute(x, axis, [(i, (i + by) % RING) for i in range(RING)])  7.26 us
    ppermute x1, waiting for transfers between devices, shards(): others = lax.ppermute(couple, 'tp', [(i, i ^ 2) for i in range(RING)])  7.09 us
    ppermute x2, starting transfers between devices, swap_cores(): return lax.ppermute(x, 'pool', [(0, 1), (1, 0)])  6.89 us
  transfers between devices with their start and end apart: 28, of which 15 were waited for; matrix products, arithmetic and copies ran while one was open for 6% of the time, Pallas kernels for 14%

profile of v3, /device:TPU:1, one launch (start us, length us, event | category | flops | bytes accessed | tf_op | source)
XLA Modules:
  0.0 134.5 jit_solution(5715298858195118607)
XLA Ops:
  2.8 1.3 fusion.49
  4.6 2.3 %fusion.13 = f32[32,2,6,128]{3,2,1,0:T(8,128)S(1)} fusion(f32[32,2,6,128]{3,2,1,0:T(8,128)S(1)} %get-tuple-element.78, f32[32,2,128]{2,1,0:T(2,128)S(1)} %reshape.232, f32[32,2,6]{2,1,0:T(2,128)S(1)} %get-tuple-element.76, f32[32,2,6]{2,1,0:T(2,128)S(1)} %get-tuple-element.75, f32[32,2,6]{2,1,0:T(2,128)S(1)} %multiply_maximum_fusion, ...), kind=kOutput, calls=%fused_computation.14 | convolution fusion | flops 12828672 | bytes 2527744 | tf_op jit(solution)/shard_map/rghc,rcgo->rgho/dot_general | solution.py:42
  8.4 1.5 %collective-permute-start = (bf16[4,16,1536]{2,1,0:T(8,128)(2,1)S(1)}, bf16[4,16,1536]{2,1,0:T(8,128)(2,1)S(1)}, u32[]{:S(2)}, u32[]{:S(2)}) collective-permute-start(bf16[4,16,1536]{2,1,0:T(8,128)(2,1)S(1)} %get-tuple-element.74), channel_id=1, source_target_pairs={{0,64},{64,0},{1,65},{65,1},{2,66},{66,2},{3,67},{67,3},{4,68},{68... | collective-permute-start | bytes 589832 | tf_op jit(solution)/shard_map/ppermute | solution.py:53
  11.1 1.8 %collective-permute-start.1 = (bf16[32,1536]{1,0:T(8,128)(2,1)S(1)}, bf16[32,1536]{1,0:T(8,128)(2,1)S(1)}, u32[]{:S(2)}, u32[]{:S(2)}) collective-permute-start(bf16[32,1536]{1,0:T(8,128)(2,1)S(1)} %bitcast.95), channel_id=1, source_target_pairs={{0,16},{16,32},{32,48},{48,0},{1,17},{17,33},{33,49},{49,1},{2,18}... | collective-permute-start | bytes 294920 | tf_op jit(solution)/shard_map/ppermute | solution.py:49
  12.8 3.3 %collective-permute-start.2 = (bf16[32,1536]{1,0:T(8,128)(2,1)S(1)}, bf16[32,1536]{1,0:T(8,128)(2,1)S(1)}, u32[]{:S(2)}, u32[]{:S(2)}) collective-permute-start(bf16[32,1536]{1,0:T(8,128)(2,1)S(1)} %bitcast.94), channel_id=1, source_target_pairs={{0,32},{16,48},{32,0},{48,16},{1,33},{17,49},{33,1},{49,17},{2,34}... | collective-permute-start | bytes 294920 | tf_op jit(solution)/shard_map/ppermute | solution.py:49
  16.9 1.3 collective-permute-start.4
  18.3 2.5 %collective-permute-done.2 = bf16[32,1536]{1,0:T(8,128)(2,1)S(1)} collective-permute-done((bf16[32,1536]{1,0:T(8,128)(2,1)S(1)}, bf16[32,1536]{1,0:T(8,128)(2,1)S(1)}, u32[]{:S(2)}, u32[]{:S(2)}) %collective-permute-start.2) | collective-permute-done | bytes 98336 | tf_op jit(solution)/shard_map/ppermute | solution.py:49
  20.9 3.0 %collective-permute-start.5 = (bf16[128,1536]{1,0:T(8,128)(2,1)S(1)}, bf16[128,1536]{1,0:T(8,128)(2,1)S(1)}, u32[]{:S(2)}, u32[]{:S(2)}) collective-permute-start(bf16[128,1536]{1,0:T(8,128)(2,1)S(1)} %pad_maximum_fusion.2), channel_id=1, source_target_pairs={{0,8},{1,9},{2,10},{3,11},{4,12},{5,13},{6,14},{7,15},{8,0},{9,1},... | collective-permute-start | bytes 1179656 | tf_op jit(solution)/shard_map/ppermute | solution.py:63
  24.3 2.3 %collective-permute-start.7 = (bf16[128,1536]{1,0:T(8,128)(2,1)S(1)}, bf16[128,1536]{1,0:T(8,128)(2,1)S(1)}, u32[]{:S(2)}, u32[]{:S(2)}) collective-permute-start(bf16[128,1536]{1,0:T(8,128)(2,1)S(1)} %pad_maximum_fusion.2), channel_id=1, source_target_pairs={{0,12},{1,13},{2,14},{3,15},{4,0},{5,1},{6,2},{7,3},{8,4},{9,5},{1... | collective-permute-start | bytes 1179656 | tf_op jit(solution)/shard_map/ppermute | solution.py:63
  26.6 7.1 %collective-permute-done.6 = f32[2,1824]{1,0:T(2,128)S(1)} collective-permute-done((f32[2,1824]{1,0:T(2,128)S(1)}, f32[2,1824]{1,0:T(2,128)S(1)}, u32[]{:S(2)}, u32[]{:S(2)}) %collective-permute-start.6) | collective-permute-done | bytes 14624 | tf_op jit(solution)/shard_map/ppermute | solution.py:366
  35.1 1.7 %collective-permute-start.8 = (bf16[2,128,1536]{2,1,0:T(8,128)(2,1)S(1)}, bf16[2,128,1536]{2,1,0:T(8,128)(2,1)S(1)}, u32[]{:S(2)}, u32[]{:S(2)}) collective-permute-start(bf16[2,128,1536]{2,1,0:T(8,128)(2,1)S(1)} %pad_maximum_fusion.own_0), channel_id=1, source_target_pairs={{0,3},{1,0},{2,1},{3,2},{4,7},{5,4},{6,5},{7,6},{8,11},{9,8},{10,9... | collective-permute-start | bytes 2359304 | tf_op jit(solution)/shard_map/ppermute | solution.py:63
  38.6 7.6 %collective-permute-done.11.below_1 = bf16[2,128,1536]{2,1,0:T(8,128)(2,1)S(1)} collective-permute-done((bf16[2,128,1536]{2,1,0:T(8,128)(2,1)S(1)}, bf16[2,128,1536]{2,1,0:T(8,128)(2,1)S(1)}, u32[]{:S(2)}, u32[]{:S(2)}) %collective-permute-start.11) | collective-permute-done | bytes 786464 | tf_op jit(solution)/shard_map/ppermute | solution.py:63
  46.3 2.8 %collective-permute-start.9 = (bf16[2,128,1536]{2,1,0:T(8,128)(2,1)S(1)}, bf16[2,128,1536]{2,1,0:T(8,128)(2,1)S(1)}, u32[]{:S(2)}, u32[]{:S(2)}) collective-permute-start(bf16[2,128,1536]{2,1,0:T(8,128)(2,1)S(1)} %collective-permute-done.8.above_0), channel_id=1, source_target_pairs={{0,3},{1,0},{2,1},{3,2},{4,7},{5,4},{6,5},{7,6},{8,11},{9,8},{10,9... | collective-permute-start | bytes 2359304 | tf_op jit(solution)/shard_map/ppermute | solution.py:63
  49.1 5.6 %collective-permute-done.13.above_1 = bf16[2,128,1536]{2,1,0:T(8,128)(2,1)S(1)} collective-permute-done((bf16[2,128,1536]{2,1,0:T(8,128)(2,1)S(1)}, bf16[2,128,1536]{2,1,0:T(8,128)(2,1)S(1)}, u32[]{:S(2)}, u32[]{:S(2)}) %collective-permute-start.13) | collective-permute-done | bytes 786464 | tf_op jit(solution)/shard_map/ppermute | solution.py:63
  54.7 10.6 %early.1 = (f32[512,512]{1,0:T(8,128)S(1)}, f32[512,512]{1,0:T(8,128)S(1)}, f32[512,128]{1,0:T(8,128)S(1)}, bf16[6144,512]{1,0:T(8,128)(2,1)S(1)}, bf16[6144,512]{1,0:T(8,128)(2,1)S(1)}) custom-call(s32[2]{0:T(128)S(1)} %pad_add_fusion.place, bf16[2,128,1536]{2,1,0:T(8,128)(2,1)S(1)} %pad_maximum_fusion.own_0, ...), custom_call_target="tpu_custom_call" | custom-call | flops 4831838208 | bytes 17301504 | tf_op jit(solution)/shard_map/early/pallas_call | solution.py:255
  65.3 6.1 %late.1 = (bf16[512,512]{1,0:T(8,128)(2,1)S(1)}, bf16[2,128,1536]{2,1,0:T(8,128)(2,1)S(1)}, bf16[2,128,1536]{2,1,0:T(8,128)(2,1)S(1)}) custom-call(s32[2]{0:T(128)S(1)} %pad_add_fusion.place, bf16[2,128,1536]{2,1,0:T(8,128)(2,1)S(1)} %collective-permute-done.9.far_0, bf16[2,128,1536]{2,1,0:T(8,128)(2,1)S(1)} %collective-permute-done.12.far_1, ...), custom_call_target="tpu_custom_call" | custom-call | flops 2415919104 | bytes 3145728 | tf_op jit(solution)/shard_map/late/pallas_call | solution.py:278
  71.4 2.9 %collective-permute-start.19 = (bf16[2,128,1536]{2,1,0:T(8,128)(2,1)S(1)}, bf16[2,128,1536]{2,1,0:T(8,128)(2,1)S(1)}, u32[]{:S(2)}, u32[]{:S(2)}) collective-permute-start(bf16[2,128,1536]{2,1,0:T(8,128)(2,1)S(1)} %get-tuple-element.50), channel_id=1, source_target_pairs={{0,3},{1,0},{2,1},{3,2},{4,7},{5,4},{6,5},{7,6},{8,11},{9,8},{10,9... | collective-permute-start | bytes 2359304 | tf_op jit(solution)/shard_map/ppermute | solution.py:63
  74.3 7.7 %rest.1 = (bf16[2,128,1536]{2,1,0:T(8,128)(2,1)S(1)}, bf16[2,128,1536]{2,1,0:T(8,128)(2,1)S(1)}, bf16[2,128,1536]{2,1,0:T(8,128)(2,1)S(1)}, bf16[2,128,1536]{2,1...) custom-call(s32[2]{0:T(128)S(1)} %pad_add_fusion.place, ...), custom_call_target="tpu_custom_call" | custom-call | flops 2415919104 | bytes 11010048 | tf_op jit(solution)/shard_map/rest/pallas_call | solution.py:304
  82.0 2.7 %collective-permute-start.17 = (bf16[2,128,1536]{2,1,0:T(8,128)(2,1)S(1)}, bf16[2,128,1536]{2,1,0:T(8,128)(2,1)}, u32[]{:S(2)}, u32[]{:S(2)}) collective-permute-start(bf16[2,128,1536]{2,1,0:T(8,128)(2,1)S(1)} %get-tuple-element.46), channel_id=1, source_target_pairs={{0,3},{1,0},{2,1},{3,2},{4,7},{5,4},{6,5},{7,6},{8,11},{9,8},{10,9... | collective-permute-start | bytes 2359304 | tf_op jit(solution)/shard_map/ppermute | solution.py:63
  85.9 1.8 %collective-permute-start.20 = (bf16[2,128,1536]{2,1,0:T(8,128)(2,1)}, bf16[2,128,1536]{2,1,0:T(8,128)(2,1)}, u32[]{:S(2)}, u32[]{:S(2)}) collective-permute-start(bf16[2,128,1536]{2,1,0:T(8,128)(2,1)} %add_convert_fusion), channel_id=1, source_target_pairs={{0,3},{1,0},{2,1},{3,2},{4,7},{5,4},{6,5},{7,6},{8,11},{9,8},{10,9... | collective-permute-start | bytes 2359304 | tf_op jit(solution)/shard_map/ppermute | solution.py:63
  89.4 5.7 %collective-permute-done.18 = bf16[2,128,1536]{2,1,0:T(8,128)(2,1)} collective-permute-done((bf16[2,128,1536]{2,1,0:T(8,128)(2,1)}, bf16[2,128,1536]{2,1,0:T(8,128)(2,1)}, u32[]{:S(2)}, u32[]{:S(2)}) %collective-permute-start.18) | collective-permute-done | bytes 786464 | tf_op jit(solution)/shard_map/ppermute | solution.py:63
  95.1 7.1 %collective-permute-done.20 = bf16[2,128,1536]{2,1,0:T(8,128)(2,1)} collective-permute-done((bf16[2,128,1536]{2,1,0:T(8,128)(2,1)}, bf16[2,128,1536]{2,1,0:T(8,128)(2,1)}, u32[]{:S(2)}, u32[]{:S(2)}) %collective-permute-start.20) | collective-permute-done | bytes 786464 | tf_op jit(solution)/shard_map/ppermute | solution.py:63
  102.2 1.6 %fusion.19 = (bf16[128,1536]{1,0:T(8,128)(2,1)S(1)}, bf16[128,1536]{1,0:T(8,128)(2,1)S(1)}) fusion(bf16[2,128,1536]{2,1,0:T(8,128)(2,1)} %collective-permute-done.20, bf16[2,128,1536]{2,1,0:T(8,128)(2,1)} %collective-permute-done.18, bf16[2,128,1536]{2,1,0:T(8,128)(2,1)S(1)} %get-tuple-element.47), kind=kLoop, calls=%fused_computation.30 | loop fusion | flops 2359296 | bytes 3145728 | tf_op jit(solution)/shard_map/convert_element_type | solution.py:396
  103.9 2.9 %collective-permute-start.22 = (bf16[128,1536]{1,0:T(8,128)(2,1)S(1)}, bf16[128,1536]{1,0:T(8,128)(2,1)}, u32[]{:S(2)}, u32[]{:S(2)}) collective-permute-start(bf16[128,1536]{1,0:T(8,128)(2,1)S(1)} %get-tuple-element.62), channel_id=1, source_target_pairs={{0,8},{1,9},{2,10},{3,11},{4,12},{5,13},{6,14},{7,15},{8,0},{9,1},... | collective-permute-start | bytes 1179656 | tf_op jit(solution)/shard_map/ppermute | solution.py:63
  110.5 2.0 %collective-permute-done.22 = bf16[128,1536]{1,0:T(8,128)(2,1)} collective-permute-done((bf16[128,1536]{1,0:T(8,128)(2,1)S(1)}, bf16[128,1536]{1,0:T(8,128)(2,1)}, u32[]{:S(2)}, u32[]{:S(2)}) %collective-permute-start.22) | collective-permute-done | bytes 393248 | tf_op jit(solution)/shard_map/ppermute | solution.py:63
  112.5 4.5 %collective-permute-done.23 = bf16[128,1536]{1,0:T(8,128)(2,1)} collective-permute-done((bf16[128,1536]{1,0:T(8,128)(2,1)S(1)}, bf16[128,1536]{1,0:T(8,128)(2,1)}, u32[]{:S(2)}, u32[]{:S(2)}) %collective-permute-start.23) | collective-permute-done | bytes 393248 | tf_op jit(solution)/shard_map/ppermute | solution.py:63
  117.1 1.9 %fusion.16 = bf16[128,1536]{1,0:T(8,128)(2,1)S(1)} fusion(bf16[128,1536]{1,0:T(8,128)(2,1)} %collective-permute-done.23, bf16[128,1536]{1,0:T(8,128)(2,1)} %collective-permute-done.22, bf16[128,1536]{1,0:T(8,128)(2,1)} %collective-permute-done.21, bf16[2,128,1536]{2,1,0:T(8,128)(2,1)} %collective-permute-done.17, ...), kind=kLoop, calls=%fused_computation.18 | loop fusion | flops 2359296 | bytes 2752512 | tf_op jit(solution)/shard_map/convert_element_type | solution.py:399
  119.1 1.9 %collective-permute-start.24 = (bf16[2,16,1536]{2,1,0:T(8,128)(2,1)S(1)}, bf16[2,16,1536]{2,1,0:T(8,128)(2,1)S(1)}, u32[]{:S(2)}, u32[]{:S(2)}) collective-permute-start(bf16[2,16,1536]{2,1,0:T(8,128)(2,1)S(1)} %bitcast.100), channel_id=1, source_target_pairs={{0,48},{16,0},{32,16},{48,32},{1,49},{17,1},{33,17},{49,33},{2,50}... | collective-permute-start | bytes 294920 | tf_op jit(solution)/shard_map/ppermute | solution.py:49
  121.0 1.3 collective-permute-start.25
  122.3 1.3 collective-permute-done.24
  123.6 2.4 %collective-permute-done.25 = bf16[2,16,1536]{2,1,0:T(8,128)(2,1)S(1)} collective-permute-done((bf16[2,16,1536]{2,1,0:T(8,128)(2,1)S(1)}, bf16[2,16,1536]{2,1,0:T(8,128)(2,1)S(1)}, u32[]{:S(2)}, u32[]{:S(2)}) %collective-permute-start.25) | collective-permute-done | bytes 98336 | tf_op jit(solution)/shard_map/ppermute | solution.py:49
  127.1 5.4 %collective-permute-start.27 = (bf16[4,16,1536]{2,1,0:T(8,128)(2,1)S(1)}, bf16[4,16,1536]{2,1,0:T(8,128)(2,1)S(1)}, u32[]{:S(2)}, u32[]{:S(2)}) collective-permute-start(bf16[4,16,1536]{2,1,0:T(8,128)(2,1)S(1)} %get-tuple-element.64), channel_id=1, source_target_pairs={{0,64},{64,0},{1,65},{65,1},{2,66},{66,2},{3,67},{67,3},{4,68},{68... | collective-permute-start | bytes 589832 | tf_op jit(solution)/shard_map/ppermute | solution.py:53
  (110 shorter events, 20.3 us)
Async XLA Ops:
  0.0 4.5 %copy-start.3 = (bf16[32,256]{1,0:T(8,128)(2,1)S(1)}, bf16[32,256]{1,0:T(8,128)(2,1)}, u32[]{:S(2)}) copy-start(bf16[32,256]{1,0:T(8,128)(2,1)} %param.17) | copy-start | bytes 49156
  4.6 3.3 %copy-start.5 = (bf16[1536]{0:T(1024)(128)(2,1)S(1)}, bf16[1536]{0:T(1024)(128)(2,1)}, u32[]{:S(2)}) copy-start(bf16[1536]{0:T(1024)(128)(2,1)} %param.20) | copy-start | bytes 9220
  4.6 3.3 %copy-start.2 = (bf16[32,1536]{1,0:T(8,128)(2,1)S(1)}, bf16[32,1536]{1,0:T(8,128)(2,1)}, u32[]{:S(2)}) copy-start(bf16[32,1536]{1,0:T(8,128)(2,1)} %param.19) | copy-start | bytes 294916
  8.4 2.6 %collective-permute-start = (bf16[4,16,1536]{2,1,0:T(8,128)(2,1)S(1)}, bf16[4,16,1536]{2,1,0:T(8,128)(2,1)S(1)}, u32[]{:S(2)}, u32[]{:S(2)}) collective-permute-start(bf16[4,16,1536]{2,1,0:T(8,128)(2,1)S(1)} %get-tuple-element.74), channel_id=1, source_target_pairs={{0,64},{64,0},{1,65},{65,1},{2,66},{66,2},{3,67},{67,3},{4,68},{68... | collective-permute-start | bytes 589832 | tf_op jit(solution)/shard_map/ppermute | solution.py:53
  11.1 7.2 %collective-permute-start.1 = (bf16[32,1536]{1,0:T(8,128)(2,1)S(1)}, bf16[32,1536]{1,0:T(8,128)(2,1)S(1)}, u32[]{:S(2)}, u32[]{:S(2)}) collective-permute-start(bf16[32,1536]{1,0:T(8,128)(2,1)S(1)} %bitcast.95), channel_id=1, source_target_pairs={{0,16},{16,32},{32,48},{48,0},{1,17},{17,33},{33,49},{49,1},{2,18}... | collective-permute-start | bytes 294920 | tf_op jit(solution)/shard_map/ppermute | solution.py:49
  12.8 8.0 %collective-permute-start.2 = (bf16[32,1536]{1,0:T(8,128)(2,1)S(1)}, bf16[32,1536]{1,0:T(8,128)(2,1)S(1)}, u32[]{:S(2)}, u32[]{:S(2)}) collective-permute-start(bf16[32,1536]{1,0:T(8,128)(2,1)S(1)} %bitcast.94), channel_id=1, source_target_pairs={{0,32},{16,48},{32,0},{48,16},{1,33},{17,49},{33,1},{49,17},{2,34}... | collective-permute-start | bytes 294920 | tf_op jit(solution)/shard_map/ppermute | solution.py:49
  16.1 4.7 %collective-permute-start.3 = (bf16[32,1536]{1,0:T(8,128)(2,1)S(1)}, bf16[32,1536]{1,0:T(8,128)(2,1)S(1)}, u32[]{:S(2)}, u32[]{:S(2)}) collective-permute-start(bf16[32,1536]{1,0:T(8,128)(2,1)S(1)} %bitcast.93), channel_id=1, source_target_pairs={{0,48},{16,0},{32,16},{48,32},{1,49},{17,1},{33,17},{49,33},{2,50}... | collective-permute-start | bytes 294920 | tf_op jit(solution)/shard_map/ppermute | solution.py:49
  16.9 3.9 %collective-permute-start.4 = (f32[1824]{0:T(1024)S(1)}, f32[1824]{0:T(1024)S(1)}, u32[]{:S(2)}, u32[]{:S(2)}) collective-permute-start(f32[1824]{0:T(1024)S(1)} %pad_maximum_fusion.9), channel_id=1, source_target_pairs={{0,1},{1,0},{2,3},{3,2},{4,5},{5,4},{6,7},{7,6},{8,9},{9,8},{10,11... | collective-permute-start | bytes 21896 | tf_op jit(solution)/shard_map/ppermute | solution.py:362
  20.9 12.8 %collective-permute-start.5 = (bf16[128,1536]{1,0:T(8,128)(2,1)S(1)}, bf16[128,1536]{1,0:T(8,128)(2,1)S(1)}, u32[]{:S(2)}, u32[]{:S(2)}) collective-permute-start(bf16[128,1536]{1,0:T(8,128)(2,1)S(1)} %pad_maximum_fusion.2), channel_id=1, source_target_pairs={{0,8},{1,9},{2,10},{3,11},{4,12},{5,13},{6,14},{7,15},{8,0},{9,1},... | collective-permute-start | bytes 1179656 | tf_op jit(solution)/shard_map/ppermute | solution.py:63
  23.9 9.9 %collective-permute-start.10 = (bf16[128,1536]{1,0:T(8,128)(2,1)S(1)}, bf16[128,1536]{1,0:T(8,128)(2,1)S(1)}, u32[]{:S(2)}, u32[]{:S(2)}) collective-permute-start(bf16[128,1536]{1,0:T(8,128)(2,1)S(1)} %pad_maximum_fusion.2), channel_id=1, source_target_pairs={{0,4},{1,5},{2,6},{3,7},{4,8},{5,9},{6,10},{7,11},{8,12},{9,13},{1... | collective-permute-start | bytes 1179656 | tf_op jit(solution)/shard_map/ppermute | solution.py:63
  24.3 10.7 %collective-permute-start.7 = (bf16[128,1536]{1,0:T(8,128)(2,1)S(1)}, bf16[128,1536]{1,0:T(8,128)(2,1)S(1)}, u32[]{:S(2)}, u32[]{:S(2)}) collective-permute-start(bf16[128,1536]{1,0:T(8,128)(2,1)S(1)} %pad_maximum_fusion.2), channel_id=1, source_target_pairs={{0,12},{1,13},{2,14},{3,15},{4,0},{5,1},{6,2},{7,3},{8,4},{9,5},{1... | collective-permute-start | bytes 1179656 | tf_op jit(solution)/shard_map/ppermute | solution.py:63
  26.6 7.1 %collective-permute-start.6 = (f32[2,1824]{1,0:T(2,128)S(1)}, f32[2,1824]{1,0:T(2,128)S(1)}, u32[]{:S(2)}, u32[]{:S(2)}) collective-permute-start(f32[2,1824]{1,0:T(2,128)S(1)} %pad_maximum_fusion.7), channel_id=1, source_target_pairs={{0,2},{1,3},{2,0},{3,1},{4,6},{5,7},{6,4},{7,5},{8,10},{9,11},{10,... | collective-permute-start | bytes 43784 | tf_op jit(solution)/shard_map/ppermute | solution.py:366
  33.8 12.4 %collective-permute-start.11 = (bf16[2,128,1536]{2,1,0:T(8,128)(2,1)S(1)}, bf16[2,128,1536]{2,1,0:T(8,128)(2,1)S(1)}, u32[]{:S(2)}, u32[]{:S(2)}) collective-permute-start(bf16[2,128,1536]{2,1,0:T(8,128)(2,1)S(1)} %pad_maximum_fusion.1.own_1), channel_id=1, source_target_pairs={{0,1},{1,2},{2,3},{3,0},{4,5},{5,6},{6,7},{7,4},{8,9},{9,10},{10,1... | collective-permute-start | bytes 2359304 | tf_op jit(solution)/shard_map/ppermute | solution.py:63
  35.1 11.2 %collective-permute-start.8 = (bf16[2,128,1536]{2,1,0:T(8,128)(2,1)S(1)}, bf16[2,128,1536]{2,1,0:T(8,128)(2,1)S(1)}, u32[]{:S(2)}, u32[]{:S(2)}) collective-permute-start(bf16[2,128,1536]{2,1,0:T(8,128)(2,1)S(1)} %pad_maximum_fusion.own_0), channel_id=1, source_target_pairs={{0,3},{1,0},{2,1},{3,2},{4,7},{5,4},{6,5},{7,6},{8,11},{9,8},{10,9... | collective-permute-start | bytes 2359304 | tf_op jit(solution)/shard_map/ppermute | solution.py:63
  36.9 17.8 %collective-permute-start.13 = (bf16[2,128,1536]{2,1,0:T(8,128)(2,1)S(1)}, bf16[2,128,1536]{2,1,0:T(8,128)(2,1)S(1)}, u32[]{:S(2)}, u32[]{:S(2)}) collective-permute-start(bf16[2,128,1536]{2,1,0:T(8,128)(2,1)S(1)} %pad_maximum_fusion.1.own_1), channel_id=1, source_target_pairs={{0,3},{1,0},{2,1},{3,2},{4,7},{5,4},{6,5},{7,6},{8,11},{9,8},{10,9... | collective-permute-start | bytes 2359304 | tf_op jit(solution)/shard_map/ppermute | solution.py:63
  38.2 16.6 %collective-permute-start.14 = (bf16[2,128,1536]{2,1,0:T(8,128)(2,1)S(1)}, bf16[2,128,1536]{2,1,0:T(8,128)(2,1)S(1)}, u32[]{:S(2)}, u32[]{:S(2)}) collective-permute-start(bf16[2,128,1536]{2,1,0:T(8,128)(2,1)S(1)} %pad_maximum_fusion.own_0), channel_id=1, source_target_pairs={{0,1},{1,2},{2,3},{3,0},{4,5},{5,6},{6,7},{7,4},{8,9},{9,10},{10,1... | collective-permute-start | bytes 2359304 | tf_op jit(solution)/shard_map/ppermute | solution.py:63
  46.3 19.0 %collective-permute-start.12 = (bf16[2,128,1536]{2,1,0:T(8,128)(2,1)S(1)}, bf16[2,128,1536]{2,1,0:T(8,128)(2,1)S(1)}, u32[]{:S(2)}, u32[]{:S(2)}) collective-permute-start(bf16[2,128,1536]{2,1,0:T(8,128)(2,1)S(1)} %collective-permute-done.11.below_1), channel_id=1, source_target_pairs={{0,1},{1,2},{2,3},{3,0},{4,5},{5,6},{6,7},{7,4},{8,9},{9,10},{10,1... | collective-permute-start | bytes 2359304 | tf_op jit(solution)/shard_map/ppermute | solution.py:63
  46.3 19.0 %collective-permute-start.9 = (bf16[2,128,1536]{2,1,0:T(8,128)(2,1)S(1)}, bf16[2,128,1536]{2,1,0:T(8,128)(2,1)S(1)}, u32[]{:S(2)}, u32[]{:S(2)}) collective-permute-start(bf16[2,128,1536]{2,1,0:T(8,128)(2,1)S(1)} %collective-permute-done.8.above_0), channel_id=1, source_target_pairs={{0,3},{1,0},{2,1},{3,2},{4,7},{5,4},{6,5},{7,6},{8,11},{9,8},{10,9... | collective-permute-start | bytes 2359304 | tf_op jit(solution)/shard_map/ppermute | solution.py:63
  71.4 13.4 %collective-permute-start.19 = (bf16[2,128,1536]{2,1,0:T(8,128)(2,1)S(1)}, bf16[2,128,1536]{2,1,0:T(8,128)(2,1)S(1)}, u32[]{:S(2)}, u32[]{:S(2)}) collective-permute-start(bf16[2,128,1536]{2,1,0:T(8,128)(2,1)S(1)} %get-tuple-element.50), channel_id=1, source_target_pairs={{0,3},{1,0},{2,1},{3,2},{4,7},{5,4},{6,5},{7,6},{8,11},{9,8},{10,9... | collective-permute-start | bytes 2359304 | tf_op jit(solution)/shard_map/ppermute | solution.py:63
  74.3 13.5 %collective-permute-start.15 = (bf16[2,128,1536]{2,1,0:T(8,128)(2,1)S(1)}, bf16[2,128,1536]{2,1,0:T(8,128)(2,1)S(1)}, u32[]{:S(2)}, u32[]{:S(2)}) collective-permute-start(bf16[2,128,1536]{2,1,0:T(8,128)(2,1)S(1)} %get-tuple-element.45), channel_id=1, source_target_pairs={{0,1},{1,2},{2,3},{3,0},{4,5},{5,6},{6,7},{7,4},{8,9},{9,10},{10,1... | collective-permute-start | bytes 2359304 | tf_op jit(solution)/shard_map/ppermute | solution.py:63
  81.9 13.2 %collective-permute-start.18 = (bf16[2,128,1536]{2,1,0:T(8,128)(2,1)}, bf16[2,128,1536]{2,1,0:T(8,128)(2,1)}, u32[]{:S(2)}, u32[]{:S(2)}) collective-permute-start(bf16[2,128,1536]{2,1,0:T(8,128)(2,1)} %get-tuple-element.48), channel_id=1, source_target_pairs={{0,1},{1,2},{2,3},{3,0},{4,5},{5,6},{6,7},{7,4},{8,9},{9,10},{10,1... | collective-permute-start | bytes 2359304 | tf_op jit(solution)/shard_map/ppermute | solution.py:63
  82.0 25.5 %collective-permute-start.17 = (bf16[2,128,1536]{2,1,0:T(8,128)(2,1)S(1)}, bf16[2,128,1536]{2,1,0:T(8,128)(2,1)}, u32[]{:S(2)}, u32[]{:S(2)}) collective-permute-start(bf16[2,128,1536]{2,1,0:T(8,128)(2,1)S(1)} %get-tuple-element.46), channel_id=1, source_target_pairs={{0,3},{1,0},{2,1},{3,2},{4,7},{5,4},{6,5},{7,6},{8,11},{9,8},{10,9... | collective-permute-start | bytes 2359304 | tf_op jit(solution)/shard_map/ppermute | solution.py:63
  85.9 16.4 %collective-permute-start.20 = (bf16[2,128,1536]{2,1,0:T(8,128)(2,1)}, bf16[2,128,1536]{2,1,0:T(8,128)(2,1)}, u32[]{:S(2)}, u32[]{:S(2)}) collective-permute-start(bf16[2,128,1536]{2,1,0:T(8,128)(2,1)} %add_convert_fusion), channel_id=1, source_target_pairs={{0,3},{1,0},{2,1},{3,2},{4,7},{5,4},{6,5},{7,6},{8,11},{9,8},{10,9... | collective-permute-start | bytes 2359304 | tf_op jit(solution)/shard_map/ppermute | solution.py:63
  88.8 18.8 %collective-permute-start.16 = (bf16[2,128,1536]{2,1,0:T(8,128)(2,1)}, bf16[2,128,1536]{2,1,0:T(8,128)(2,1)}, u32[]{:S(2)}, u32[]{:S(2)}) collective-permute-start(bf16[2,128,1536]{2,1,0:T(8,128)(2,1)} %add_convert_fusion.1), channel_id=1, source_target_pairs={{0,1},{1,2},{2,3},{3,0},{4,5},{5,6},{6,7},{7,4},{8,9},{9,10},{10,1... | collective-permute-start | bytes 2359304 | tf_op jit(solution)/shard_map/ppermute | solution.py:63
  103.9 8.6 %collective-permute-start.22 = (bf16[128,1536]{1,0:T(8,128)(2,1)S(1)}, bf16[128,1536]{1,0:T(8,128)(2,1)}, u32[]{:S(2)}, u32[]{:S(2)}) collective-permute-start(bf16[128,1536]{1,0:T(8,128)(2,1)S(1)} %get-tuple-element.62), channel_id=1, source_target_pairs={{0,8},{1,9},{2,10},{3,11},{4,12},{5,13},{6,14},{7,15},{8,0},{9,1},... | collective-permute-start | bytes 1179656 | tf_op jit(solution)/shard_map/ppermute | solution.py:63
  106.8 10.2 %collective-permute-start.23 = (bf16[128,1536]{1,0:T(8,128)(2,1)S(1)}, bf16[128,1536]{1,0:T(8,128)(2,1)}, u32[]{:S(2)}, u32[]{:S(2)}) collective-permute-start(bf16[128,1536]{1,0:T(8,128)(2,1)S(1)} %get-tuple-element.61), channel_id=1, source_target_pairs={{0,12},{1,13},{2,14},{3,15},{4,0},{5,1},{6,2},{7,3},{8,4},{9,5},{1... | collective-permute-start | bytes 1179656 | tf_op jit(solution)/shard_map/ppermute | solution.py:63
  108.8 8.3 %collective-permute-start.21 = (bf16[128,1536]{1,0:T(8,128)(2,1)S(1)}, bf16[128,1536]{1,0:T(8,128)(2,1)}, u32[]{:S(2)}, u32[]{:S(2)}) collective-permute-start(bf16[128,1536]{1,0:T(8,128)(2,1)S(1)} %fusion.17), channel_id=1, source_target_pairs={{0,4},{1,5},{2,6},{3,7},{4,8},{5,9},{6,10},{7,11},{8,12},{9,13},{1... | collective-permute-start | bytes 1179656 | tf_op jit(solution)/shard_map/ppermute | solution.py:63
  117.1 17.4 %copy-start.1 = (bf16[32,128,256]{2,1,0:T(8,128)(2,1)S(1)}, bf16[32,128,256]{2,1,0:T(8,128)(2,1)}, u32[]{:S(2)}) copy-start(bf16[32,128,256]{2,1,0:T(8,128)(2,1)} %param.14) | copy-start | bytes 6291460
  119.1 4.5 %collective-permute-start.24 = (bf16[2,16,1536]{2,1,0:T(8,128)(2,1)S(1)}, bf16[2,16,1536]{2,1,0:T(8,128)(2,1)S(1)}, u32[]{:S(2)}, u32[]{:S(2)}) collective-permute-start(bf16[2,16,1536]{2,1,0:T(8,128)(2,1)S(1)} %bitcast.100), channel_id=1, source_target_pairs={{0,48},{16,0},{32,16},{48,32},{1,49},{17,1},{33,17},{49,33},{2,50}... | collective-permute-start | bytes 294920 | tf_op jit(solution)/shard_map/ppermute | solution.py:49
  121.0 5.0 %collective-permute-start.25 = (bf16[2,16,1536]{2,1,0:T(8,128)(2,1)S(1)}, bf16[2,16,1536]{2,1,0:T(8,128)(2,1)S(1)}, u32[]{:S(2)}, u32[]{:S(2)}) collective-permute-start(bf16[2,16,1536]{2,1,0:T(8,128)(2,1)S(1)} %bitcast.98), channel_id=1, source_target_pairs={{0,32},{16,48},{32,0},{48,16},{1,33},{17,49},{33,1},{49,17},{2,34}... | collective-permute-start | bytes 294920 | tf_op jit(solution)/shard_map/ppermute | solution.py:49
  122.2 4.8 %collective-permute-start.26 = (bf16[2,16,1536]{2,1,0:T(8,128)(2,1)S(1)}, bf16[2,16,1536]{2,1,0:T(8,128)(2,1)S(1)}, u32[]{:S(2)}, u32[]{:S(2)}) collective-permute-start(bf16[2,16,1536]{2,1,0:T(8,128)(2,1)S(1)} %bitcast.96), channel_id=1, source_target_pairs={{0,16},{16,32},{32,48},{48,0},{1,17},{17,33},{33,49},{49,1},{2,18}... | collective-permute-start | bytes 294920 | tf_op jit(solution)/shard_map/ppermute | solution.py:49
  127.1 6.5 %collective-permute-start.27 = (bf16[4,16,1536]{2,1,0:T(8,128)(2,1)S(1)}, bf16[4,16,1536]{2,1,0:T(8,128)(2,1)S(1)}, u32[]{:S(2)}, u32[]{:S(2)}) collective-permute-start(bf16[4,16,1536]{2,1,0:T(8,128)(2,1)S(1)} %get-tuple-element.64), channel_id=1, source_target_pairs={{0,64},{64,0},{1,65},{65,1},{2,66},{66,2},{3,67},{67,3},{4,68},{68... | collective-permute-start | bytes 589832 | tf_op jit(solution)/shard_map/ppermute | solution.py:53
  (3 other events, 8.3 us)

commit v4 on v3

--- a/solution.py
+++ b/solution.py
@@ -87,16 +87,11 @@
     square[position * block : (position + 1) * block, :] += total
 
 
-def early_kernel(
-    place, own_0, own_1, above_0, above_1, below_0, below_1, inverse, w_gate, w_up,
+def add_products(
+    core, me, arrived, more, inverse, w_gate, w_up,
     gate, upper, square, gate_in, up_in, rows, sem, gate_sem, up_sem,
 ):
-    core, me = place[0], place[1]
     _, _, block, features = rows.shape
-    arrived = {0: (own_0, own_1), 1: (above_0, above_1), 3: (below_0, below_1)}
-    gate[...] = jnp.zeros_like(gate)
-    upper[...] = jnp.zeros_like(upper)
-    square[...] = jnp.zeros_like(square)
 
     def weights(quarter):
         cut = turned(me, quarter, features)
@@ -109,10 +104,10 @@
         @pl.when(core == flipped)
         def _():
             work = dict(pieces_of(flipped, arrived))
-            order = list(work) + [q for q in range(RING) if q not in work]
+            order = list(work) + [q for q in more if q not in work]
 
             def begin(step):
-                if step < RING:
+                if step < len(order):
                     quarter = order[step]
                     for p, source in work.get(quarter, ()):
                         pltpu.make_async_copy(source, rows.at[quarter, p], sem.at[quarter, p]).start()
@@ -130,9 +125,9 @@
                 begin(step + 2)
                 if not blocks:
                     continue
-                number = len(blocks)
-                some = pl.ds(0, number * block)
-                held = rows[quarter, :number].reshape(number * block, features)
+                low, number = blocks[0][0], len(blocks)
+                some = pl.ds(low * block, number * block)
+                held = rows[quarter, low : low + number].reshape(number * block, features)
                 cut = turned(me, quarter, features)
                 gate[some, :] += jnp.dot(held, gate_in[cut, :], preferred_element_type=f32)
                 upper[some, :] += jnp.dot(held, up_in[cut, :], preferred_element_type=f32)
@@ -140,13 +135,35 @@
                     add_squares(square, rows.at[quarter, p], p, inverse.at[quarter])
 
 
+def first_kernel(place, own_0, own_1, inverse, w_gate, w_up, gate, upper, square, gate_in, up_in, *scratch):
+    gate[...] = jnp.zeros_like(gate)
+    upper[...] = jnp.zeros_like(upper)
+    square[...] = jnp.zeros_like(square)
+    add_products(
+        place[0], place[1], {0: (own_0, own_1)}, (), inverse, w_gate, w_up,
+        gate, upper, square, gate_in, up_in, *scratch,
+    )
+
+
+def early_kernel(
+    place, above_0, above_1, below_0, below_1, gate_0, up_0, square_0, inverse, w_gate, w_up,
+    gate, upper, square, gate_in, up_in, *scratch,
+):
+    gate[...] = gate_0[...]
+    upper[...] = up_0[...]
+    square[...] = square_0[...]
+    add_products(
+        place[0], place[1], {1: (above_0, above_1), 3: (below_0, below_1)}, (2,), inverse, w_gate, w_up,
+        gate, upper, square, gate_in, up_in, *scratch,
+    )
+
+
 def late_kernel(
     place, far_0, far_1, inverse, gate_in, up_in, square_in, w_gate, w_up, w_down,
-    act, out_0, out_1, rows, gate, upper, square, downs, sem, down_sem,
+    act, out_0, out_1, gate, upper, square, downs, down_sem,
 ):
     core, me = place[0], place[1]
-    _, block, features = rows.shape
-    count = RING * block
+    _, block, features = far_0.shape
     halves, outs = (far_0, far_1), (out_0, out_1)
     last = pl.ds((RING - 1) * block, block)
 
@@ -156,33 +173,35 @@
     for flipped in range(2):
         @pl.when(core == flipped)
         def _():
-            for p in range(RING):
-                inner = p if flipped else ORDER[p]
-                pltpu.make_async_copy(halves[inner // 2].at[inner % 2], rows.at[p], sem.at[p]).start()
             for quarter in range(RING) if flipped else (2,):
                 fetch(quarter).start()
 
-    gate[...] = gate_in[...]
-    upper[...] = up_in[...]
     square[...] = square_in[...]
-    for p in range(RING):
-        pltpu.make_async_copy(far_0.at[0], rows.at[p], sem.at[p]).wait()
 
     @pl.when(core == 0)
     def _():
-        held = rows[...].reshape(count, features)
-        gate[...] += jnp.dot(held, w_gate[turned(me, 2, features), :], preferred_element_type=f32)
-        upper[...] += jnp.dot(held, w_up[turned(me, 2, features), :], preferred_element_type=f32)
-        for p in range(RING):
-            add_squares(square, rows.at[p], p, inverse.at[2])
+        cut = turned(me, 2, features)
+        for half in range(2):
+            held = halves[half][...].reshape(2 * block, features)
+            more_gate = jnp.dot(held, w_gate[cut, :], preferred_element_type=f32)
+            more_up = jnp.dot(held, w_up[cut, :], preferred_element_type=f32)
+            for i in range(2):
+                p = ORDER.index(2 * half + i)
+                some = pl.ds(p * block, block)
+                gate[some, :] = gate_in[some, :] + more_gate[i * block : (i + 1) * block]
+                upper[some, :] = up_in[some, :] + more_up[i * block : (i + 1) * block]
+                add_squares(square, halves[half].at[i], p, inverse.at[2])
 
     @pl.when(core == 1)
     def _():
-        @pl.loop(0, RING)
-        def _(quarter):
-            gate[last, :] += jnp.dot(rows[quarter], w_gate[turned(me, quarter, features), :], preferred_element_type=f32)
-            upper[last, :] += jnp.dot(rows[quarter], w_up[turned(me, quarter, features), :], preferred_element_type=f32)
-            add_squares(square, rows.at[quarter], RING - 1, inverse.at[quarter])
+        gate[...] = gate_in[...]
+        upper[...] = up_in[...]
+        for quarter in range(RING):
+            cut = turned(me, quarter, features)
+            piece = halves[quarter // 2].at[quarter % 2]
+            gate[last, :] += jnp.dot(piece[...], w_gate[cut, :], preferred_element_type=f32)
+            upper[last, :] += jnp.dot(piece[...], w_up[cut, :], preferred_element_type=f32)
+            add_squares(square, piece, RING - 1, inverse.at[quarter])
 
     mean = jnp.sum(square[...], -1, keepdims=True) / (RING * features)
     scale = lax.rsqrt(mean + 1e-05)
@@ -247,27 +266,31 @@
     return pl.CostEstimate(flops=2 * macs, bytes_accessed=moved, transcendentals=raised)
 
 
-def early(place, pieces, inverse, w_gate, w_up):
+def weighed(kernel, name, keep, place, pieces, begun, inverse, w_gate, w_up):
     _, block, features = pieces[0].shape
     units = w_gate.shape[1]
     count = RING * block
     weights = [pltpu.with_memory_space_constraint(w, pltpu.HBM) for w in (w_gate, w_up)]
+    inside = [pltpu.VMEM(w.shape, bf16) for w in weights]
     return pl.pallas_call(
-        early_kernel,
-        out_shape=[jax.ShapeDtypeStruct((count, n), f32) for n in (units, units, 128)]
-        + [pltpu.VMEM(w.shape, bf16) for w in weights],
-        in_specs=[SCALARS] + [ANYWHERE] * 6 + [INSIDE] + [pl.BlockSpec(memory_space=pltpu.HBM)] * 2,
-        out_specs=[INSIDE] * 5,
-        scratch_shapes=[
+        kernel,
+        out_shape=[jax.ShapeDtypeStruct((count, n), f32) for n in (units, units, 128)] + (inside if keep else []),
+        in_specs=[SCALARS] + [ANYWHERE] * len(pieces) + [INSIDE] * (len(begun) + 1)
+        + [pl.BlockSpec(memory_space=pltpu.HBM)] * 2,
+        out_specs=[INSIDE] * (5 if keep else 3),
+        scratch_shapes=([] if keep else inside)
+        + [
             pltpu.VMEM((RING, RING, block, features), bf16),
             pltpu.SemaphoreType.DMA((RING, RING)),
             pltpu.SemaphoreType.DMA((RING,)),
             pltpu.SemaphoreType.DMA((RING,)),
         ],
-        compiler_params=pltpu.CompilerParams(vmem_limit_bytes=16 * MIB),
-        cost_estimate=cost(3 * count * features * units * 2, 3 * count * features * 2 + 4 * w_gate.size),
-        name="early",
-    )(place, *pieces, inverse, *weights)
+        compiler_params=pltpu.CompilerParams(vmem_limit_bytes=(16 if keep else 28) * MIB),
+        cost_estimate=cost(
+            len(pieces) // 2 * count * features * units * 2, len(pieces) * count * features + 4 * w_gate.size
+        ),
+        name=name,
+    )(place, *pieces, *begun, inverse, *weights)
 
 
 def late(place, far, inverse, gate, upper, square, w_gate, w_up, w_down):
@@ -278,15 +301,13 @@
     return pl.pallas_call(
         late_kernel,
         out_shape=[jax.ShapeDtypeStruct((count, units), bf16), half, half],
-        in_specs=[SCALARS] + [ANYWHERE] * 2 + [INSIDE] * 6 + [pl.BlockSpec(memory_space=pltpu.HBM)],
+        in_specs=[SCALARS] + [INSIDE] * 8 + [pl.BlockSpec(memory_space=pltpu.HBM)],
         out_specs=[INSIDE] * 3,
         scratch_shapes=[
-            pltpu.VMEM((RING, block, features), bf16),
             pltpu.VMEM((count, units), f32),
             pltpu.VMEM((count, units), f32),
             pltpu.VMEM((count, 128), f32),
             pltpu.VMEM((RING, units, features), bf16),
-            pltpu.SemaphoreType.DMA((RING,)),
             pltpu.SemaphoreType.DMA((RING,)),
         ],
         compiler_params=pltpu.CompilerParams(vmem_limit_bytes=20 * MIB),
@@ -380,8 +401,12 @@
         for half in range(2):
             above[half] = cross(own[half], 1, -1)
             below[half] = cross(own[half], 1, 1)
+        begun = weighed(first_kernel, "first", False, place, own, [], inverse, w_gate, w_up)
+        begun, above[1] = lax.optimization_barrier((begun, above[1]))
         far = [cross(above[0], 1, -1), cross(below[1], 1, 1)]
-        gate, upper, square, gate_in, up_in = early(place, own + above + below, inverse, w_gate, w_up)
+        gate, upper, square, gate_in, up_in = weighed(
+            early_kernel, "early", True, place, above + below, begun, inverse, w_gate, w_up
+        )
         act, far_0, far_1 = late(place, far, inverse, gate, upper, square, gate_in, up_in, w_down)
         relay_0, relay_1 = cross(far_0, 1, 1), cross(far_1, 1, -1)
         own_0, own_1, above_0, above_1, below_0, below_1 = rest(place, act, w_down, far_0.shape)

time: 135 us -> 132 us (0.978)
  waiting for transfers between devices: 48.9 us -> 43.1 us
  Pallas kernels: 24.3 us -> 27.3 us
    ppermute x18, waiting for transfers between devices: 32.8 us -> 27.1 us  [cross(): return lax.ppermute(x, ('pool', 'x', 'tp'), pairs)]
    pallas_call x1 -> x2, Pallas kernels: 10.6 us -> 15.2 us  [weighed(): pl.pallas_call(kernel, out_shape=[jax.ShapeDtypeStruct((count, n), f32) f...]
    pallas_call x1, Pallas kernels: 6.06 us -> 4.45 us  [late(): pl.pallas_call(late_kernel, out_shape=[jax.ShapeDtypeStruct((count, units...]
  transfers between devices with their start and end apart: 28 -> 28, of which waited for: 15 -> 13; matrix products, arithmetic and copies ran while one was open for 6% -> 6% of each run, Pallas kernels for 14% -> 17%
where the time goes in v4:
time: 132 us
  waiting for transfers between devices  43.1 us (33%)
  starting transfers between devices  41.8 us (32%)
  Pallas kernels  27.3 us (21%)
  other arithmetic  9.94 us (8%)
  matrix products  5.22 us (4%)
  local copies, waits for them, and re-layouts  3.97 us (3%)
    ppermute x18, waiting for transfers between devices, cross(): return lax.ppermute(x, ('pool', 'x', 'tp'), pairs)  27.1 us
    ppermute x18, starting transfers between devices, cross(): return lax.ppermute(x, ('pool', 'x', 'tp'), pairs)  23.4 us
    pallas_call x2, Pallas kernels, weighed(): pl.pallas_call(kernel, out_shape=[jax.ShapeDtypeStruct((count, n), f32) f...  15.2 us
    ppermute x6, starting transfers between devices, along(): return lax.ppermute(x, axis, [(i, (i + by) % RING) for i in range(RING)])  9.15 us
    ppermute x2, starting transfers between devices, swap_cores(): return lax.ppermute(x, 'pool', [(0, 1), (1, 0)])  7.85 us
    pallas_call x1, Pallas kernels, rest(): pl.pallas_call(rest_kernel, out_shape=[jax.ShapeDtypeStruct(shape, bf16)]...  7.69 us
    ppermute x6, waiting for transfers between devices, along(): return lax.ppermute(x, axis, [(i, (i + by) % RING) for i in range(RING)])  7.17 us
    ppermute x1, waiting for transfers between devices, shards(): others = lax.ppermute(couple, 'tp', [(i, i ^ 2) for i in range(RING)])  7.09 us
  transfers between devices with their start and end apart: 28, of which 13 were waited for; matrix products, arithmetic and copies ran while one was open for 6% of the time, Pallas kernels for 17%

profile of v4, /device:TPU:1, one launch (start us, length us, event | category | flops | bytes accessed | tf_op | source)
XLA Modules:
  0.0 131.7 jit_solution(16942035292266329231)
XLA Ops:
  2.8 1.3 fusion.49
  4.6 2.3 %fusion.13 = f32[32,2,6,128]{3,2,1,0:T(8,128)S(1)} fusion(f32[32,2,6,128]{3,2,1,0:T(8,128)S(1)} %get-tuple-element.92, f32[32,2,128]{2,1,0:T(2,128)S(1)} %reshape.232, f32[32,2,6]{2,1,0:T(2,128)S(1)} %get-tuple-element.90, f32[32,2,6]{2,1,0:T(2,128)S(1)} %get-tuple-element.89, f32[32,2,6]{2,1,0:T(2,128)S(1)} %multiply_maximum_fusion, ...), kind=kOutput, calls=%fused_computation.14 | convolution fusion | flops 12828672 | bytes 2527744 | tf_op jit(solution)/shard_map/rghc,rcgo->rgho/dot_general | solution.py:42
  8.4 1.5 %collective-permute-start = (bf16[4,16,1536]{2,1,0:T(8,128)(2,1)S(1)}, bf16[4,16,1536]{2,1,0:T(8,128)(2,1)S(1)}, u32[]{:S(2)}, u32[]{:S(2)}) collective-permute-start(bf16[4,16,1536]{2,1,0:T(8,128)(2,1)S(1)} %get-tuple-element.88), channel_id=1, source_target_pairs={{0,64},{64,0},{1,65},{65,1},{2,66},{66,2},{3,67},{67,3},{4,68},{68... | collective-permute-start | bytes 589832 | tf_op jit(solution)/shard_map/ppermute | solution.py:53
  11.1 1.8 %collective-permute-start.1 = (bf16[32,1536]{1,0:T(8,128)(2,1)S(1)}, bf16[32,1536]{1,0:T(8,128)(2,1)S(1)}, u32[]{:S(2)}, u32[]{:S(2)}) collective-permute-start(bf16[32,1536]{1,0:T(8,128)(2,1)S(1)} %bitcast.95), channel_id=1, source_target_pairs={{0,16},{16,32},{32,48},{48,0},{1,17},{17,33},{33,49},{49,1},{2,18}... | collective-permute-start | bytes 294920 | tf_op jit(solution)/shard_map/ppermute | solution.py:49
  12.8 3.3 %collective-permute-start.2 = (bf16[32,1536]{1,0:T(8,128)(2,1)S(1)}, bf16[32,1536]{1,0:T(8,128)(2,1)S(1)}, u32[]{:S(2)}, u32[]{:S(2)}) collective-permute-start(bf16[32,1536]{1,0:T(8,128)(2,1)S(1)} %bitcast.94), channel_id=1, source_target_pairs={{0,32},{16,48},{32,0},{48,16},{1,33},{17,49},{33,1},{49,17},{2,34}... | collective-permute-start | bytes 294920 | tf_op jit(solution)/shard_map/ppermute | solution.py:49
  17.0 1.3 collective-permute-start.4
  18.3 2.5 %collective-permute-done.2 = bf16[32,1536]{1,0:T(8,128)(2,1)S(1)} collective-permute-done((bf16[32,1536]{1,0:T(8,128)(2,1)S(1)}, bf16[32,1536]{1,0:T(8,128)(2,1)S(1)}, u32[]{:S(2)}, u32[]{:S(2)}) %collective-permute-start.2) | collective-permute-done | bytes 98336 | tf_op jit(solution)/shard_map/ppermute | solution.py:49
  20.9 3.0 %collective-permute-start.5 = (bf16[128,1536]{1,0:T(8,128)(2,1)S(1)}, bf16[128,1536]{1,0:T(8,128)(2,1)S(1)}, u32[]{:S(2)}, u32[]{:S(2)}) collective-permute-start(bf16[128,1536]{1,0:T(8,128)(2,1)S(1)} %pad_maximum_fusion.2), channel_id=1, source_target_pairs={{0,8},{1,9},{2,10},{3,11},{4,12},{5,13},{6,14},{7,15},{8,0},{9,1},... | collective-permute-start | bytes 1179656 | tf_op jit(solution)/shard_map/ppermute | solution.py:63
  24.3 2.3 %collective-permute-start.7 = (bf16[128,1536]{1,0:T(8,128)(2,1)S(1)}, bf16[128,1536]{1,0:T(8,128)(2,1)S(1)}, u32[]{:S(2)}, u32[]{:S(2)}) collective-permute-start(bf16[128,1536]{1,0:T(8,128)(2,1)S(1)} %pad_maximum_fusion.2), channel_id=1, source_target_pairs={{0,12},{1,13},{2,14},{3,15},{4,0},{5,1},{6,2},{7,3},{8,4},{9,5},{1... | collective-permute-start | bytes 1179656 | tf_op jit(solution)/shard_map/ppermute | solution.py:63
  26.6 7.1 %collective-permute-done.6 = f32[2,1824]{1,0:T(2,128)S(1)} collective-permute-done((f32[2,1824]{1,0:T(2,128)S(1)}, f32[2,1824]{1,0:T(2,128)S(1)}, u32[]{:S(2)}, u32[]{:S(2)}) %collective-permute-start.6) | collective-permute-done | bytes 14624 | tf_op jit(solution)/shard_map/ppermute | solution.py:387
  35.1 1.7 %collective-permute-start.8 = (bf16[2,128,1536]{2,1,0:T(8,128)(2,1)S(1)}, bf16[2,128,1536]{2,1,0:T(8,128)(2,1)S(1)}, u32[]{:S(2)}, u32[]{:S(2)}) collective-permute-start(bf16[2,128,1536]{2,1,0:T(8,128)(2,1)S(1)} %pad_maximum_fusion.own_0), channel_id=1, source_target_pairs={{0,3},{1,0},{2,1},{3,2},{4,7},{5,4},{6,5},{7,6},{8,11},{9,8},{10,9... | collective-permute-start | bytes 2359304 | tf_op jit(solution)/shard_map/ppermute | solution.py:63
  38.6 7.6 %collective-permute-done.11.below_1 = bf16[2,128,1536]{2,1,0:T(8,128)(2,1)S(1)} collective-permute-done((bf16[2,128,1536]{2,1,0:T(8,128)(2,1)S(1)}, bf16[2,128,1536]{2,1,0:T(8,128)(2,1)S(1)}, u32[]{:S(2)}, u32[]{:S(2)}) %collective-permute-start.11) | collective-permute-done | bytes 786464 | tf_op jit(solution)/shard_map/ppermute | solution.py:63
  46.3 2.8 %collective-permute-start.9 = (bf16[2,128,1536]{2,1,0:T(8,128)(2,1)S(1)}, bf16[2,128,1536]{2,1,0:T(8,128)(2,1)S(1)}, u32[]{:S(2)}, u32[]{:S(2)}) collective-permute-start(bf16[2,128,1536]{2,1,0:T(8,128)(2,1)S(1)} %collective-permute-done.8.above_0), channel_id=1, source_target_pairs={{0,3},{1,0},{2,1},{3,2},{4,7},{5,4},{6,5},{7,6},{8,11},{9,8},{10,9... | collective-permute-start | bytes 2359304 | tf_op jit(solution)/shard_map/ppermute | solution.py:63
  49.1 7.1 %first.1 = (f32[512,512]{1,0:T(8,128)S(1)}, f32[512,512]{1,0:T(8,128)S(1)}, f32[512,128]{1,0:T(8,128)S(1)}) custom-call(s32[2]{0:T(128)S(1)} %pad_add_fusion.place, bf16[2,128,1536]{2,1,0:T(8,128)(2,1)S(1)} %pad_maximum_fusion.own_0, bf16[2,128,1536]{2,1,0:T(8,128)(2,1)S(1)} %pad_maximum_fusion.1.own_1, f32[4,1,1536]{2,1,0:T(1,128)S(1)} %div.73.inverse, ...), custom_call_target="tpu_custom_call" | custom-call | flops 1610612736 | bytes 14155776 | tf_op jit(solution)/shard_map/first/pallas_call | solution.py:275
  56.3 8.1 %early.1 = (f32[512,512]{1,0:T(8,128)S(1)}, f32[512,512]{1,0:T(8,128)S(1)}, f32[512,128]{1,0:T(8,128)S(1)}, bf16[6144,512]{1,0:T(8,128)(2,1)S(1)}, bf16[6144,512]{1,0:T(8,128)(2,1)S(1)}) custom-call(s32[2]{0:T(128)S(1)} %pad_add_fusion.place, bf16[2,128,1536]{2,1,0:T(8,128)(2,1)S(1)} %collective-permute-done.8.above_0, ...), custom_call_target="tpu_custom_call" | custom-call | flops 3221225472 | bytes 15728640 | tf_op jit(solution)/shard_map/early/pallas_call | solution.py:275
  64.4 4.4 %late.1 = (bf16[512,512]{1,0:T(8,128)(2,1)S(1)}, bf16[2,128,1536]{2,1,0:T(8,128)(2,1)S(1)}, bf16[2,128,1536]{2,1,0:T(8,128)(2,1)S(1)}) custom-call(s32[2]{0:T(128)S(1)} %pad_add_fusion.place, bf16[2,128,1536]{2,1,0:T(8,128)(2,1)S(1)} %collective-permute-done.9.far_0, bf16[2,128,1536]{2,1,0:T(8,128)(2,1)S(1)} %collective-permute-done.12.far_1, ...), custom_call_target="tpu_custom_call" | custom-call | flops 2415919104 | bytes 3145728 | tf_op jit(solution)/shard_map/late/pallas_call | solution.py:301
  68.8 1.4 %collective-permute-start.19 = (bf16[2,128,1536]{2,1,0:T(8,128)(2,1)S(1)}, bf16[2,128,1536]{2,1,0:T(8,128)(2,1)S(1)}, u32[]{:S(2)}, u32[]{:S(2)}) collective-permute-start(bf16[2,128,1536]{2,1,0:T(8,128)(2,1)S(1)} %get-tuple-element.64), channel_id=1, source_target_pairs={{0,3},{1,0},{2,1},{3,2},{4,7},{5,4},{6,5},{7,6},{8,11},{9,8},{10,9... | collective-permute-start | bytes 2359304 | tf_op jit(solution)/shard_map/ppermute | solution.py:63
  70.4 7.7 %rest.1 = (bf16[2,128,1536]{2,1,0:T(8,128)(2,1)S(1)}, bf16[2,128,1536]{2,1,0:T(8,128)(2,1)S(1)}, bf16[2,128,1536]{2,1,0:T(8,128)(2,1)S(1)}, bf16[2,128,1536]{2,1...) custom-call(s32[2]{0:T(128)S(1)} %pad_add_fusion.place, ...), custom_call_target="tpu_custom_call" | custom-call | flops 2415919104 | bytes 11010048 | tf_op jit(solution)/shard_map/rest/pallas_call | solution.py:325
  78.2 2.7 %collective-permute-start.17 = (bf16[2,128,1536]{2,1,0:T(8,128)(2,1)S(1)}, bf16[2,128,1536]{2,1,0:T(8,128)(2,1)}, u32[]{:S(2)}, u32[]{:S(2)}) collective-permute-start(bf16[2,128,1536]{2,1,0:T(8,128)(2,1)S(1)} %get-tuple-element.60), channel_id=1, source_target_pairs={{0,3},{1,0},{2,1},{3,2},{4,7},{5,4},{6,5},{7,6},{8,11},{9,8},{10,9... | collective-permute-start | bytes 2359304 | tf_op jit(solution)/shard_map/ppermute | solution.py:63
  81.9 1.8 %collective-permute-start.20 = (bf16[2,128,1536]{2,1,0:T(8,128)(2,1)}, bf16[2,128,1536]{2,1,0:T(8,128)(2,1)}, u32[]{:S(2)}, u32[]{:S(2)}) collective-permute-start(bf16[2,128,1536]{2,1,0:T(8,128)(2,1)} %add_convert_fusion), channel_id=1, source_target_pairs={{0,3},{1,0},{2,1},{3,2},{4,7},{5,4},{6,5},{7,6},{8,11},{9,8},{10,9... | collective-permute-start | bytes 2359304 | tf_op jit(solution)/shard_map/ppermute | solution.py:63
  85.4 5.8 %collective-permute-done.18 = bf16[2,128,1536]{2,1,0:T(8,128)(2,1)} collective-permute-done((bf16[2,128,1536]{2,1,0:T(8,128)(2,1)}, bf16[2,128,1536]{2,1,0:T(8,128)(2,1)}, u32[]{:S(2)}, u32[]{:S(2)}) %collective-permute-start.18) | collective-permute-done | bytes 786464 | tf_op jit(solution)/shard_map/ppermute | solution.py:63
  91.2 7.1 %collective-permute-done.20 = bf16[2,128,1536]{2,1,0:T(8,128)(2,1)} collective-permute-done((bf16[2,128,1536]{2,1,0:T(8,128)(2,1)}, bf16[2,128,1536]{2,1,0:T(8,128)(2,1)}, u32[]{:S(2)}, u32[]{:S(2)}) %collective-permute-start.20) | collective-permute-done | bytes 786464 | tf_op jit(solution)/shard_map/ppermute | solution.py:63
  98.3 1.6 %fusion.19 = (bf16[128,1536]{1,0:T(8,128)(2,1)S(1)}, bf16[128,1536]{1,0:T(8,128)(2,1)S(1)}) fusion(bf16[2,128,1536]{2,1,0:T(8,128)(2,1)} %collective-permute-done.20, bf16[2,128,1536]{2,1,0:T(8,128)(2,1)} %collective-permute-done.18, bf16[2,128,1536]{2,1,0:T(8,128)(2,1)S(1)} %get-tuple-element.61), kind=kLoop, calls=%fused_computation.30 | loop fusion | flops 2359296 | bytes 3145728 | tf_op jit(solution)/shard_map/convert_element_type | solution.py:421
  99.9 3.1 %collective-permute-start.22 = (bf16[128,1536]{1,0:T(8,128)(2,1)S(1)}, bf16[128,1536]{1,0:T(8,128)(2,1)}, u32[]{:S(2)}, u32[]{:S(2)}) collective-permute-start(bf16[128,1536]{1,0:T(8,128)(2,1)S(1)} %get-tuple-element.76), channel_id=1, source_target_pairs={{0,8},{1,9},{2,10},{3,11},{4,12},{5,13},{6,14},{7,15},{8,0},{9,1},... | collective-permute-start | bytes 1179656 | tf_op jit(solution)/shard_map/ppermute | solution.py:63
  103.8 1.3 fusion.17
  106.8 1.8 %collective-permute-done.22 = bf16[128,1536]{1,0:T(8,128)(2,1)} collective-permute-done((bf16[128,1536]{1,0:T(8,128)(2,1)S(1)}, bf16[128,1536]{1,0:T(8,128)(2,1)}, u32[]{:S(2)}, u32[]{:S(2)}) %collective-permute-start.22) | collective-permute-done | bytes 393248 | tf_op jit(solution)/shard_map/ppermute | solution.py:63
  108.6 4.6 %collective-permute-done.23 = bf16[128,1536]{1,0:T(8,128)(2,1)} collective-permute-done((bf16[128,1536]{1,0:T(8,128)(2,1)S(1)}, bf16[128,1536]{1,0:T(8,128)(2,1)}, u32[]{:S(2)}, u32[]{:S(2)}) %collective-permute-start.23) | collective-permute-done | bytes 393248 | tf_op jit(solution)/shard_map/ppermute | solution.py:63
  113.2 2.0 %fusion.16 = bf16[128,1536]{1,0:T(8,128)(2,1)S(1)} fusion(bf16[128,1536]{1,0:T(8,128)(2,1)} %collective-permute-done.23, bf16[128,1536]{1,0:T(8,128)(2,1)} %collective-permute-done.22, bf16[128,1536]{1,0:T(8,128)(2,1)} %collective-permute-done.21, bf16[2,128,1536]{2,1,0:T(8,128)(2,1)} %collective-permute-done.17, ...), kind=kLoop, calls=%fused_computation.18 | loop fusion | flops 2359296 | bytes 2752512 | tf_op jit(solution)/shard_map/convert_element_type | solution.py:424
  115.2 1.9 %collective-permute-start.24 = (bf16[2,16,1536]{2,1,0:T(8,128)(2,1)S(1)}, bf16[2,16,1536]{2,1,0:T(8,128)(2,1)S(1)}, u32[]{:S(2)}, u32[]{:S(2)}) collective-permute-start(bf16[2,16,1536]{2,1,0:T(8,128)(2,1)S(1)} %bitcast.100), channel_id=1, source_target_pairs={{0,48},{16,0},{32,16},{48,32},{1,49},{17,1},{33,17},{49,33},{2,50}... | collective-permute-start | bytes 294920 | tf_op jit(solution)/shard_map/ppermute | solution.py:49
  117.1 1.5 %collective-permute-start.25 = (bf16[2,16,1536]{2,1,0:T(8,128)(2,1)S(1)}, bf16[2,16,1536]{2,1,0:T(8,128)(2,1)S(1)}, u32[]{:S(2)}, u32[]{:S(2)}) collective-permute-start(bf16[2,16,1536]{2,1,0:T(8,128)(2,1)S(1)} %bitcast.98), channel_id=1, source_target_pairs={{0,32},{16,48},{32,0},{48,16},{1,33},{17,49},{33,1},{49,17},{2,34}... | collective-permute-start | bytes 294920 | tf_op jit(solution)/shard_map/ppermute | solution.py:49
  119.7 2.4 %collective-permute-done.25 = bf16[2,16,1536]{2,1,0:T(8,128)(2,1)S(1)} collective-permute-done((bf16[2,16,1536]{2,1,0:T(8,128)(2,1)S(1)}, bf16[2,16,1536]{2,1,0:T(8,128)(2,1)S(1)}, u32[]{:S(2)}, u32[]{:S(2)}) %collective-permute-start.25) | collective-permute-done | bytes 98336 | tf_op jit(solution)/shard_map/ppermute | solution.py:49
  123.3 6.3 %collective-permute-start.27 = (bf16[4,16,1536]{2,1,0:T(8,128)(2,1)S(1)}, bf16[4,16,1536]{2,1,0:T(8,128)(2,1)S(1)}, u32[]{:S(2)}, u32[]{:S(2)}) collective-permute-start(bf16[4,16,1536]{2,1,0:T(8,128)(2,1)S(1)} %get-tuple-element.78), channel_id=1, source_target_pairs={{0,64},{64,0},{1,65},{65,1},{2,66},{66,2},{3,67},{67,3},{4,68},{68... | collective-permute-start | bytes 589832 | tf_op jit(solution)/shard_map/ppermute | solution.py:53
  (111 shorter events, 20.3 us)
Async XLA Ops:
  0.0 4.5 %copy-start.3 = (bf16[32,256]{1,0:T(8,128)(2,1)S(1)}, bf16[32,256]{1,0:T(8,128)(2,1)}, u32[]{:S(2)}) copy-start(bf16[32,256]{1,0:T(8,128)(2,1)} %param.17) | copy-start | bytes 49156
  4.6 3.3 %copy-start.5 = (bf16[1536]{0:T(1024)(128)(2,1)S(1)}, bf16[1536]{0:T(1024)(128)(2,1)}, u32[]{:S(2)}) copy-start(bf16[1536]{0:T(1024)(128)(2,1)} %param.20) | copy-start | bytes 9220
  4.6 3.3 %copy-start.2 = (bf16[32,1536]{1,0:T(8,128)(2,1)S(1)}, bf16[32,1536]{1,0:T(8,128)(2,1)}, u32[]{:S(2)}) copy-start(bf16[32,1536]{1,0:T(8,128)(2,1)} %param.19) | copy-start | bytes 294916
  8.4 2.6 %collective-permute-start = (bf16[4,16,1536]{2,1,0:T(8,128)(2,1)S(1)}, bf16[4,16,1536]{2,1,0:T(8,128)(2,1)S(1)}, u32[]{:S(2)}, u32[]{:S(2)}) collective-permute-start(bf16[4,16,1536]{2,1,0:T(8,128)(2,1)S(1)} %get-tuple-element.88), channel_id=1, source_target_pairs={{0,64},{64,0},{1,65},{65,1},{2,66},{66,2},{3,67},{67,3},{4,68},{68... | collective-permute-start | bytes 589832 | tf_op jit(solution)/shard_map/ppermute | solution.py:53
  11.1 7.2 %collective-permute-start.1 = (bf16[32,1536]{1,0:T(8,128)(2,1)S(1)}, bf16[32,1536]{1,0:T(8,128)(2,1)S(1)}, u32[]{:S(2)}, u32[]{:S(2)}) collective-permute-start(bf16[32,1536]{1,0:T(8,128)(2,1)S(1)} %bitcast.95), channel_id=1, source_target_pairs={{0,16},{16,32},{32,48},{48,0},{1,17},{17,33},{33,49},{49,1},{2,18}... | collective-permute-start | bytes 294920 | tf_op jit(solution)/shard_map/ppermute | solution.py:49
  12.8 8.0 %collective-permute-start.2 = (bf16[32,1536]{1,0:T(8,128)(2,1)S(1)}, bf16[32,1536]{1,0:T(8,128)(2,1)S(1)}, u32[]{:S(2)}, u32[]{:S(2)}) collective-permute-start(bf16[32,1536]{1,0:T(8,128)(2,1)S(1)} %bitcast.94), channel_id=1, source_target_pairs={{0,32},{16,48},{32,0},{48,16},{1,33},{17,49},{33,1},{49,17},{2,34}... | collective-permute-start | bytes 294920 | tf_op jit(solution)/shard_map/ppermute | solution.py:49
  16.2 4.7 %collective-permute-start.3 = (bf16[32,1536]{1,0:T(8,128)(2,1)S(1)}, bf16[32,1536]{1,0:T(8,128)(2,1)S(1)}, u32[]{:S(2)}, u32[]{:S(2)}) collective-permute-start(bf16[32,1536]{1,0:T(8,128)(2,1)S(1)} %bitcast.93), channel_id=1, source_target_pairs={{0,48},{16,0},{32,16},{48,32},{1,49},{17,1},{33,17},{49,33},{2,50}... | collective-permute-start | bytes 294920 | tf_op jit(solution)/shard_map/ppermute | solution.py:49
  17.0 3.9 %collective-permute-start.4 = (f32[1824]{0:T(1024)S(1)}, f32[1824]{0:T(1024)S(1)}, u32[]{:S(2)}, u32[]{:S(2)}) collective-permute-start(f32[1824]{0:T(1024)S(1)} %pad_maximum_fusion.9), channel_id=1, source_target_pairs={{0,1},{1,0},{2,3},{3,2},{4,5},{5,4},{6,7},{7,6},{8,9},{9,8},{10,11... | collective-permute-start | bytes 21896 | tf_op jit(solution)/shard_map/ppermute | solution.py:383
  20.9 12.8 %collective-permute-start.5 = (bf16[128,1536]{1,0:T(8,128)(2,1)S(1)}, bf16[128,1536]{1,0:T(8,128)(2,1)S(1)}, u32[]{:S(2)}, u32[]{:S(2)}) collective-permute-start(bf16[128,1536]{1,0:T(8,128)(2,1)S(1)} %pad_maximum_fusion.2), channel_id=1, source_target_pairs={{0,8},{1,9},{2,10},{3,11},{4,12},{5,13},{6,14},{7,15},{8,0},{9,1},... | collective-permute-start | bytes 1179656 | tf_op jit(solution)/shard_map/ppermute | solution.py:63
  23.9 9.9 %collective-permute-start.10 = (bf16[128,1536]{1,0:T(8,128)(2,1)S(1)}, bf16[128,1536]{1,0:T(8,128)(2,1)S(1)}, u32[]{:S(2)}, u32[]{:S(2)}) collective-permute-start(bf16[128,1536]{1,0:T(8,128)(2,1)S(1)} %pad_maximum_fusion.2), channel_id=1, source_target_pairs={{0,4},{1,5},{2,6},{3,7},{4,8},{5,9},{6,10},{7,11},{8,12},{9,13},{1... | collective-permute-start | bytes 1179656 | tf_op jit(solution)/shard_map/ppermute | solution.py:63
  24.3 10.7 %collective-permute-start.7 = (bf16[128,1536]{1,0:T(8,128)(2,1)S(1)}, bf16[128,1536]{1,0:T(8,128)(2,1)S(1)}, u32[]{:S(2)}, u32[]{:S(2)}) collective-permute-start(bf16[128,1536]{1,0:T(8,128)(2,1)S(1)} %pad_maximum_fusion.2), channel_id=1, source_target_pairs={{0,12},{1,13},{2,14},{3,15},{4,0},{5,1},{6,2},{7,3},{8,4},{9,5},{1... | collective-permute-start | bytes 1179656 | tf_op jit(solution)/shard_map/ppermute | solution.py:63
  26.6 7.1 %collective-permute-start.6 = (f32[2,1824]{1,0:T(2,128)S(1)}, f32[2,1824]{1,0:T(2,128)S(1)}, u32[]{:S(2)}, u32[]{:S(2)}) collective-permute-start(f32[2,1824]{1,0:T(2,128)S(1)} %pad_maximum_fusion.7), channel_id=1, source_target_pairs={{0,2},{1,3},{2,0},{3,1},{4,6},{5,7},{6,4},{7,5},{8,10},{9,11},{10,... | collective-permute-start | bytes 43784 | tf_op jit(solution)/shard_map/ppermute | solution.py:387
  33.9 12.4 %collective-permute-start.11 = (bf16[2,128,1536]{2,1,0:T(8,128)(2,1)S(1)}, bf16[2,128,1536]{2,1,0:T(8,128)(2,1)S(1)}, u32[]{:S(2)}, u32[]{:S(2)}) collective-permute-start(bf16[2,128,1536]{2,1,0:T(8,128)(2,1)S(1)} %pad_maximum_fusion.1.own_1), channel_id=1, source_target_pairs={{0,1},{1,2},{2,3},{3,0},{4,5},{5,6},{6,7},{7,4},{8,9},{9,10},{10,1... | collective-permute-start | bytes 2359304 | tf_op jit(solution)/shard_map/ppermute | solution.py:63
  35.1 11.2 %collective-permute-start.8 = (bf16[2,128,1536]{2,1,0:T(8,128)(2,1)S(1)}, bf16[2,128,1536]{2,1,0:T(8,128)(2,1)S(1)}, u32[]{:S(2)}, u32[]{:S(2)}) collective-permute-start(bf16[2,128,1536]{2,1,0:T(8,128)(2,1)S(1)} %pad_maximum_fusion.own_0), channel_id=1, source_target_pairs={{0,3},{1,0},{2,1},{3,2},{4,7},{5,4},{6,5},{7,6},{8,11},{9,8},{10,9... | collective-permute-start | bytes 2359304 | tf_op jit(solution)/shard_map/ppermute | solution.py:63
  36.9 19.3 %collective-permute-start.13 = (bf16[2,128,1536]{2,1,0:T(8,128)(2,1)S(1)}, bf16[2,128,1536]{2,1,0:T(8,128)(2,1)S(1)}, u32[]{:S(2)}, u32[]{:S(2)}) collective-permute-start(bf16[2,128,1536]{2,1,0:T(8,128)(2,1)S(1)} %pad_maximum_fusion.1.own_1), channel_id=1, source_target_pairs={{0,3},{1,0},{2,1},{3,2},{4,7},{5,4},{6,5},{7,6},{8,11},{9,8},{10,9... | collective-permute-start | bytes 2359304 | tf_op jit(solution)/shard_map/ppermute | solution.py:63
  38.2 18.1 %collective-permute-start.14 = (bf16[2,128,1536]{2,1,0:T(8,128)(2,1)S(1)}, bf16[2,128,1536]{2,1,0:T(8,128)(2,1)S(1)}, u32[]{:S(2)}, u32[]{:S(2)}) collective-permute-start(bf16[2,128,1536]{2,1,0:T(8,128)(2,1)S(1)} %pad_maximum_fusion.own_0), channel_id=1, source_target_pairs={{0,1},{1,2},{2,3},{3,0},{4,5},{5,6},{6,7},{7,4},{8,9},{9,10},{10,1... | collective-permute-start | bytes 2359304 | tf_op jit(solution)/shard_map/ppermute | solution.py:63
  46.3 18.1 %collective-permute-start.12 = (bf16[2,128,1536]{2,1,0:T(8,128)(2,1)S(1)}, bf16[2,128,1536]{2,1,0:T(8,128)(2,1)S(1)}, u32[]{:S(2)}, u32[]{:S(2)}) collective-permute-start(bf16[2,128,1536]{2,1,0:T(8,128)(2,1)S(1)} %collective-permute-done.11.below_1), channel_id=1, source_target_pairs={{0,1},{1,2},{2,3},{3,0},{4,5},{5,6},{6,7},{7,4},{8,9},{9,10},{10,1... | collective-permute-start | bytes 2359304 | tf_op jit(solution)/shard_map/ppermute | solution.py:63
  46.3 18.1 %collective-permute-start.9 = (bf16[2,128,1536]{2,1,0:T(8,128)(2,1)S(1)}, bf16[2,128,1536]{2,1,0:T(8,128)(2,1)S(1)}, u32[]{:S(2)}, u32[]{:S(2)}) collective-permute-start(bf16[2,128,1536]{2,1,0:T(8,128)(2,1)S(1)} %collective-permute-done.8.above_0), channel_id=1, source_target_pairs={{0,3},{1,0},{2,1},{3,2},{4,7},{5,4},{6,5},{7,6},{8,11},{9,8},{10,9... | collective-permute-start | bytes 2359304 | tf_op jit(solution)/shard_map/ppermute | solution.py:63
  68.8 12.0 %collective-permute-start.19 = (bf16[2,128,1536]{2,1,0:T(8,128)(2,1)S(1)}, bf16[2,128,1536]{2,1,0:T(8,128)(2,1)S(1)}, u32[]{:S(2)}, u32[]{:S(2)}) collective-permute-start(bf16[2,128,1536]{2,1,0:T(8,128)(2,1)S(1)} %get-tuple-element.64), channel_id=1, source_target_pairs={{0,3},{1,0},{2,1},{3,2},{4,7},{5,4},{6,5},{7,6},{8,11},{9,8},{10,9... | collective-permute-start | bytes 2359304 | tf_op jit(solution)/shard_map/ppermute | solution.py:63
  70.3 13.4 %collective-permute-start.15 = (bf16[2,128,1536]{2,1,0:T(8,128)(2,1)S(1)}, bf16[2,128,1536]{2,1,0:T(8,128)(2,1)S(1)}, u32[]{:S(2)}, u32[]{:S(2)}) collective-permute-start(bf16[2,128,1536]{2,1,0:T(8,128)(2,1)S(1)} %get-tuple-element.59), channel_id=1, source_target_pairs={{0,1},{1,2},{2,3},{3,0},{4,5},{5,6},{6,7},{7,4},{8,9},{9,10},{10,1... | collective-permute-start | bytes 2359304 | tf_op jit(solution)/shard_map/ppermute | solution.py:63
  78.1 13.1 %collective-permute-start.18 = (bf16[2,128,1536]{2,1,0:T(8,128)(2,1)}, bf16[2,128,1536]{2,1,0:T(8,128)(2,1)}, u32[]{:S(2)}, u32[]{:S(2)}) collective-permute-start(bf16[2,128,1536]{2,1,0:T(8,128)(2,1)} %get-tuple-element.62), channel_id=1, source_target_pairs={{0,1},{1,2},{2,3},{3,0},{4,5},{5,6},{6,7},{7,4},{8,9},{9,10},{10,1... | collective-permute-start | bytes 2359304 | tf_op jit(solution)/shard_map/ppermute | solution.py:63
  78.2 25.6 %collective-permute-start.17 = (bf16[2,128,1536]{2,1,0:T(8,128)(2,1)S(1)}, bf16[2,128,1536]{2,1,0:T(8,128)(2,1)}, u32[]{:S(2)}, u32[]{:S(2)}) collective-permute-start(bf16[2,128,1536]{2,1,0:T(8,128)(2,1)S(1)} %get-tuple-element.60), channel_id=1, source_target_pairs={{0,3},{1,0},{2,1},{3,2},{4,7},{5,4},{6,5},{7,6},{8,11},{9,8},{10,9... | collective-permute-start | bytes 2359304 | tf_op jit(solution)/shard_map/ppermute | solution.py:63
  81.9 16.4 %collective-permute-start.20 = (bf16[2,128,1536]{2,1,0:T(8,128)(2,1)}, bf16[2,128,1536]{2,1,0:T(8,128)(2,1)}, u32[]{:S(2)}, u32[]{:S(2)}) collective-permute-start(bf16[2,128,1536]{2,1,0:T(8,128)(2,1)} %add_convert_fusion), channel_id=1, source_target_pairs={{0,3},{1,0},{2,1},{3,2},{4,7},{5,4},{6,5},{7,6},{8,11},{9,8},{10,9... | collective-permute-start | bytes 2359304 | tf_op jit(solution)/shard_map/ppermute | solution.py:63
  84.8 19.0 %collective-permute-start.16 = (bf16[2,128,1536]{2,1,0:T(8,128)(2,1)}, bf16[2,128,1536]{2,1,0:T(8,128)(2,1)}, u32[]{:S(2)}, u32[]{:S(2)}) collective-permute-start(bf16[2,128,1536]{2,1,0:T(8,128)(2,1)} %add_convert_fusion.1), channel_id=1, source_target_pairs={{0,1},{1,2},{2,3},{3,0},{4,5},{5,6},{6,7},{7,4},{8,9},{9,10},{10,1... | collective-permute-start | bytes 2359304 | tf_op jit(solution)/shard_map/ppermute | solution.py:63
  99.9 8.7 %collective-permute-start.22 = (bf16[128,1536]{1,0:T(8,128)(2,1)S(1)}, bf16[128,1536]{1,0:T(8,128)(2,1)}, u32[]{:S(2)}, u32[]{:S(2)}) collective-permute-start(bf16[128,1536]{1,0:T(8,128)(2,1)S(1)} %get-tuple-element.76), channel_id=1, source_target_pairs={{0,8},{1,9},{2,10},{3,11},{4,12},{5,13},{6,14},{7,15},{8,0},{9,1},... | collective-permute-start | bytes 1179656 | tf_op jit(solution)/shard_map/ppermute | solution.py:63
  103.0 10.2 %collective-permute-start.23 = (bf16[128,1536]{1,0:T(8,128)(2,1)S(1)}, bf16[128,1536]{1,0:T(8,128)(2,1)}, u32[]{:S(2)}, u32[]{:S(2)}) collective-permute-start(bf16[128,1536]{1,0:T(8,128)(2,1)S(1)} %get-tuple-element.75), channel_id=1, source_target_pairs={{0,12},{1,13},{2,14},{3,15},{4,0},{5,1},{6,2},{7,3},{8,4},{9,5},{1... | collective-permute-start | bytes 1179656 | tf_op jit(solution)/shard_map/ppermute | solution.py:63
  105.1 8.1 %collective-permute-start.21 = (bf16[128,1536]{1,0:T(8,128)(2,1)S(1)}, bf16[128,1536]{1,0:T(8,128)(2,1)}, u32[]{:S(2)}, u32[]{:S(2)}) collective-permute-start(bf16[128,1536]{1,0:T(8,128)(2,1)S(1)} %fusion.17), channel_id=1, source_target_pairs={{0,4},{1,5},{2,6},{3,7},{4,8},{5,9},{6,10},{7,11},{8,12},{9,13},{1... | collective-permute-start | bytes 1179656 | tf_op jit(solution)/shard_map/ppermute | solution.py:63
  113.2 18.5 %copy-start.1 = (bf16[32,128,256]{2,1,0:T(8,128)(2,1)S(1)}, bf16[32,128,256]{2,1,0:T(8,128)(2,1)}, u32[]{:S(2)}) copy-start(bf16[32,128,256]{2,1,0:T(8,128)(2,1)} %param.14) | copy-start | bytes 6291460
  115.2 4.5 %collective-permute-start.24 = (bf16[2,16,1536]{2,1,0:T(8,128)(2,1)S(1)}, bf16[2,16,1536]{2,1,0:T(8,128)(2,1)S(1)}, u32[]{:S(2)}, u32[]{:S(2)}) collective-permute-start(bf16[2,16,1536]{2,1,0:T(8,128)(2,1)S(1)} %bitcast.100), channel_id=1, source_target_pairs={{0,48},{16,0},{32,16},{48,32},{1,49},{17,1},{33,17},{49,33},{2,50}... | collective-permute-start | bytes 294920 | tf_op jit(solution)/shard_map/ppermute | solution.py:49
  117.1 5.0 %collective-permute-start.25 = (bf16[2,16,1536]{2,1,0:T(8,128)(2,1)S(1)}, bf16[2,16,1536]{2,1,0:T(8,128)(2,1)S(1)}, u32[]{:S(2)}, u32[]{:S(2)}) collective-permute-start(bf16[2,16,1536]{2,1,0:T(8,128)(2,1)S(1)} %bitcast.98), channel_id=1, source_target_pairs={{0,32},{16,48},{32,0},{48,16},{1,33},{17,49},{33,1},{49,17},{2,34}... | collective-permute-start | bytes 294920 | tf_op jit(solution)/shard_map/ppermute | solution.py:49
  118.5 4.7 %collective-permute-start.26 = (bf16[2,16,1536]{2,1,0:T(8,128)(2,1)S(1)}, bf16[2,16,1536]{2,1,0:T(8,128)(2,1)S(1)}, u32[]{:S(2)}, u32[]{:S(2)}) collective-permute-start(bf16[2,16,1536]{2,1,0:T(8,128)(2,1)S(1)} %bitcast.96), channel_id=1, source_target_pairs={{0,16},{16,32},{32,48},{48,0},{1,17},{17,33},{33,49},{49,1},{2,18}... | collective-permute-start | bytes 294920 | tf_op jit(solution)/shard_map/ppermute | solution.py:49
  123.3 7.4 %collective-permute-start.27 = (bf16[4,16,1536]{2,1,0:T(8,128)(2,1)S(1)}, bf16[4,16,1536]{2,1,0:T(8,128)(2,1)S(1)}, u32[]{:S(2)}, u32[]{:S(2)}) collective-permute-start(bf16[4,16,1536]{2,1,0:T(8,128)(2,1)S(1)} %get-tuple-element.78), channel_id=1, source_target_pairs={{0,64},{64,0},{1,65},{65,1},{2,66},{66,2},{3,67},{67,3},{4,68},{68... | collective-permute-start | bytes 589832 | tf_op jit(solution)/shard_map/ppermute | solution.py:53
  (3 other events, 8.3 us)

commit v5 on v4

--- a/solution.py
+++ b/solution.py
@@ -362,15 +362,15 @@
     shared = jnp.concatenate([stats.reshape(-1), norm_gain.astype(f32)])
 
     near = ((expert_ids // RING + me_pool) % 2) * RING + (expert_ids % RING - me_z + RING) % RING
-    flat = near.reshape(-1)
-    expert_hot = (flat[:, None] == jnp.arange(experts, dtype=jnp.int32)[None, :]).astype(jnp.int32)
-    earlier = jnp.cumsum(expert_hot, 0) - expert_hot
-    slot = jnp.sum(earlier * expert_hot, 1)
     size = CAP // GROUPS
-    position = (((slot // size) * experts + flat) * size + slot % size).reshape(rows, TOP)
-    places = jnp.arange(experts * CAP, dtype=jnp.int32)
-    hot = position[:, :, None] == places[None, None, :]
-    dispatch = jnp.any(hot, 1).T.astype(bf16)
+    wanted = near.T[:, None, :] == jnp.arange(experts, dtype=jnp.int32)[None, :, None]
+    named = wanted[0] | wanted[1]
+    tokens = jnp.arange(rows, dtype=jnp.int32)
+    before = (tokens[:, None] < tokens[None, :]).astype(bf16)
+    slot = jnp.dot(named.astype(bf16), before, preferred_element_type=f32)
+    slots = jnp.arange(CAP, dtype=jnp.int32).astype(f32)
+    hot = (slot[:, None, :] == slots[None, :, None]) & named[:, None, :]
+    dispatch = hot.astype(bf16).reshape(experts * CAP, rows)
     bucket = jnp.dot(dispatch, raised, preferred_element_type=f32).astype(bf16)
     buckets = bucket.reshape(GROUPS, 2, RING, size, features)
 
@@ -428,7 +428,8 @@
     logits = stats[:, :experts] * scale
     chosen = jnp.take_along_axis(logits, expert_ids, 1)
     gates = jax.nn.softmax(chosen, -1)
-    combine = jnp.sum(jnp.where(hot, gates[:, :, None], 0.0), 1)
+    share = jnp.sum(jnp.where(wanted, gates.T[:, None, :], 0.0), 0)
+    combine = jnp.where(hot, share[:, None, :], 0.0).reshape(experts * CAP, rows).T
     results = jnp.stack(returned).reshape(experts * CAP, features)
     mixed = jnp.dot(combine, results.astype(f32), precision=lax.Precision.HIGHEST)
     return (hfloat + mixed).astype(bf16)

time: 132 us -> 133 us (level)
  waiting for transfers between devices: 43.1 us -> 41 us
  other arithmetic: 9.94 us -> 11.5 us
    ppermute x18, waiting for transfers between devices: 27.1 us -> 25 us  [cross(): return lax.ppermute(x, ('pool', 'x', 'tp'), pairs)]
  transfers between devices with their start and end apart: 28 -> 28, of which waited for: 13 -> 13; matrix products, arithmetic and copies ran while one was open for 6% -> 8% of each run, Pallas kernels for 17% -> 17%
where the time goes in v5:
time: 133 us; the launch traced here: 132 us
  starting transfers between devices  41.8 us (31%)
  waiting for transfers between devices  41 us (31%)
  Pallas kernels  28.5 us (21%)
  other arithmetic  11.5 us (9%)
  matrix products  5.33 us (4%)
  local copies, waits for them, and re-layouts  3.69 us (3%)
    ppermute x18, waiting for transfers between devices, cross(): return lax.ppermute(x, ('pool', 'x', 'tp'), pairs)  25 us
    ppermute x18, starting transfers between devices, cross(): return lax.ppermute(x, ('pool', 'x', 'tp'), pairs)  23.4 us
    pallas_call x2, Pallas kernels, weighed(): pl.pallas_call(kernel, out_shape=[jax.ShapeDtypeStruct((count, n), f32) f...  15.2 us
    ppermute x6, starting transfers between devices, along(): return lax.ppermute(x, axis, [(i, (i + by) % RING) for i in range(RING)])  9.13 us
    ppermute x2, starting transfers between devices, swap_cores(): return lax.ppermute(x, 'pool', [(0, 1), (1, 0)])  7.87 us
    pallas_call x1, Pallas kernels, rest(): pl.pallas_call(rest_kernel, out_shape=[jax.ShapeDtypeStruct(shape, bf16)]...  7.67 us
    ppermute x6, waiting for transfers between devices, along(): return lax.ppermute(x, axis, [(i, (i + by) % RING) for i in range(RING)])  7.19 us
    ppermute x1, waiting for transfers between devices, shards(): others = lax.ppermute(couple, 'tp', [(i, i ^ 2) for i in range(RING)])  7.09 us
  transfers between devices with their start and end apart: 28, of which 13 were waited for; matrix products, arithmetic and copies ran while one was open for 8% of the time, Pallas kernels for 17%

profile of v5, /device:TPU:1, one launch (start us, length us, event | category | flops | bytes accessed | tf_op | source)
XLA Modules:
  0.0 132.1 jit_solution(5596242412081431027)
XLA Ops:
  4.6 2.3 %fusion.13 = f32[32,2,6,128]{3,2,1,0:T(8,128)S(1)} fusion(f32[32,2,6,128]{3,2,1,0:T(8,128)S(1)} %get-tuple-element.92, f32[32,2,128]{2,1,0:T(2,128)S(1)} %reshape.235, f32[32,2,6]{2,1,0:T(2,128)S(1)} %get-tuple-element.90, f32[32,2,6]{2,1,0:T(2,128)S(1)} %get-tuple-element.89, f32[32,2,6]{2,1,0:T(2,128)S(1)} %multiply_maximum_fusion, ...), kind=kOutput, calls=%fused_computation.14 | convolution fusion | flops 12828672 | bytes 2527744 | tf_op jit(solution)/shard_map/rghc,rcgo->rgho/dot_general | solution.py:42
  7.8 1.5 %collective-permute-start = (bf16[4,16,1536]{2,1,0:T(8,128)(2,1)S(1)}, bf16[4,16,1536]{2,1,0:T(8,128)(2,1)S(1)}, u32[]{:S(2)}, u32[]{:S(2)}) collective-permute-start(bf16[4,16,1536]{2,1,0:T(8,128)(2,1)S(1)} %get-tuple-element.88), channel_id=1, source_target_pairs={{0,64},{64,0},{1,65},{65,1},{2,66},{66,2},{3,67},{67,3},{4,68},{68... | collective-permute-start | bytes 589832 | tf_op jit(solution)/shard_map/ppermute | solution.py:53
  10.5 1.8 %collective-permute-start.1 = (bf16[32,1536]{1,0:T(8,128)(2,1)S(1)}, bf16[32,1536]{1,0:T(8,128)(2,1)S(1)}, u32[]{:S(2)}, u32[]{:S(2)}) collective-permute-start(bf16[32,1536]{1,0:T(8,128)(2,1)S(1)} %bitcast.110), channel_id=1, source_target_pairs={{0,16},{16,32},{32,48},{48,0},{1,17},{17,33},{33,49},{49,1},{2,18}... | collective-permute-start | bytes 294920 | tf_op jit(solution)/shard_map/ppermute | solution.py:49
  12.2 3.3 %collective-permute-start.2 = (bf16[32,1536]{1,0:T(8,128)(2,1)S(1)}, bf16[32,1536]{1,0:T(8,128)(2,1)S(1)}, u32[]{:S(2)}, u32[]{:S(2)}) collective-permute-start(bf16[32,1536]{1,0:T(8,128)(2,1)S(1)} %bitcast.109), channel_id=1, source_target_pairs={{0,32},{16,48},{32,0},{48,16},{1,33},{17,49},{33,1},{49,17},{2,34}... | collective-permute-start | bytes 294920 | tf_op jit(solution)/shard_map/ppermute | solution.py:49
  16.4 1.3 collective-permute-start.4
  17.7 2.5 %collective-permute-done.2 = bf16[32,1536]{1,0:T(8,128)(2,1)S(1)} collective-permute-done((bf16[32,1536]{1,0:T(8,128)(2,1)S(1)}, bf16[32,1536]{1,0:T(8,128)(2,1)S(1)}, u32[]{:S(2)}, u32[]{:S(2)}) %collective-permute-start.2) | collective-permute-done | bytes 98336 | tf_op jit(solution)/shard_map/ppermute | solution.py:49
  20.3 3.0 %collective-permute-start.5 = (bf16[128,1536]{1,0:T(8,128)(2,1)S(1)}, bf16[128,1536]{1,0:T(8,128)(2,1)S(1)}, u32[]{:S(2)}, u32[]{:S(2)}) collective-permute-start(bf16[128,1536]{1,0:T(8,128)(2,1)S(1)} %pad_maximum_fusion.2), channel_id=1, source_target_pairs={{0,8},{1,9},{2,10},{3,11},{4,12},{5,13},{6,14},{7,15},{8,0},{9,1},... | collective-permute-start | bytes 1179656 | tf_op jit(solution)/shard_map/ppermute | solution.py:63
  23.7 2.3 %collective-permute-start.7 = (bf16[128,1536]{1,0:T(8,128)(2,1)S(1)}, bf16[128,1536]{1,0:T(8,128)(2,1)S(1)}, u32[]{:S(2)}, u32[]{:S(2)}) collective-permute-start(bf16[128,1536]{1,0:T(8,128)(2,1)S(1)} %pad_maximum_fusion.2), channel_id=1, source_target_pairs={{0,12},{1,13},{2,14},{3,15},{4,0},{5,1},{6,2},{7,3},{8,4},{9,5},{1... | collective-permute-start | bytes 1179656 | tf_op jit(solution)/shard_map/ppermute | solution.py:63
  26.0 7.1 %collective-permute-done.6 = f32[2,1824]{1,0:T(2,128)S(1)} collective-permute-done((f32[2,1824]{1,0:T(2,128)S(1)}, f32[2,1824]{1,0:T(2,128)S(1)}, u32[]{:S(2)}, u32[]{:S(2)}) %collective-permute-start.6) | collective-permute-done | bytes 14624 | tf_op jit(solution)/shard_map/ppermute | solution.py:387
  34.5 1.7 %collective-permute-start.8 = (bf16[2,128,1536]{2,1,0:T(8,128)(2,1)S(1)}, bf16[2,128,1536]{2,1,0:T(8,128)(2,1)S(1)}, u32[]{:S(2)}, u32[]{:S(2)}) collective-permute-start(bf16[2,128,1536]{2,1,0:T(8,128)(2,1)S(1)} %pad_maximum_fusion.own_0), channel_id=1, source_target_pairs={{0,3},{1,0},{2,1},{3,2},{4,7},{5,4},{6,5},{7,6},{8,11},{9,8},{10,9... | collective-permute-start | bytes 2359304 | tf_op jit(solution)/shard_map/ppermute | solution.py:63
  38.0 7.6 %collective-permute-done.11.below_1 = bf16[2,128,1536]{2,1,0:T(8,128)(2,1)S(1)} collective-permute-done((bf16[2,128,1536]{2,1,0:T(8,128)(2,1)S(1)}, bf16[2,128,1536]{2,1,0:T(8,128)(2,1)S(1)}, u32[]{:S(2)}, u32[]{:S(2)}) %collective-permute-start.11) | collective-permute-done | bytes 786464 | tf_op jit(solution)/shard_map/ppermute | solution.py:63
  45.7 2.8 %collective-permute-start.9 = (bf16[2,128,1536]{2,1,0:T(8,128)(2,1)S(1)}, bf16[2,128,1536]{2,1,0:T(8,128)(2,1)S(1)}, u32[]{:S(2)}, u32[]{:S(2)}) collective-permute-start(bf16[2,128,1536]{2,1,0:T(8,128)(2,1)S(1)} %collective-permute-done.8.above_0), channel_id=1, source_target_pairs={{0,3},{1,0},{2,1},{3,2},{4,7},{5,4},{6,5},{7,6},{8,11},{9,8},{10,9... | collective-permute-start | bytes 2359304 | tf_op jit(solution)/shard_map/ppermute | solution.py:63
  48.5 7.1 %first.1 = (f32[512,512]{1,0:T(8,128)S(1)}, f32[512,512]{1,0:T(8,128)S(1)}, f32[512,128]{1,0:T(8,128)S(1)}) custom-call(s32[2]{0:T(128)S(1)} %pad_add_fusion.place, bf16[2,128,1536]{2,1,0:T(8,128)(2,1)S(1)} %pad_maximum_fusion.own_0, bf16[2,128,1536]{2,1,0:T(8,128)(2,1)S(1)} %pad_maximum_fusion.1.own_1, f32[4,1,1536]{2,1,0:T(1,128)S(1)} %div.58.inverse, ...), custom_call_target="tpu_custom_call" | custom-call | flops 1610612736 | bytes 14155776 | tf_op jit(solution)/shard_map/first/pallas_call | solution.py:275
  55.6 8.1 %early.1 = (f32[512,512]{1,0:T(8,128)S(1)}, f32[512,512]{1,0:T(8,128)S(1)}, f32[512,128]{1,0:T(8,128)S(1)}, bf16[6144,512]{1,0:T(8,128)(2,1)S(1)}, bf16[6144,512]{1,0:T(8,128)(2,1)S(1)}) custom-call(s32[2]{0:T(128)S(1)} %pad_add_fusion.place, bf16[2,128,1536]{2,1,0:T(8,128)(2,1)S(1)} %collective-permute-done.8.above_0, ...), custom_call_target="tpu_custom_call" | custom-call | flops 3221225472 | bytes 15728640 | tf_op jit(solution)/shard_map/early/pallas_call | solution.py:275
  63.8 5.6 %late.1 = (bf16[512,512]{1,0:T(8,128)(2,1)S(1)}, bf16[2,128,1536]{2,1,0:T(8,128)(2,1)}, bf16[2,128,1536]{2,1,0:T(8,128)(2,1)}) custom-call(s32[2]{0:T(128)S(1)} %pad_add_fusion.place, bf16[2,128,1536]{2,1,0:T(8,128)(2,1)S(1)} %collective-permute-done.9.far_0, bf16[2,128,1536]{2,1,0:T(8,128)(2,1)S(1)} %collective-permute-done.12.far_1, ...), custom_call_target="tpu_custom_call" | custom-call | flops 2415919104 | bytes 3145728 | tf_op jit(solution)/shard_map/late/pallas_call | solution.py:301
  69.4 1.4 %collective-permute-start.19 = (bf16[2,128,1536]{2,1,0:T(8,128)(2,1)}, bf16[2,128,1536]{2,1,0:T(8,128)(2,1)}, u32[]{:S(2)}, u32[]{:S(2)}) collective-permute-start(bf16[2,128,1536]{2,1,0:T(8,128)(2,1)} %get-tuple-element.64), channel_id=1, source_target_pairs={{0,3},{1,0},{2,1},{3,2},{4,7},{5,4},{6,5},{7,6},{8,11},{9,8},{10,9... | collective-permute-start | bytes 2359304 | tf_op jit(solution)/shard_map/ppermute | solution.py:63
  71.3 7.7 %rest.1 = (bf16[2,128,1536]{2,1,0:T(8,128)(2,1)S(1)}, bf16[2,128,1536]{2,1,0:T(8,128)(2,1)S(1)}, bf16[2,128,1536]{2,1,0:T(8,128)(2,1)S(1)}, bf16[2,128,1536]{2,1...) custom-call(s32[2]{0:T(128)S(1)} %pad_add_fusion.place, ...), custom_call_target="tpu_custom_call" | custom-call | flops 2415919104 | bytes 11010048 | tf_op jit(solution)/shard_map/rest/pallas_call | solution.py:325
  79.0 2.7 %collective-permute-start.17 = (bf16[2,128,1536]{2,1,0:T(8,128)(2,1)S(1)}, bf16[2,128,1536]{2,1,0:T(8,128)(2,1)}, u32[]{:S(2)}, u32[]{:S(2)}) collective-permute-start(bf16[2,128,1536]{2,1,0:T(8,128)(2,1)S(1)} %get-tuple-element.60), channel_id=1, source_target_pairs={{0,3},{1,0},{2,1},{3,2},{4,7},{5,4},{6,5},{7,6},{8,11},{9,8},{10,9... | collective-permute-start | bytes 2359304 | tf_op jit(solution)/shard_map/ppermute | solution.py:63
  81.7 2.2 %add_convert_fusion = bf16[2,128,1536]{2,1,0:T(8,128)(2,1)} fusion(bf16[2,128,1536]{2,1,0:T(8,128)(2,1)} %collective-permute-done.19, bf16[2,128,1536]{2,1,0:T(8,128)(2,1)S(1)} %get-tuple-element.63), kind=kLoop, calls=%fused_computation.10 | loop fusion | flops 1572864 | bytes 2359296 | tf_op jit(solution)/shard_map/convert_element_type | solution.py:416
  83.9 1.8 %collective-permute-start.20 = (bf16[2,128,1536]{2,1,0:T(8,128)(2,1)}, bf16[2,128,1536]{2,1,0:T(8,128)(2,1)}, u32[]{:S(2)}, u32[]{:S(2)}) collective-permute-start(bf16[2,128,1536]{2,1,0:T(8,128)(2,1)} %add_convert_fusion), channel_id=1, source_target_pairs={{0,3},{1,0},{2,1},{3,2},{4,7},{5,4},{6,5},{7,6},{8,11},{9,8},{10,9... | collective-permute-start | bytes 2359304 | tf_op jit(solution)/shard_map/ppermute | solution.py:63
  85.7 2.3 %add_convert_fusion.1 = bf16[2,128,1536]{2,1,0:T(8,128)(2,1)} fusion(bf16[2,128,1536]{2,1,0:T(8,128)(2,1)} %collective-permute-done.15, bf16[2,128,1536]{2,1,0:T(8,128)(2,1)S(1)} %get-tuple-element.58), kind=kLoop, calls=%fused_computation.11 | loop fusion | flops 1572864 | bytes 2359296 | tf_op jit(solution)/shard_map/convert_element_type | solution.py:415
  89.2 2.7 %collective-permute-done.18 = bf16[2,128,1536]{2,1,0:T(8,128)(2,1)} collective-permute-done((bf16[2,128,1536]{2,1,0:T(8,128)(2,1)}, bf16[2,128,1536]{2,1,0:T(8,128)(2,1)}, u32[]{:S(2)}, u32[]{:S(2)}) %collective-permute-start.18) | collective-permute-done | bytes 786464 | tf_op jit(solution)/shard_map/ppermute | solution.py:63
  91.9 7.2 %collective-permute-done.20 = bf16[2,128,1536]{2,1,0:T(8,128)(2,1)} collective-permute-done((bf16[2,128,1536]{2,1,0:T(8,128)(2,1)}, bf16[2,128,1536]{2,1,0:T(8,128)(2,1)}, u32[]{:S(2)}, u32[]{:S(2)}) %collective-permute-start.20) | collective-permute-done | bytes 786464 | tf_op jit(solution)/shard_map/ppermute | solution.py:63
  99.2 1.6 %fusion.19 = (bf16[128,1536]{1,0:T(8,128)(2,1)S(1)}, bf16[128,1536]{1,0:T(8,128)(2,1)S(1)}) fusion(bf16[2,128,1536]{2,1,0:T(8,128)(2,1)} %collective-permute-done.20, bf16[2,128,1536]{2,1,0:T(8,128)(2,1)} %collective-permute-done.18, bf16[2,128,1536]{2,1,0:T(8,128)(2,1)S(1)} %get-tuple-element.61), kind=kLoop, calls=%fused_computation.30 | loop fusion | flops 2359296 | bytes 3145728 | tf_op jit(solution)/shard_map/convert_element_type | solution.py:421
  100.8 3.1 %collective-permute-start.22 = (bf16[128,1536]{1,0:T(8,128)(2,1)S(1)}, bf16[128,1536]{1,0:T(8,128)(2,1)S(1)}, u32[]{:S(2)}, u32[]{:S(2)}) collective-permute-start(bf16[128,1536]{1,0:T(8,128)(2,1)S(1)} %get-tuple-element.76), channel_id=1, source_target_pairs={{0,8},{1,9},{2,10},{3,11},{4,12},{5,13},{6,14},{7,15},{8,0},{9,1},... | collective-permute-start | bytes 1179656 | tf_op jit(solution)/shard_map/ppermute | solution.py:63
  106.7 2.6 %collective-permute-done.22 = bf16[128,1536]{1,0:T(8,128)(2,1)S(1)} collective-permute-done((bf16[128,1536]{1,0:T(8,128)(2,1)S(1)}, bf16[128,1536]{1,0:T(8,128)(2,1)S(1)}, u32[]{:S(2)}, u32[]{:S(2)}) %collective-permute-start.22) | collective-permute-done | bytes 393248 | tf_op jit(solution)/shard_map/ppermute | solution.py:63
  109.3 4.6 %collective-permute-done.23 = bf16[128,1536]{1,0:T(8,128)(2,1)S(1)} collective-permute-done((bf16[128,1536]{1,0:T(8,128)(2,1)S(1)}, bf16[128,1536]{1,0:T(8,128)(2,1)S(1)}, u32[]{:S(2)}, u32[]{:S(2)}) %collective-permute-start.23) | collective-permute-done | bytes 393248 | tf_op jit(solution)/shard_map/ppermute | solution.py:63
  114.0 1.6 %fusion.16 = bf16[128,1536]{1,0:T(8,128)(2,1)S(1)} fusion(bf16[128,1536]{1,0:T(8,128)(2,1)S(1)} %collective-permute-done.23, bf16[128,1536]{1,0:T(8,128)(2,1)S(1)} %collective-permute-done.22, bf16[128,1536]{1,0:T(8,128)(2,1)S(1)} %collective-permute-done.21, bf16[2,128,1536]{2,1,0:T(8,128)(2,1)} %collective-permute-done.17, ...), kind=kLoop, calls=%fused_computation.18 | loop fusion | flops 2359296 | bytes 2752512 | tf_op jit(solution)/shard_map/convert_element_type | solution.py:424
  115.6 1.9 %collective-permute-start.24 = (bf16[2,16,1536]{2,1,0:T(8,128)(2,1)S(1)}, bf16[2,16,1536]{2,1,0:T(8,128)(2,1)S(1)}, u32[]{:S(2)}, u32[]{:S(2)}) collective-permute-start(bf16[2,16,1536]{2,1,0:T(8,128)(2,1)S(1)} %bitcast.115), channel_id=1, source_target_pairs={{0,48},{16,0},{32,16},{48,32},{1,49},{17,1},{33,17},{49,33},{2,50}... | collective-permute-start | bytes 294920 | tf_op jit(solution)/shard_map/ppermute | solution.py:49
  117.5 1.4 %collective-permute-start.25 = (bf16[2,16,1536]{2,1,0:T(8,128)(2,1)S(1)}, bf16[2,16,1536]{2,1,0:T(8,128)(2,1)S(1)}, u32[]{:S(2)}, u32[]{:S(2)}) collective-permute-start(bf16[2,16,1536]{2,1,0:T(8,128)(2,1)S(1)} %bitcast.113), channel_id=1, source_target_pairs={{0,32},{16,48},{32,0},{48,16},{1,33},{17,49},{33,1},{49,17},{2,34}... | collective-permute-start | bytes 294920 | tf_op jit(solution)/shard_map/ppermute | solution.py:49
  120.1 2.4 %collective-permute-done.25 = bf16[2,16,1536]{2,1,0:T(8,128)(2,1)S(1)} collective-permute-done((bf16[2,16,1536]{2,1,0:T(8,128)(2,1)S(1)}, bf16[2,16,1536]{2,1,0:T(8,128)(2,1)S(1)}, u32[]{:S(2)}, u32[]{:S(2)}) %collective-permute-start.25) | collective-permute-done | bytes 98336 | tf_op jit(solution)/shard_map/ppermute | solution.py:49
  123.7 6.4 %collective-permute-start.27 = (bf16[4,16,1536]{2,1,0:T(8,128)(2,1)S(1)}, bf16[4,16,1536]{2,1,0:T(8,128)(2,1)S(1)}, u32[]{:S(2)}, u32[]{:S(2)}) collective-permute-start(bf16[4,16,1536]{2,1,0:T(8,128)(2,1)S(1)} %get-tuple-element.78), channel_id=1, source_target_pairs={{0,64},{64,0},{1,65},{65,1},{2,66},{66,2},{3,67},{67,3},{4,68},{68... | collective-permute-start | bytes 589832 | tf_op jit(solution)/shard_map/ppermute | solution.py:53
  (110 shorter events, 20.2 us)
Async XLA Ops:
  0.0 2.8 %copy-start = (bf16[32,128,256]{2,1,0:T(8,128)(2,1)S(1)}, bf16[32,128,256]{2,1,0:T(8,128)(2,1)}, u32[]{:S(2)}) copy-start(bf16[32,128,256]{2,1,0:T(8,128)(2,1)} %param.14) | copy-start | bytes 6291460
  0.0 4.5 %copy-start.3 = (bf16[32,256]{1,0:T(8,128)(2,1)S(1)}, bf16[32,256]{1,0:T(8,128)(2,1)}, u32[]{:S(2)}) copy-start(bf16[32,256]{1,0:T(8,128)(2,1)} %param.17) | copy-start | bytes 49156
  4.6 2.7 %copy-start.5 = (bf16[1536]{0:T(1024)(128)(2,1)S(1)}, bf16[1536]{0:T(1024)(128)(2,1)}, u32[]{:S(2)}) copy-start(bf16[1536]{0:T(1024)(128)(2,1)} %param.20) | copy-start | bytes 9220
  7.8 2.6 %collective-permute-start = (bf16[4,16,1536]{2,1,0:T(8,128)(2,1)S(1)}, bf16[4,16,1536]{2,1,0:T(8,128)(2,1)S(1)}, u32[]{:S(2)}, u32[]{:S(2)}) collective-permute-start(bf16[4,16,1536]{2,1,0:T(8,128)(2,1)S(1)} %get-tuple-element.88), channel_id=1, source_target_pairs={{0,64},{64,0},{1,65},{65,1},{2,66},{66,2},{3,67},{67,3},{4,68},{68... | collective-permute-start | bytes 589832 | tf_op jit(solution)/shard_map/ppermute | solution.py:53
  10.5 7.2 %collective-permute-start.1 = (bf16[32,1536]{1,0:T(8,128)(2,1)S(1)}, bf16[32,1536]{1,0:T(8,128)(2,1)S(1)}, u32[]{:S(2)}, u32[]{:S(2)}) collective-permute-start(bf16[32,1536]{1,0:T(8,128)(2,1)S(1)} %bitcast.110), channel_id=1, source_target_pairs={{0,16},{16,32},{32,48},{48,0},{1,17},{17,33},{33,49},{49,1},{2,18}... | collective-permute-start | bytes 294920 | tf_op jit(solution)/shard_map/ppermute | solution.py:49
  12.2 8.0 %collective-permute-start.2 = (bf16[32,1536]{1,0:T(8,128)(2,1)S(1)}, bf16[32,1536]{1,0:T(8,128)(2,1)S(1)}, u32[]{:S(2)}, u32[]{:S(2)}) collective-permute-start(bf16[32,1536]{1,0:T(8,128)(2,1)S(1)} %bitcast.109), channel_id=1, source_target_pairs={{0,32},{16,48},{32,0},{48,16},{1,33},{17,49},{33,1},{49,17},{2,34}... | collective-permute-start | bytes 294920 | tf_op jit(solution)/shard_map/ppermute | solution.py:49
  15.5 4.7 %collective-permute-start.3 = (bf16[32,1536]{1,0:T(8,128)(2,1)S(1)}, bf16[32,1536]{1,0:T(8,128)(2,1)S(1)}, u32[]{:S(2)}, u32[]{:S(2)}) collective-permute-start(bf16[32,1536]{1,0:T(8,128)(2,1)S(1)} %bitcast.108), channel_id=1, source_target_pairs={{0,48},{16,0},{32,16},{48,32},{1,49},{17,1},{33,17},{49,33},{2,50}... | collective-permute-start | bytes 294920 | tf_op jit(solution)/shard_map/ppermute | solution.py:49
  16.4 3.9 %collective-permute-start.4 = (f32[1824]{0:T(1024)S(1)}, f32[1824]{0:T(1024)S(1)}, u32[]{:S(2)}, u32[]{:S(2)}) collective-permute-start(f32[1824]{0:T(1024)S(1)} %pad_maximum_fusion.9), channel_id=1, source_target_pairs={{0,1},{1,0},{2,3},{3,2},{4,5},{5,4},{6,7},{7,6},{8,9},{9,8},{10,11... | collective-permute-start | bytes 21896 | tf_op jit(solution)/shard_map/ppermute | solution.py:383
  20.3 12.8 %collective-permute-start.5 = (bf16[128,1536]{1,0:T(8,128)(2,1)S(1)}, bf16[128,1536]{1,0:T(8,128)(2,1)S(1)}, u32[]{:S(2)}, u32[]{:S(2)}) collective-permute-start(bf16[128,1536]{1,0:T(8,128)(2,1)S(1)} %pad_maximum_fusion.2), channel_id=1, source_target_pairs={{0,8},{1,9},{2,10},{3,11},{4,12},{5,13},{6,14},{7,15},{8,0},{9,1},... | collective-permute-start | bytes 1179656 | tf_op jit(solution)/shard_map/ppermute | solution.py:63
  23.3 9.9 %collective-permute-start.10 = (bf16[128,1536]{1,0:T(8,128)(2,1)S(1)}, bf16[128,1536]{1,0:T(8,128)(2,1)S(1)}, u32[]{:S(2)}, u32[]{:S(2)}) collective-permute-start(bf16[128,1536]{1,0:T(8,128)(2,1)S(1)} %pad_maximum_fusion.2), channel_id=1, source_target_pairs={{0,4},{1,5},{2,6},{3,7},{4,8},{5,9},{6,10},{7,11},{8,12},{9,13},{1... | collective-permute-start | bytes 1179656 | tf_op jit(solution)/shard_map/ppermute | solution.py:63
  23.7 10.7 %collective-permute-start.7 = (bf16[128,1536]{1,0:T(8,128)(2,1)S(1)}, bf16[128,1536]{1,0:T(8,128)(2,1)S(1)}, u32[]{:S(2)}, u32[]{:S(2)}) collective-permute-start(bf16[128,1536]{1,0:T(8,128)(2,1)S(1)} %pad_maximum_fusion.2), channel_id=1, source_target_pairs={{0,12},{1,13},{2,14},{3,15},{4,0},{5,1},{6,2},{7,3},{8,4},{9,5},{1... | collective-permute-start | bytes 1179656 | tf_op jit(solution)/shard_map/ppermute | solution.py:63
  25.9 7.1 %collective-permute-start.6 = (f32[2,1824]{1,0:T(2,128)S(1)}, f32[2,1824]{1,0:T(2,128)S(1)}, u32[]{:S(2)}, u32[]{:S(2)}) collective-permute-start(f32[2,1824]{1,0:T(2,128)S(1)} %pad_maximum_fusion.7), channel_id=1, source_target_pairs={{0,2},{1,3},{2,0},{3,1},{4,6},{5,7},{6,4},{7,5},{8,10},{9,11},{10,... | collective-permute-start | bytes 43784 | tf_op jit(solution)/shard_map/ppermute | solution.py:387
  33.2 12.4 %collective-permute-start.11 = (bf16[2,128,1536]{2,1,0:T(8,128)(2,1)S(1)}, bf16[2,128,1536]{2,1,0:T(8,128)(2,1)S(1)}, u32[]{:S(2)}, u32[]{:S(2)}) collective-permute-start(bf16[2,128,1536]{2,1,0:T(8,128)(2,1)S(1)} %pad_maximum_fusion.1.own_1), channel_id=1, source_target_pairs={{0,1},{1,2},{2,3},{3,0},{4,5},{5,6},{6,7},{7,4},{8,9},{9,10},{10,1... | collective-permute-start | bytes 2359304 | tf_op jit(solution)/shard_map/ppermute | solution.py:63
  34.5 11.2 %collective-permute-start.8 = (bf16[2,128,1536]{2,1,0:T(8,128)(2,1)S(1)}, bf16[2,128,1536]{2,1,0:T(8,128)(2,1)S(1)}, u32[]{:S(2)}, u32[]{:S(2)}) collective-permute-start(bf16[2,128,1536]{2,1,0:T(8,128)(2,1)S(1)} %pad_maximum_fusion.own_0), channel_id=1, source_target_pairs={{0,3},{1,0},{2,1},{3,2},{4,7},{5,4},{6,5},{7,6},{8,11},{9,8},{10,9... | collective-permute-start | bytes 2359304 | tf_op jit(solution)/shard_map/ppermute | solution.py:63
  36.3 19.3 %collective-permute-start.13 = (bf16[2,128,1536]{2,1,0:T(8,128)(2,1)S(1)}, bf16[2,128,1536]{2,1,0:T(8,128)(2,1)S(1)}, u32[]{:S(2)}, u32[]{:S(2)}) collective-permute-start(bf16[2,128,1536]{2,1,0:T(8,128)(2,1)S(1)} %pad_maximum_fusion.1.own_1), channel_id=1, source_target_pairs={{0,3},{1,0},{2,1},{3,2},{4,7},{5,4},{6,5},{7,6},{8,11},{9,8},{10,9... | collective-permute-start | bytes 2359304 | tf_op jit(solution)/shard_map/ppermute | solution.py:63
  37.6 18.1 %collective-permute-start.14 = (bf16[2,128,1536]{2,1,0:T(8,128)(2,1)S(1)}, bf16[2,128,1536]{2,1,0:T(8,128)(2,1)S(1)}, u32[]{:S(2)}, u32[]{:S(2)}) collective-permute-start(bf16[2,128,1536]{2,1,0:T(8,128)(2,1)S(1)} %pad_maximum_fusion.own_0), channel_id=1, source_target_pairs={{0,1},{1,2},{2,3},{3,0},{4,5},{5,6},{6,7},{7,4},{8,9},{9,10},{10,1... | collective-permute-start | bytes 2359304 | tf_op jit(solution)/shard_map/ppermute | solution.py:63
  45.7 18.1 %collective-permute-start.12 = (bf16[2,128,1536]{2,1,0:T(8,128)(2,1)S(1)}, bf16[2,128,1536]{2,1,0:T(8,128)(2,1)S(1)}, u32[]{:S(2)}, u32[]{:S(2)}) collective-permute-start(bf16[2,128,1536]{2,1,0:T(8,128)(2,1)S(1)} %collective-permute-done.11.below_1), channel_id=1, source_target_pairs={{0,1},{1,2},{2,3},{3,0},{4,5},{5,6},{6,7},{7,4},{8,9},{9,10},{10,1... | collective-permute-start | bytes 2359304 | tf_op jit(solution)/shard_map/ppermute | solution.py:63
  45.7 18.1 %collective-permute-start.9 = (bf16[2,128,1536]{2,1,0:T(8,128)(2,1)S(1)}, bf16[2,128,1536]{2,1,0:T(8,128)(2,1)S(1)}, u32[]{:S(2)}, u32[]{:S(2)}) collective-permute-start(bf16[2,128,1536]{2,1,0:T(8,128)(2,1)S(1)} %collective-permute-done.8.above_0), channel_id=1, source_target_pairs={{0,3},{1,0},{2,1},{3,2},{4,7},{5,4},{6,5},{7,6},{8,11},{9,8},{10,9... | collective-permute-start | bytes 2359304 | tf_op jit(solution)/shard_map/ppermute | solution.py:63
  69.4 12.3 %collective-permute-start.19 = (bf16[2,128,1536]{2,1,0:T(8,128)(2,1)}, bf16[2,128,1536]{2,1,0:T(8,128)(2,1)}, u32[]{:S(2)}, u32[]{:S(2)}) collective-permute-start(bf16[2,128,1536]{2,1,0:T(8,128)(2,1)} %get-tuple-element.64), channel_id=1, source_target_pairs={{0,3},{1,0},{2,1},{3,2},{4,7},{5,4},{6,5},{7,6},{8,11},{9,8},{10,9... | collective-permute-start | bytes 2359304 | tf_op jit(solution)/shard_map/ppermute | solution.py:63
  70.8 14.9 %collective-permute-start.15 = (bf16[2,128,1536]{2,1,0:T(8,128)(2,1)}, bf16[2,128,1536]{2,1,0:T(8,128)(2,1)}, u32[]{:S(2)}, u32[]{:S(2)}) collective-permute-start(bf16[2,128,1536]{2,1,0:T(8,128)(2,1)} %get-tuple-element.59), channel_id=1, source_target_pairs={{0,1},{1,2},{2,3},{3,0},{4,5},{5,6},{6,7},{7,4},{8,9},{9,10},{10,1... | collective-permute-start | bytes 2359304 | tf_op jit(solution)/shard_map/ppermute | solution.py:63
  79.0 13.0 %collective-permute-start.18 = (bf16[2,128,1536]{2,1,0:T(8,128)(2,1)}, bf16[2,128,1536]{2,1,0:T(8,128)(2,1)}, u32[]{:S(2)}, u32[]{:S(2)}) collective-permute-start(bf16[2,128,1536]{2,1,0:T(8,128)(2,1)} %get-tuple-element.62), channel_id=1, source_target_pairs={{0,1},{1,2},{2,3},{3,0},{4,5},{5,6},{6,7},{7,4},{8,9},{9,10},{10,1... | collective-permute-start | bytes 2359304 | tf_op jit(solution)/shard_map/ppermute | solution.py:63
  79.0 25.6 %collective-permute-start.17 = (bf16[2,128,1536]{2,1,0:T(8,128)(2,1)S(1)}, bf16[2,128,1536]{2,1,0:T(8,128)(2,1)}, u32[]{:S(2)}, u32[]{:S(2)}) collective-permute-start(bf16[2,128,1536]{2,1,0:T(8,128)(2,1)S(1)} %get-tuple-element.60), channel_id=1, source_target_pairs={{0,3},{1,0},{2,1},{3,2},{4,7},{5,4},{6,5},{7,6},{8,11},{9,8},{10,9... | collective-permute-start | bytes 2359304 | tf_op jit(solution)/shard_map/ppermute | solution.py:63
  83.9 15.2 %collective-permute-start.20 = (bf16[2,128,1536]{2,1,0:T(8,128)(2,1)}, bf16[2,128,1536]{2,1,0:T(8,128)(2,1)}, u32[]{:S(2)}, u32[]{:S(2)}) collective-permute-start(bf16[2,128,1536]{2,1,0:T(8,128)(2,1)} %add_convert_fusion), channel_id=1, source_target_pairs={{0,3},{1,0},{2,1},{3,2},{4,7},{5,4},{6,5},{7,6},{8,11},{9,8},{10,9... | collective-permute-start | bytes 2359304 | tf_op jit(solution)/shard_map/ppermute | solution.py:63
  88.0 16.7 %collective-permute-start.16 = (bf16[2,128,1536]{2,1,0:T(8,128)(2,1)}, bf16[2,128,1536]{2,1,0:T(8,128)(2,1)}, u32[]{:S(2)}, u32[]{:S(2)}) collective-permute-start(bf16[2,128,1536]{2,1,0:T(8,128)(2,1)} %add_convert_fusion.1), channel_id=1, source_target_pairs={{0,1},{1,2},{2,3},{3,0},{4,5},{5,6},{6,7},{7,4},{8,9},{9,10},{10,1... | collective-permute-start | bytes 2359304 | tf_op jit(solution)/shard_map/ppermute | solution.py:63
  100.8 8.5 %collective-permute-start.22 = (bf16[128,1536]{1,0:T(8,128)(2,1)S(1)}, bf16[128,1536]{1,0:T(8,128)(2,1)S(1)}, u32[]{:S(2)}, u32[]{:S(2)}) collective-permute-start(bf16[128,1536]{1,0:T(8,128)(2,1)S(1)} %get-tuple-element.76), channel_id=1, source_target_pairs={{0,8},{1,9},{2,10},{3,11},{4,12},{5,13},{6,14},{7,15},{8,0},{9,1},... | collective-permute-start | bytes 1179656 | tf_op jit(solution)/shard_map/ppermute | solution.py:63
  103.9 10.1 %collective-permute-start.23 = (bf16[128,1536]{1,0:T(8,128)(2,1)S(1)}, bf16[128,1536]{1,0:T(8,128)(2,1)S(1)}, u32[]{:S(2)}, u32[]{:S(2)}) collective-permute-start(bf16[128,1536]{1,0:T(8,128)(2,1)S(1)} %get-tuple-element.75), channel_id=1, source_target_pairs={{0,12},{1,13},{2,14},{3,15},{4,0},{5,1},{6,2},{7,3},{8,4},{9,5},{1... | collective-permute-start | bytes 1179656 | tf_op jit(solution)/shard_map/ppermute | solution.py:63
  105.9 8.0 %collective-permute-start.21 = (bf16[128,1536]{1,0:T(8,128)(2,1)S(1)}, bf16[128,1536]{1,0:T(8,128)(2,1)S(1)}, u32[]{:S(2)}, u32[]{:S(2)}) collective-permute-start(bf16[128,1536]{1,0:T(8,128)(2,1)S(1)} %fusion.17), channel_id=1, source_target_pairs={{0,4},{1,5},{2,6},{3,7},{4,8},{5,9},{6,10},{7,11},{8,12},{9,13},{1... | collective-permute-start | bytes 1179656 | tf_op jit(solution)/shard_map/ppermute | solution.py:63
  114.0 18.2 %copy-start.1 = (bf16[32,128,256]{2,1,0:T(8,128)(2,1)S(1)}, bf16[32,128,256]{2,1,0:T(8,128)(2,1)}, u32[]{:S(2)}) copy-start(bf16[32,128,256]{2,1,0:T(8,128)(2,1)} %param.14) | copy-start | bytes 6291460
  115.6 4.5 %collective-permute-start.24 = (bf16[2,16,1536]{2,1,0:T(8,128)(2,1)S(1)}, bf16[2,16,1536]{2,1,0:T(8,128)(2,1)S(1)}, u32[]{:S(2)}, u32[]{:S(2)}) collective-permute-start(bf16[2,16,1536]{2,1,0:T(8,128)(2,1)S(1)} %bitcast.115), channel_id=1, source_target_pairs={{0,48},{16,0},{32,16},{48,32},{1,49},{17,1},{33,17},{49,33},{2,50}... | collective-permute-start | bytes 294920 | tf_op jit(solution)/shard_map/ppermute | solution.py:49
  117.5 5.0 %collective-permute-start.25 = (bf16[2,16,1536]{2,1,0:T(8,128)(2,1)S(1)}, bf16[2,16,1536]{2,1,0:T(8,128)(2,1)S(1)}, u32[]{:S(2)}, u32[]{:S(2)}) collective-permute-start(bf16[2,16,1536]{2,1,0:T(8,128)(2,1)S(1)} %bitcast.113), channel_id=1, source_target_pairs={{0,32},{16,48},{32,0},{48,16},{1,33},{17,49},{33,1},{49,17},{2,34}... | collective-permute-start | bytes 294920 | tf_op jit(solution)/shard_map/ppermute | solution.py:49
  118.9 4.7 %collective-permute-start.26 = (bf16[2,16,1536]{2,1,0:T(8,128)(2,1)S(1)}, bf16[2,16,1536]{2,1,0:T(8,128)(2,1)S(1)}, u32[]{:S(2)}, u32[]{:S(2)}) collective-permute-start(bf16[2,16,1536]{2,1,0:T(8,128)(2,1)S(1)} %bitcast.111), channel_id=1, source_target_pairs={{0,16},{16,32},{32,48},{48,0},{1,17},{17,33},{33,49},{49,1},{2,18}... | collective-permute-start | bytes 294920 | tf_op jit(solution)/shard_map/ppermute | solution.py:49
  123.7 7.4 %collective-permute-start.27 = (bf16[4,16,1536]{2,1,0:T(8,128)(2,1)S(1)}, bf16[4,16,1536]{2,1,0:T(8,128)(2,1)S(1)}, u32[]{:S(2)}, u32[]{:S(2)}) collective-permute-start(bf16[4,16,1536]{2,1,0:T(8,128)(2,1)S(1)} %get-tuple-element.78), channel_id=1, source_target_pairs={{0,64},{64,0},{1,65},{65,1},{2,66},{66,2},{3,67},{67,3},{4,68},{68... | collective-permute-start | bytes 589832 | tf_op jit(solution)/shard_map/ppermute | solution.py:53
  (3 other events, 7.5 us)
